TPU v7x, 32 devices: a whole 2x2x4 slice. The times are simulated.
32 devices in a mesh: head: 2 (over core), seq: 16 (over z, y, x).
Axes of the slice: x: 2, y: 2, z: 4, core: 2. Of those that a mesh axis runs over, the one named last changes fastest.
Arguments:
- tokens: bfloat16 [2, 2048, 2048], P('head', 'seq'), may hold values from -6 to 6
- log_decay: float32 [2, 2048, 48], P(None, 'seq', 'head'), may hold values from -1 to 0
- norm_gain: bfloat16 [2048], P(('head', 'seq')), may hold values from 0.5 to 1.5
- qkv_proj: bfloat16 [2048, 1536], P(('head', 'seq')), may hold values from -0.125 to 0.125
- attn_proj: bfloat16 [1024, 2048], P(None, ('head', 'seq')), may hold values from -2 to 2
- inner_proj: bfloat16 [2048, 6704], P(('head', 'seq')), may hold values from -0.125 to 0.125
- conv_weight: bfloat16 [4, 3584], P(None, ('head', 'seq')), may hold values from -3 to 3
- conv_bias: bfloat16 [3584], P(('head', 'seq')), may hold values from -2 to 2
- step_bias: float32 [48], P('head'), may hold values from -4 to -1
- skip_gain: float32 [48], P('head'), may hold values from 0.5 to 8
- inner_gain: bfloat16 [3072], P(('head', 'seq')), may hold values from 0.5 to 1.5
- inner_out: bfloat16 [3072, 2048], P(None, ('head', 'seq')), may hold values from -0.109375 to 0.109375
- ff_gain: bfloat16 [2048], P(('head', 'seq')), may hold values from 0.5 to 1.5
- gate_up: bfloat16 [2048, 8192], P(('head', 'seq')), may hold values from -0.125 to 0.125
- down_proj: bfloat16 [4096, 2048], P(None, ('head', 'seq')), may hold values from -0.09375 to 0.09375
- cotangent: bfloat16 [2, 2048, 2048], P('head', 'seq'), may hold values from -6 to 6
Outputs:
- output: bfloat16 [2, 2048, 2048], P('head', 'seq')
- grad_tokens: float32 [2, 2048, 2048], P('head', 'seq')
- grad_norm_gain: float32 [2048], P(('head', 'seq'))
- grad_qkv_proj: float32 [2048, 1536], P(('head', 'seq'))
- grad_attn_proj: float32 [1024, 2048], P(None, ('head', 'seq'))
- grad_inner_proj: float32 [2048, 6704], P(('head', 'seq'))
- grad_conv_weight: float32 [4, 3584], P(None, ('head', 'seq'))
- grad_conv_bias: float32 [3584], P(('head', 'seq'))
- grad_step_bias: float32 [48], P('head')
- grad_skip_gain: float32 [48], P('head')
- grad_inner_gain: float32 [3072], P(('head', 'seq'))
- grad_inner_out: float32 [3072, 2048], P(None, ('head', 'seq'))
- grad_ff_gain: float32 [2048], P(('head', 'seq'))
- grad_gate_up: float32 [2048, 8192], P(('head', 'seq'))
- grad_down_proj: float32 [4096, 2048], P(None, ('head', 'seq'))
All inputs are finite; a program needn't handle non-finite values.
Results may differ from a plain program's by a relative error of at most 0.033.
Values may be sent and summed in bfloat16 or wider, within the bound.
No kernel may reach another device: no remote copies, remote signals or barrier semaphores. Data moves between devices by JAX's collectives and lax.ppermute only.
A program may use at most 576 MiB of HBM per device.

v0:
```python
import math

import jax
import jax.numpy as jnp
from jax import lax
from jax.sharding import PartitionSpec as P

FF = 4096
QH = 8
KVH = 2
HD = 128
MH = 48
MP = 64
NS = 256
KC = 4


EPSILON = 1e-05
ROPE_BASE = 100000000000.0
NEGATIVE = -1e30
HIGHEST = lax.Precision.HIGHEST


def passed_along(value, axis, steps):
    count = lax.axis_size(axis)
    initial, last = (max(0, -steps), min(count, count - steps))
    return lax.ppermute(value, axis, [(source, source + steps) for source in range(initial, last)])


def carried_in(array, axis, combine, identity):
    count, mine = (lax.axis_size(axis), lax.axis_index(axis))
    everything = jax.tree.map(
        lambda part, kind: lax.all_gather(part.astype(kind), axis),
        array,
        (jnp.bfloat16, jnp.bfloat16),
    )
    start = jax.tree.map(
        lambda part, zero: jnp.broadcast_to(jnp.asarray(zero, part.dtype), part.shape),
        array,
        identity,
    )

    def carried_hop(k, before):
        reached = k < mine
        new = combine(
            before, jax.tree.map(lambda part, own: part[k].astype(own.dtype), everything, array)
        )
        return jax.tree.map(lambda a, b: jnp.where(reached, a, b), new, before)

    return lax.fori_loop(0, count, carried_hop, start)


def entering(array, axis, combine, identity):
    count, mine = (lax.axis_size(axis), lax.axis_index(axis))
    everything = jax.tree.map(
        lambda part, kind: lax.all_gather(part.astype(kind), axis),
        array,
        jax.tree.map(lambda a: jnp.bfloat16 if a.dtype == jnp.float32 else a.dtype, array),
    )
    start = jax.tree.map(
        lambda part, zero: jnp.broadcast_to(jnp.asarray(zero, part.dtype), part.shape),
        array,
        identity,
    )

    def entering_hop(k, before):
        at = count - 1 - k
        reached = at > mine
        new = combine(
            before, jax.tree.map(lambda part, own: part[at].astype(own.dtype), everything, array)
        )
        return jax.tree.map(lambda a, b: jnp.where(reached, a, b), new, before)

    return lax.fori_loop(0, count, entering_hop, start)


def shortened(array):
    return jax.tree.map(lambda a: a.astype(jnp.bfloat16) if a.dtype == jnp.float32 else a, array)


def rounded(value):
    return lax.optimization_barrier(value.astype(jnp.bfloat16)).astype(jnp.float32)


def rms_norm(value, gain):
    return value * lax.rsqrt(jnp.mean(value * value, axis=-1, keepdims=True) + EPSILON) * gain


def rotary(value, positions):
    halfway = value.shape[-1] // 2
    frequency = ROPE_BASE ** (-2.0 * jnp.arange(halfway, dtype=jnp.float32) / value.shape[-1])
    angle = positions[:, None] * frequency[None, :]
    cosine = jnp.cos(angle)[:, None, :]
    sine_part = jnp.sin(angle)[:, None, :]
    first = value[..., :halfway]
    second = value[..., halfway:]
    return jnp.concatenate(
        [first * cosine - second * sine_part, second * cosine + first * sine_part], axis=-1
    )


def block_decay(log_decay):
    return jnp.exp(jnp.cumsum(log_decay, axis=1)[:, -1, :])


def inner_output(inner_x, step_in, state_maps, step_bias, skip_gain, state_in, log_decay):
    nstate = state_maps.shape[-1] // 2
    input_map = state_maps[..., :nstate]
    output_map = state_maps[..., nstate:]
    step_size = jax.nn.softplus(step_in + step_bias)
    cumulative = jnp.cumsum(log_decay, axis=1)
    scaled_x = inner_x * step_size[..., None]
    intersection = jnp.einsum("stn,sun->stu", output_map, input_map, precision=HIGHEST)
    length_blk = log_decay.shape[1]
    lower_mask = jnp.arange(length_blk)[:, None] >= jnp.arange(length_blk)[None, :]
    spread = cumulative[:, :, None, :] - cumulative[:, None, :, :]
    mixing = (
        jnp.where(lower_mask[None, :, :, None], jnp.exp(jnp.minimum(spread, 0.0)), 0.0)
        * intersection[..., None]
    )
    within = jnp.einsum("stuh,suhp->sthp", mixing, scaled_x, precision=HIGHEST)
    carried = (
        jnp.einsum("shpn,stn->sthp", state_in, output_map, precision=HIGHEST)
        * jnp.exp(cumulative)[..., None]
    )
    return within + carried + skip_gain[:, None] * inner_x


def inner_state(inner_x, step_in, state_maps, step_bias, log_decay):
    nstate = state_maps.shape[-1] // 2
    input_map = state_maps[..., :nstate]
    step_size = jax.nn.softplus(step_in + step_bias)
    cumulative = jnp.cumsum(log_decay, axis=1)
    tail_weight = jnp.exp(cumulative[:, -1:, :] - cumulative) * step_size
    return jnp.einsum("suh,suhp,sun->shpn", tail_weight, inner_x, input_map, precision=HIGHEST)


def over_blocks(function, carried, arrays, offset, limit):
    row_count = arrays[0].shape[1]
    step_rows = math.gcd(row_count, 1024)

    def advance(number, running):
        pieces = tuple(
            (
                lax.dynamic_slice_in_dim(member, number * step_rows, step_rows, 1)
                for member in arrays
            )
        )
        return function(running, pieces, offset + number * step_rows)

    upper = (limit + step_rows - 1) // step_rows
    return lax.fori_loop(0, upper, advance, carried)


def attend_block(carried, pair, offset, queries, query_pos, score_scale):
    row_top, row_total, accumulated = carried
    key_blk, value_blk = pair
    scores = (
        jnp.einsum("sqkgd,sjkd->sqkgj", queries, key_blk, preferred_element_type=jnp.float32)
        * score_scale
    )
    key_pos = offset + jnp.arange(key_blk.shape[1])
    allowed = (key_pos[None, :] <= query_pos[:, None])[None, :, None, None, :]
    masked = jnp.where(allowed, scores, NEGATIVE)
    new_top = jnp.maximum(row_top, jnp.max(masked, axis=-1))
    factor = jnp.exp(row_top - new_top)
    weights = jnp.where(allowed, jnp.exp(masked - new_top[..., None]), 0.0)
    row_total = factor * row_total + jnp.sum(weights, axis=-1)
    accumulated = factor[..., None] * accumulated + jnp.einsum(
        "sqkgj,sjkd->sqkgd",
        weights.astype(jnp.bfloat16),
        value_blk,
        preferred_element_type=jnp.float32,
    )
    return (new_top, row_total, accumulated)


def score_grads(
    queries, grad_heads, log_total, row_delta, key_blk, value_blk, offset, query_pos, score_scale
):
    scores = (
        jnp.einsum("sqkgd,sjkd->sqkgj", queries, key_blk, preferred_element_type=jnp.float32)
        * score_scale
    )
    key_pos = offset + jnp.arange(key_blk.shape[1])
    allowed = (key_pos[None, :] <= query_pos[:, None])[None, :, None, None, :]
    prob_rows = jnp.where(allowed, jnp.exp(scores - log_total[..., None]), 0.0)
    grad_probs = jnp.einsum(
        "sqkgd,sjkd->sqkgj", grad_heads, value_blk, preferred_element_type=jnp.float32
    )
    grad_scores = (prob_rows * (grad_probs - row_delta[..., None])).astype(jnp.bfloat16)
    return (prob_rows.astype(jnp.bfloat16), grad_scores)


def body(
    tokens,
    log_decay,
    norm_gain,
    qkv_proj,
    attn_proj,
    inner_proj,
    conv_weight,
    conv_bias,
    step_bias,
    skip_gain,
    inner_gain,
    inner_out,
    ff_gain,
    gate_up,
    down_proj,
    cotangent,
):
    head_count = lax.axis_size("head")
    seq_index = lax.axis_index("seq")
    (
        gain_in,
        qkv_full,
        attn_full,
        inner_full,
        conv_full,
        conv_bias_full,
        inner_gain_full,
        out_full,
        ff_gain_full,
        gate_up_full,
        down_full,
    ) = (
        lax.all_gather(norm_gain, ("head", "seq"), axis=0, tiled=True),
        lax.all_gather(qkv_proj, ("head", "seq"), axis=0, tiled=True),
        lax.all_gather(attn_proj, ("head", "seq"), axis=1, tiled=True),
        lax.all_gather(inner_proj, ("head", "seq"), axis=0, tiled=True),
        lax.all_gather(conv_weight, ("head", "seq"), axis=1, tiled=True),
        lax.all_gather(conv_bias, ("head", "seq"), axis=0, tiled=True),
        lax.all_gather(inner_gain, ("head", "seq"), axis=0, tiled=True),
        lax.all_gather(inner_out, ("head", "seq"), axis=1, tiled=True),
        lax.all_gather(ff_gain, ("head", "seq"), axis=0, tiled=True),
        lax.all_gather(gate_up, ("head", "seq"), axis=0, tiled=True),
        lax.all_gather(down_proj, ("head", "seq"), axis=1, tiled=True),
    )
    local_seqs, block_rows, model_width = tokens.shape
    token_rows = local_seqs * block_rows
    inner_width = MH * MP
    conv_width = inner_width + 2 * NS
    groups = QH // KVH
    kv_local = KVH // head_count
    inner_local = MH // head_count
    all_seqs = local_seqs * head_count
    score_scale = HD ** (-0.5)
    key_limit = (seq_index + 1) * block_rows
    x_rows = tokens.astype(jnp.float32).reshape(token_rows, model_width)
    normed_f, norm_back = jax.vjp(rms_norm, x_rows, gain_in.astype(jnp.float32))
    normed = normed_f.astype(jnp.bfloat16)
    qkv_rows = jnp.dot(normed, qkv_full, preferred_element_type=jnp.float32).reshape(
        local_seqs, block_rows, -1
    )
    positions = (seq_index * block_rows + jnp.arange(block_rows)).astype(jnp.float32)
    query_send = rotary(
        qkv_rows[..., : QH * HD].reshape(local_seqs, block_rows, QH, HD), positions
    ).astype(jnp.bfloat16)
    key_send = rotary(
        qkv_rows[..., QH * HD : (QH + KVH) * HD].reshape(local_seqs, block_rows, KVH, HD), positions
    ).astype(jnp.bfloat16)
    value_send = qkv_rows[..., (QH + KVH) * HD :].astype(jnp.bfloat16)
    inner_raw = jnp.dot(normed, inner_full, preferred_element_type=jnp.float32).reshape(
        local_seqs, block_rows, -1
    )
    gate_z = inner_raw[..., :inner_width]
    conv_in = inner_raw[..., inner_width : inner_width + conv_width]
    step_send = inner_raw[..., inner_width + conv_width :].astype(jnp.bfloat16)
    rim_rows = passed_along(
        conv_in[:, block_rows - (KC - 1) :, :].astype(jnp.bfloat16), "seq", 1
    ).astype(jnp.float32)
    padded = jnp.concatenate([rim_rows, conv_in], axis=1)

    def convolve(padded_in, weight_taps, bias_taps):
        conv_sum = bias_taps
        for conv_tap in range(KC):
            conv_sum = (
                conv_sum + weight_taps[conv_tap] * padded_in[:, conv_tap : conv_tap + block_rows, :]
            )
        return jax.nn.silu(conv_sum)

    activated, conv_back = jax.vjp(
        convolve, padded, conv_full.astype(jnp.float32), conv_bias_full.astype(jnp.float32)
    )
    activated_send = activated.astype(jnp.bfloat16)

    def split_heads(value):
        return value.reshape(value.shape[:2] + (head_count, -1))

    map_copies = jnp.broadcast_to(
        activated_send[:, :, None, inner_width:], (local_seqs, block_rows, head_count, 2 * NS)
    )
    received = (
        lax.all_to_all(split_heads(query_send), "head", split_axis=2, concat_axis=0, tiled=True),
        lax.all_to_all(split_heads(key_send), "head", split_axis=2, concat_axis=0, tiled=True),
        lax.all_to_all(split_heads(value_send), "head", split_axis=2, concat_axis=0, tiled=True),
        lax.all_to_all(
            split_heads(activated_send[..., :inner_width]),
            "head",
            split_axis=2,
            concat_axis=0,
            tiled=True,
        ),
        lax.all_to_all(split_heads(step_send), "head", split_axis=2, concat_axis=0, tiled=True),
        lax.all_to_all(map_copies, "head", split_axis=2, concat_axis=0, tiled=True),
    )
    queries = received[0].reshape(all_seqs, block_rows, kv_local, groups, HD)
    key_heads = received[1]
    value_heads = received[2]
    inner_x = received[3].reshape(all_seqs, block_rows, inner_local, MP).astype(jnp.float32)
    step_in = received[4].reshape(all_seqs, block_rows, inner_local).astype(jnp.float32)
    state_maps = received[5].reshape(all_seqs, block_rows, 2 * NS).astype(jnp.float32)
    query_pos = seq_index * block_rows + jnp.arange(block_rows)
    key_all, value_all = (
        lax.all_gather(key_heads, "seq", axis=1, tiled=True),
        lax.all_gather(value_heads, "seq", axis=1, tiled=True),
    )

    def attend_step(carried, pair, offset):
        return attend_block(carried, pair, offset, queries, query_pos, score_scale)

    stat_shape = (all_seqs, block_rows, kv_local, groups)
    start_stats = (
        jnp.full(stat_shape, NEGATIVE, jnp.float32),
        jnp.zeros(stat_shape, jnp.float32),
        jnp.zeros(stat_shape + (HD,), jnp.float32),
    )
    row_top, row_total, accumulated = over_blocks(
        attend_step, start_stats, (key_all, value_all), 0, key_limit
    )
    attended_f = accumulated / row_total[..., None]
    log_total = row_top + jnp.log(row_total)

    def state_part(piece_x, piece_step, piece_maps, piece_bias):
        return inner_state(piece_x, piece_step, piece_maps, piece_bias, log_decay)

    def output_part(piece_x, piece_step, piece_maps, piece_bias, piece_skip, piece_state):
        return inner_output(
            piece_x, piece_step, piece_maps, piece_bias, piece_skip, piece_state, log_decay
        )

    fresh_state, state_back = jax.vjp(state_part, inner_x, step_in, state_maps, step_bias)
    block_fall = block_decay(log_decay)

    def chain_rule(earlier, later):
        return (earlier[0] * later[0], later[1] + later[0][:, :, None, None] * earlier[1])

    neutral = (jnp.ones_like(block_fall), jnp.zeros_like(fresh_state))
    state_in = carried_in((block_fall, fresh_state), "seq", chain_rule, neutral)[1]
    inner_y, output_back = jax.vjp(
        output_part, inner_x, step_in, state_maps, step_bias, skip_gain, state_in
    )
    returned = (
        lax.all_to_all(
            attended_f.astype(jnp.bfloat16).reshape(all_seqs, block_rows, 1, -1),
            "head",
            split_axis=0,
            concat_axis=2,
            tiled=True,
        ),
        lax.all_to_all(
            inner_y.astype(jnp.bfloat16).reshape(all_seqs, block_rows, 1, -1),
            "head",
            split_axis=0,
            concat_axis=2,
            tiled=True,
        ),
    )
    attended = returned[0].reshape(token_rows, QH * HD)
    inner_back_y = returned[1].reshape(local_seqs, block_rows, inner_width).astype(jnp.float32)

    def gated_norm(y_part, gate_part, gain_part):
        return rms_norm(y_part * jax.nn.silu(gate_part), gain_part)

    inner_normed_f, gated_back = jax.vjp(
        gated_norm, inner_back_y, gate_z, inner_gain_full.astype(jnp.float32)
    )
    inner_normed = inner_normed_f.astype(jnp.bfloat16).reshape(token_rows, inner_width)
    hidden = (
        x_rows
        + jnp.dot(attended, attn_full, preferred_element_type=jnp.float32)
        + jnp.dot(inner_normed, out_full, preferred_element_type=jnp.float32)
    )
    normed_ff_f, ff_back = jax.vjp(rms_norm, hidden, ff_gain_full.astype(jnp.float32))
    normed_ff = normed_ff_f.astype(jnp.bfloat16)
    gate_vals = jnp.dot(normed_ff, gate_up_full, preferred_element_type=jnp.float32)

    def swiglu(values_in):
        return jax.nn.silu(values_in[:, :FF]) * values_in[:, FF:]

    mixed_f, swiglu_back = jax.vjp(swiglu, gate_vals)
    mixed_rows = mixed_f.astype(jnp.bfloat16)
    output = (
        (hidden + jnp.dot(mixed_rows, down_full, preferred_element_type=jnp.float32))
        .astype(jnp.bfloat16)
        .reshape(tokens.shape)
    )
    grad_out = cotangent.reshape(token_rows, model_width)
    grad_down = jnp.einsum("rf,rd->fd", mixed_rows, grad_out, preferred_element_type=jnp.float32)
    grad_gate_vals = swiglu_back(
        jnp.einsum("rd,fd->rf", grad_out, down_full, preferred_element_type=jnp.float32)
    )[0].astype(jnp.bfloat16)
    grad_gate_up = jnp.einsum(
        "rd,re->de", normed_ff, grad_gate_vals, preferred_element_type=jnp.float32
    )
    grad_hidden_norm, grad_ff_gain = ff_back(
        jnp.einsum("re,de->rd", grad_gate_vals, gate_up_full, preferred_element_type=jnp.float32)
    )
    grad_hidden = grad_out.astype(jnp.float32) + grad_hidden_norm
    grad_branch = grad_hidden.astype(jnp.bfloat16)
    grad_attn = jnp.einsum("rc,rd->cd", attended, grad_branch, preferred_element_type=jnp.float32)
    grad_inner_out = jnp.einsum(
        "rc,rd->cd", inner_normed, grad_branch, preferred_element_type=jnp.float32
    )
    grad_attended = jnp.einsum(
        "rd,cd->rc", grad_branch, attn_full, preferred_element_type=jnp.float32
    ).astype(jnp.bfloat16)
    grad_y, grad_gate_z, grad_inner_gain = gated_back(
        jnp.einsum("rd,cd->rc", grad_branch, out_full, preferred_element_type=jnp.float32).reshape(
            local_seqs, block_rows, inner_width
        )
    )
    sent_grads = (
        lax.all_to_all(
            split_heads(grad_attended.reshape(local_seqs, block_rows, QH * HD)),
            "head",
            split_axis=2,
            concat_axis=0,
            tiled=True,
        ),
        lax.all_to_all(
            split_heads(grad_y.astype(jnp.bfloat16)),
            "head",
            split_axis=2,
            concat_axis=0,
            tiled=True,
        ),
    )
    grad_heads = sent_grads[0].reshape(all_seqs, block_rows, kv_local, groups, HD)
    grad_inner_y = sent_grads[1].reshape(all_seqs, block_rows, inner_local, MP).astype(jnp.float32)
    row_delta = jnp.sum(grad_heads.astype(jnp.float32) * attended_f, axis=-1)

    def query_step(carried, pair, offset):
        prob_rows, grad_scores = score_grads(
            queries,
            grad_heads,
            log_total,
            row_delta,
            pair[0],
            pair[1],
            offset,
            query_pos,
            score_scale,
        )
        return carried + jnp.einsum(
            "sqkgj,sjkd->sqkgd", grad_scores, pair[0], preferred_element_type=jnp.float32
        )

    grad_queries = (
        over_blocks(query_step, jnp.zeros_like(attended_f), (key_all, value_all), 0, key_limit)
        * score_scale
    )
    count = block_rows * lax.axis_size("seq")
    step_rows = math.gcd(count, 1024)
    term_shape = (step_rows, all_seqs, kv_local, 2 * HD)

    def compute_block(offset):
        key_blk = lax.dynamic_slice_in_dim(key_all, offset, step_rows, 1)
        value_blk = lax.dynamic_slice_in_dim(value_all, offset, step_rows, 1)
        prob_rows, grad_scores = score_grads(
            queries,
            grad_heads,
            log_total,
            row_delta,
            key_blk,
            value_blk,
            offset,
            query_pos,
            score_scale,
        )
        grad_keys = (
            jnp.einsum(
                "sqkgj,sqkgd->jskd", grad_scores, queries, preferred_element_type=jnp.float32
            )
            * score_scale
        )
        grad_values = jnp.einsum(
            "sqkgj,sqkgd->jskd", prob_rows, grad_heads, preferred_element_type=jnp.float32
        )
        return jnp.concatenate([grad_keys, grad_values], axis=-1)

    def one_block(offset):
        return lax.cond(
            offset < key_limit,
            compute_block,
            lambda unused: jnp.zeros(term_shape, jnp.float32),
            offset,
        )

    block_terms = lax.map(
        lambda number: one_block(number * step_rows), jnp.arange(count // step_rows)
    )
    key_grads = lax.psum_scatter(
        block_terms.reshape((count,) + block_terms.shape[2:]),
        "seq",
        scatter_dimension=0,
        tiled=True,
    )
    grad_key_heads = jnp.moveaxis(key_grads[..., :HD], 0, 1)
    grad_value_heads = jnp.moveaxis(key_grads[..., HD:], 0, 1)
    grad_x_a, grad_step_a, grad_maps_a, grad_bias_a, grad_skip, grad_state = output_back(
        grad_inner_y
    )
    grad_carry = entering((block_fall, grad_state), "seq", chain_rule, neutral)[1]
    grad_x_b, grad_step_b, grad_maps_b, grad_bias_b = state_back(grad_carry)
    grad_step_bias, grad_skip_gain = lax.psum((grad_bias_a + grad_bias_b, grad_skip), "seq")
    returned_grads = (
        lax.all_to_all(
            grad_queries.reshape(all_seqs, block_rows, 1, -1).astype(jnp.bfloat16),
            "head",
            split_axis=0,
            concat_axis=2,
            tiled=True,
        ).astype(jnp.float32),
        lax.all_to_all(
            grad_key_heads.astype(jnp.bfloat16), "head", split_axis=0, concat_axis=2, tiled=True
        ).astype(grad_key_heads.dtype),
        lax.all_to_all(
            grad_value_heads.astype(jnp.bfloat16), "head", split_axis=0, concat_axis=2, tiled=True
        ).astype(grad_value_heads.dtype),
        lax.all_to_all(
            (grad_x_a + grad_x_b).reshape(all_seqs, block_rows, 1, -1).astype(jnp.bfloat16),
            "head",
            split_axis=0,
            concat_axis=2,
            tiled=True,
        ).astype(jnp.float32),
        lax.all_to_all(
            (grad_step_a + grad_step_b).reshape(all_seqs, block_rows, 1, -1).astype(jnp.bfloat16),
            "head",
            split_axis=0,
            concat_axis=2,
            tiled=True,
        ).astype(jnp.float32),
        lax.all_to_all(
            (grad_maps_a + grad_maps_b)[:, :, None, :].astype(jnp.bfloat16),
            "head",
            split_axis=0,
            concat_axis=2,
            tiled=True,
        ).astype(jnp.float32),
    )
    grad_q = rounded(returned_grads[0].reshape(local_seqs, block_rows, QH, HD))
    grad_k = rounded(returned_grads[1])
    grad_v = returned_grads[2].reshape(token_rows, KVH * HD)
    grad_qkv_rows = jnp.concatenate(
        [
            rotary(grad_q, -positions).reshape(token_rows, -1),
            rotary(grad_k, -positions).reshape(token_rows, -1),
            grad_v,
        ],
        axis=-1,
    ).astype(jnp.bfloat16)
    grad_x_in = rounded(returned_grads[3].reshape(local_seqs, block_rows, inner_width))
    grad_step = rounded(returned_grads[4].reshape(token_rows, MH))
    grad_maps = rounded(jnp.sum(returned_grads[5], axis=2))
    grad_padded, grad_conv_weight, grad_conv_bias = conv_back(
        jnp.concatenate([grad_x_in, grad_maps], axis=-1)
    )
    rim_grad = passed_along(shortened(grad_padded[:, : KC - 1, :]), "seq", -1)
    grad_conv_in = grad_padded[:, KC - 1 :, :].at[:, block_rows - (KC - 1) :, :].add(rim_grad)
    grad_inner_rows = jnp.concatenate(
        [grad_gate_z.reshape(token_rows, -1), grad_conv_in.reshape(token_rows, -1), grad_step],
        axis=-1,
    ).astype(jnp.bfloat16)
    grad_qkv_weight = jnp.einsum(
        "rd,re->de", normed, grad_qkv_rows, preferred_element_type=jnp.float32
    )
    grad_inner_weight = jnp.einsum(
        "rd,re->de", normed, grad_inner_rows, preferred_element_type=jnp.float32
    )
    grad_normed = jnp.einsum(
        "re,de->rd", grad_qkv_rows, qkv_full, preferred_element_type=jnp.float32
    ) + jnp.einsum("re,de->rd", grad_inner_rows, inner_full, preferred_element_type=jnp.float32)
    grad_x_norm, grad_norm_gain = norm_back(grad_normed)
    grad_tokens = (grad_hidden + grad_x_norm).reshape(tokens.shape)
    weight_grads = (
        grad_norm_gain,
        grad_qkv_weight,
        grad_attn,
        grad_inner_weight,
        grad_conv_weight,
        grad_conv_bias,
        grad_inner_gain,
        grad_inner_out,
        grad_ff_gain,
        grad_gate_up,
        grad_down,
    )
    shares = (
        lax.psum_scatter(weight_grads[0], ("head", "seq"), scatter_dimension=0, tiled=True),
        lax.psum_scatter(weight_grads[1], ("head", "seq"), scatter_dimension=0, tiled=True),
        lax.psum_scatter(weight_grads[2], ("head", "seq"), scatter_dimension=1, tiled=True),
        lax.psum_scatter(weight_grads[3], ("head", "seq"), scatter_dimension=0, tiled=True),
        lax.psum_scatter(weight_grads[4], ("head", "seq"), scatter_dimension=1, tiled=True),
        lax.psum_scatter(weight_grads[5], ("head", "seq"), scatter_dimension=0, tiled=True),
        lax.psum_scatter(weight_grads[6], ("head", "seq"), scatter_dimension=0, tiled=True),
        lax.psum_scatter(weight_grads[7], ("head", "seq"), scatter_dimension=1, tiled=True),
        lax.psum_scatter(weight_grads[8], ("head", "seq"), scatter_dimension=0, tiled=True),
        lax.psum_scatter(weight_grads[9], ("head", "seq"), scatter_dimension=0, tiled=True),
        lax.psum_scatter(weight_grads[10], ("head", "seq"), scatter_dimension=1, tiled=True),
    )
    return (
        output,
        grad_tokens,
        shares[0],
        shares[1],
        shares[2],
        shares[3],
        shares[4],
        shares[5],
        grad_step_bias,
        grad_skip_gain,
        shares[6],
        shares[7],
        shares[8],
        shares[9],
        shares[10],
    )


def solution(mesh):
    return jax.shard_map(
        body,
        mesh=mesh,
        in_specs=(
            P("head", "seq", None),
            P(None, "seq", "head"),
            P(("head", "seq")),
            P(("head", "seq"), None),
            P(None, ("head", "seq")),
            P(("head", "seq"), None),
            P(None, ("head", "seq")),
            P(("head", "seq")),
            P("head"),
            P("head"),
            P(("head", "seq")),
            P(None, ("head", "seq")),
            P(("head", "seq")),
            P(("head", "seq"), None),
            P(None, ("head", "seq")),
            P("head", "seq", None),
        ),
        out_specs=(
            P("head", "seq", None),
            P("head", "seq", None),
            P(("head", "seq")),
            P(("head", "seq"), None),
            P(None, ("head", "seq")),
            P(("head", "seq"), None),
            P(None, ("head", "seq")),
            P(("head", "seq")),
            P("head"),
            P("head"),
            P(("head", "seq")),
            P(None, ("head", "seq")),
            P(("head", "seq")),
            P(("head", "seq"), None),
            P(None, ("head", "seq")),
        ),
        check_vma=False,
    )
```

profile of v0, /device:TPU:0, one launch (start us, length us, event | category | flops | bytes accessed | tf_op | source)
XLA Modules:
  0.0 5581.2 jit_solution(8835471642687392976)
XLA Ops:
  12.1 42.5 all-reduce.23
  57.1 26.3 all-gather.17.cloned.1.call-done
  92.3 66.9 %all-gather.5 = bf16[32,112,4]{1,2,0:T(4,128)(2,1)S(1)} all-gather(bf16[1,112,4]{1,2,0:T(4,128)(2,1)S(1)} %bitcast.783), channel_id=1, replica_groups=mesh['head'=2,'seq'=16] {'head','seq'}, dimensions={0}, use_global_device_ids=true | all-gather | bytes 29568 | tf_op jit(solution)/shard_map/all_gather | solution.py:232
  166.0 86.4 %all-gather.21.cloned.1.call-done = bf16[2048,6704]{1,0:T(8,128)(2,1)} async-done(((bf16[64,6704]{1,0:T(8,128)(2,1)}), bf16[2048,6704]{1,0:T(8,128)(2,1)}) %all-gather.21.cloned.1.call-update) | async-done | bytes 27459600 | tf_op jit(solution)/shard_map/all_gather | solution.py:231
  252.4 17.4 fusion.227
  319.2 36.6 all-gather.3
  389.2 250.3 %all-gather.33.cloned.1.call-done = bf16[32,24,64,256]{3,2,1,0:T(8,128)(2,1)} async-done(((bf16[2,24,64,256]{3,2,1,0:T(8,128)(2,1)}), bf16[32,24,64,256]{3,2,1,0:T(8,128)(2,1)}) %all-gather.33.cloned.1.call-update) | async-done | bytes 25165840 | tf_op jit(solution)/shard_map/all_gather | solution.py:33
  639.5 59.2 %while.71 = (s32[]{:T(128)}, f32[2,24,64,256]{3,2,1,0:T(8,128)S(1)}, s32[]{:T(128)}, bf16[16,2,24,64,256]{4,3,2,1,0:T(8,128)(2,1)}, bf16[16,2,24]{2,1,0:T(2,128)(2,1)}, /*index=5*/s32[]{:T(128)}, s32[]{:T(128)}) while((s32[]{:T(128)}, f32[2,24,64,256]{3,2,1,0:T(8,128)S(1)}, s32[]{:T(128)}, bf16[16,2,24,64,256]{4,3,2,1,0:T(8,128)(2,1)}, ...), condition=%wide.region_7.9_spmd.clone, body=%wide.region_6.8_spmd.clone.sunk | while | flops 3932212 | bytes 7864913 | solution.py:50
  717.3 19.2 all-gather.23.cloned.1.call-done
  746.6 53.2 all-gather.19.cloned.1.call-done
  805.0 191.0 %all-gather.25.cloned.1.call-done = bf16[2048,8192]{1,0:T(8,128)(2,1)} async-done(((bf16[64,8192]{1,0:T(8,128)(2,1)}), bf16[2048,8192]{1,0:T(8,128)(2,1)}) %all-gather.25.cloned.1.call-update) | async-done | bytes 33554448 | tf_op jit(solution)/shard_map/all_gather | solution.py:237
  996.0 17.9 fusion.218
  1013.9 98.2 %all-gather.27.cloned.1.call-done = bf16[4096,2048]{0,1:T(8,128)(2,1)} async-done(((bf16[4096,64]{0,1:T(8,128)(2,1)}), bf16[4096,2048]{0,1:T(8,128)(2,1)}) %all-gather.27.cloned.1.call-update) | async-done | bytes 16777232 | tf_op jit(solution)/shard_map/all_gather | solution.py:238
  1112.1 13.2 fusion.176
  1125.3 20.4 multiply_reduce_fusion.6
  1147.9 11.3 fusion.136
  1199.2 22.1 while.70
  1221.8 218.3 %all-gather.35.cloned.1.call-done = bf16[32,24,64,256]{3,2,1,0:T(8,128)(2,1)} async-done(((bf16[2,24,64,256]{3,2,1,0:T(8,128)(2,1)}), bf16[32,24,64,256]{3,2,1,0:T(8,128)(2,1)}) %all-gather.35.cloned.1.call-update) | async-done | bytes 25165840 | tf_op jit(solution)/shard_map/all_gather | solution.py:56
  1440.1 59.1 %while.72 = (s32[]{:T(128)}, f32[2,24,64,256]{3,2,1,0:T(8,128)S(1)}, s32[]{:T(128)}, bf16[16,2,24,64,256]{4,3,2,1,0:T(8,128)(2,1)}, bf16[16,2,24]{2,1,0:T(2,128)...) while((s32[]{:T(128)}, f32[2,24,64,256]{3,2,1,0:T(8,128)S(1)}, s32[]{:T(128)}, ...), condition=%wide.region_21.23_spmd.clone, body=%wide.region_20.22_spmd.clone.sunk | while | flops 3932216 | bytes 7864975 | solution.py:74
  1576.6 13.2 fusion.169
  1591.1 25.5 fusion.173
  1650.9 20.6 fusion.167
  1673.4 12.7 fusion.111
  1686.1 50.0 all-reduce.22
  1736.1 20.5 fusion.168
  1763.2 40.9 all-reduce.21
  1810.8 54.7 reduce-scatter.15.cloned.1.call-done
  1865.5 163.9 %reduce-scatter.13.cloned.1.call-done = f32[64,1536]{1,0:T(8,128)} async-done(((f32[2048,1536]{1,0:T(8,128)}), f32[64,1536]{1,0:T(8,128)}) %reduce-scatter.13.cloned.1.call-update) | async-done | bytes 393232 | tf_op jit(solution)/shard_map/reduce_scatter | solution.py:603
  2029.3 251.4 %reduce-scatter.19.cloned.1.call-done = f32[3072,64]{0,1:T(8,128)} async-done(((f32[3072,2048]{0,1:T(8,128)}), f32[3072,64]{0,1:T(8,128)}) %reduce-scatter.19.cloned.1.call-update) | async-done | bytes 786448 | tf_op jit(solution)/shard_map/reduce_scatter | solution.py:609
  2280.7 708.4 %reduce-scatter.23.cloned.1.call-done = f32[4096,64]{0,1:T(8,128)} async-done(((f32[4096,2048]{0,1:T(8,128)}), f32[4096,64]{0,1:T(8,128)}) %reduce-scatter.23.cloned.1.call-update) | async-done | bytes 1048592 | tf_op jit(solution)/shard_map/reduce_scatter | solution.py:612
  2989.1 1411.0 %reduce-scatter.21.cloned.1.call-done = f32[64,8192]{1,0:T(8,128)} async-done(((f32[2048,8192]{1,0:T(8,128)}), f32[64,8192]{1,0:T(8,128)}) %reduce-scatter.21.cloned.1.call-update) | async-done | bytes 2097168 | tf_op jit(solution)/shard_map/reduce_scatter | solution.py:611
  4400.1 1173.8 %reduce-scatter.17.cloned.1.call-done = f32[64,6704]{1,0:T(8,128)} async-done(((f32[2048,6704]{1,0:T(8,128)}), f32[64,6704]{1,0:T(8,128)}) %reduce-scatter.17.cloned.1.call-update) | async-done | bytes 1716240 | tf_op jit(solution)/shard_map/reduce_scatter | solution.py:605
  (517 shorter events, 470.9 us)
Async XLA Ops:
  7.2 76.2 %all-gather.17.cloned.1.call-start = ((), (), s32[]{:S(2)}) async-start(), calls=%async_computation.24 | async-start | bytes 6488064 | tf_op jit(solution)/shard_map/all_gather | solution.py:229
  7.9 244.5 %all-gather.21.cloned.1.call-start = ((), (), s32[]{:S(2)}) async-start(), calls=%async_computation.26 | async-start | bytes 28655616 | tf_op jit(solution)/shard_map/all_gather | solution.py:231
  8.7 357.8 %all-gather.29.cloned.1.call-start = ((), (), s32[]{:S(2)}) async-start(), calls=%async_computation.37 | async-start | bytes 1114112 | tf_op jit(solution)/shard_map/all_gather | solution.py:316
  54.6 197.8 %copy-start.47 = (f32[2048]{0:T(1024)}, f32[2048]{0:T(1024)S(1)}, u32[]{:S(2)}) copy-start(f32[2048]{0:T(1024)S(1)} %convert_element_type.339) | copy-start | bytes 24580
  57.1 195.4 %copy-start.76 = (f32[128]{0:T(128)}, f32[128]{0:T(128)S(1)}, u32[]{:S(2)}) copy-start(f32[128]{0:T(128)S(1)} %fusion.205) | copy-start | bytes 1540
  92.2 274.2 %all-gather.31.cloned.1.call-start = ((), (), s32[]{:S(2)}) async-start(), calls=%async_computation.38 | async-start | bytes 1114112 | tf_op jit(solution)/shard_map/all_gather | solution.py:317
  160.9 130.7 %copy-start.68 = (f32[3584]{0:T(1024)}, f32[3584]{0:T(1024)S(1)}, u32[]{:S(2)}) copy-start(f32[3584]{0:T(1024)S(1)} %get-tuple-element.724) | copy-start | bytes 43012
  160.9 130.7 %copy-start.69 = (f32[3584]{0:T(1024)}, f32[3584]{0:T(1024)S(1)}, u32[]{:S(2)}) copy-start(f32[3584]{0:T(1024)S(1)} %get-tuple-element.725) | copy-start | bytes 43012
  160.9 130.7 %copy-start.70 = (f32[3584]{0:T(1024)}, f32[3584]{0:T(1024)S(1)}, u32[]{:S(2)}) copy-start(f32[3584]{0:T(1024)S(1)} %get-tuple-element.726) | copy-start | bytes 43012
  161.5 123.4 %copy-start.89 = (f32[2,1,24]{2,1,0:T(1,128)}, f32[2,1,24]{2,1,0:T(1,128)S(1)}, u32[]{:S(2)}) copy-start(f32[2,1,24]{2,1,0:T(1,128)S(1)} %get-tuple-element.851) | copy-start | bytes 580
  275.8 13.4 collective-permute-start
  302.3 5.5 all-to-all-start.4
  305.9 333.6 %all-gather.33.cloned.1.call-start = ((), (), s32[]{:S(2)}) async-start(), calls=%async_computation.39 | async-start | bytes 26738688 | tf_op jit(solution)/shard_map/all_gather | solution.py:33
  315.0 421.4 %all-gather.23.cloned.1.call-start = ((), (), s32[]{:S(2)}) async-start(), calls=%async_computation.27 | async-start | bytes 12976128 | tf_op jit(solution)/shard_map/all_gather | solution.py:235
  315.6 484.1 %all-gather.19.cloned.1.call-start = ((), (), s32[]{:S(2)}) async-start(), calls=%async_computation.25 | async-start | bytes 4325376 | tf_op jit(solution)/shard_map/all_gather | solution.py:230
  316.4 679.6 %all-gather.25.cloned.1.call-start = ((), (), s32[]{:S(2)}) async-start(), calls=%async_computation.28 | async-start | bytes 34603008 | tf_op jit(solution)/shard_map/all_gather | solution.py:237
  317.1 794.9 %all-gather.27.cloned.1.call-start = ((), (), s32[]{:S(2)}) async-start(), calls=%async_computation.29 | async-start | bytes 17301504 | tf_op jit(solution)/shard_map/all_gather | solution.py:238
  356.3 789.4 %copy-start.52 = (f32[2048]{0:T(1024)}, f32[2048]{0:T(1024)S(1)}, u32[]{:S(2)}) copy-start(f32[2048]{0:T(1024)S(1)} %convert_element_type.363) | copy-start | bytes 24580
  707.2 92.6 %all-to-all-start.3 = ((bf16[2,128,1,512]{1,3,2,0:T(8,128)(2,1)}), bf16[2,128,1,512]{1,3,2,0:T(8,128)(2,1)}, u32[]{:S(2)}, u32[]{:S(2)}) async-start(bf16[2,128,1,512]{1,3,2,0:T(8,128)(2,1)} %bitcast.751), calls=%async_computation.3 | async-start | bytes 524288 | tf_op jit(solution)/shard_map/all_to_all | solution.py:355
  711.3 728.8 %all-gather.35.cloned.1.call-start = ((), (), s32[]{:S(2)}) async-start(), calls=%async_computation.40 | async-start | bytes 26738688 | tf_op jit(solution)/shard_map/all_gather | solution.py:56
  805.0 340.8 %copy-start.81 = (f32[128]{0:T(128)}, f32[128]{0:T(128)S(1)}, u32[]{:S(2)}) copy-start(f32[128]{0:T(128)S(1)} %fusion.207) | copy-start | bytes 1540
  1170.5 376.6 %reduce-scatter.11.cloned.1.call-start = ((), (), s32[]{:S(2)}) async-start(), calls=%async_computation.30 | async-start | bytes 4456448 | tf_op jit(solution)/shard_map/reduce_scatter | solution.py:504
  1221.3 218.8 %copy-start.1 = (f32[2,24,64,256]{3,2,1,0:T(8,128)S(1)}, f32[2,24,64,256]{3,2,1,0:T(8,128)}, u32[]{:S(2)}) copy-start(f32[2,24,64,256]{3,2,1,0:T(8,128)} %custom-call.1) | copy-start | bytes 9437188
  1221.3 588.0 %reduce-scatter.25.cloned.1.call-start = ((), (), s32[]{:S(2)}) async-start(), calls=%async_computation.41 | async-start | bytes 1892352
  1528.9 336.6 %reduce-scatter.15.cloned.1.call-start = ((), (), s32[]{:S(2)}) async-start(), calls=%async_computation.32 | async-start | bytes 8650752 | tf_op jit(solution)/shard_map/reduce_scatter | solution.py:604
  1552.6 4.7 all-to-all-start.11
  1555.9 473.5 %reduce-scatter.13.cloned.1.call-start = ((), (), s32[]{:S(2)}) async-start(), calls=%async_computation.31 | async-start | bytes 12976128 | tf_op jit(solution)/shard_map/reduce_scatter | solution.py:603
  1563.9 716.8 %reduce-scatter.19.cloned.1.call-start = ((), (), s32[]{:S(2)}) async-start(), calls=%async_computation.34 | async-start | bytes 25952256 | tf_op jit(solution)/shard_map/reduce_scatter | solution.py:609
  1575.3 1413.8 %reduce-scatter.23.cloned.1.call-start = ((), (), s32[]{:S(2)}) async-start(), calls=%async_computation.36 | async-start | bytes 34603008 | tf_op jit(solution)/shard_map/reduce_scatter | solution.py:612
  1589.9 2810.3 %reduce-scatter.21.cloned.1.call-start = ((), (), s32[]{:S(2)}) async-start(), calls=%async_computation.35 | async-start | bytes 69206016 | tf_op jit(solution)/shard_map/reduce_scatter | solution.py:611
  1616.6 3957.4 %reduce-scatter.17.cloned.1.call-start = ((), (), s32[]{:S(2)}) async-start(), calls=%async_computation.33 | async-start | bytes 57311232 | tf_op jit(solution)/shard_map/reduce_scatter | solution.py:605
  1627.7 9.1 collective-permute-start.1
  (97 other events, 1565.4 us)
Sparse Core Ops, SparseCore 0:
  10.9 72.4 all-gather.16
  86.3 166.1 all-gather.20
  255.2 53.8 all-gather.28
  311.7 54.3 all-gather.30
  369.3 270.1 all-gather.32
  642.2 94.1 all-gather.22
  739.4 60.2 all-gather.18
  802.6 193.3 all-gather.24
  999.0 113.0 all-gather.26
  1170.6 269.4 all-gather.34
  1442.4 93.2 reduce-scatter.10
  1537.8 141.3 reduce-scatter.24
  1682.2 183.2 reduce-scatter.14
  1872.9 156.3 reduce-scatter.12
  2036.2 244.4 reduce-scatter.18
  2283.6 705.5 reduce-scatter.22
  2992.0 1408.0 reduce-scatter.20
  4403.0 1170.8 reduce-scatter.16
where the time goes:
time: 5600 us; the launch traced here: 5580 us
  waiting for transfers between devices  4710 us (84%)
  blocking collectives  294 us (5%)
  matrix products  281 us (5%)
  other arithmetic  177 us (3%)
  local copies, waits for them, and re-layouts  79.9 us (1%)
    reduce_scatter x1, waiting for transfers between devices, body(): lax.psum_scatter(weight_grads[9], ('head', 'seq'), scatter_dimension=0, t...  1410 us
    reduce_scatter x1, waiting for transfers between devices, body(): lax.psum_scatter(weight_grads[3], ('head', 'seq'), scatter_dimension=0, t...  1170 us
    reduce_scatter x1, waiting for transfers between devices, body(): lax.psum_scatter(weight_grads[10], ('head', 'seq'), scatter_dimension=1,...  708 us
    reduce_scatter x1, waiting for transfers between devices, body(): lax.psum_scatter(weight_grads[7], ('head', 'seq'), scatter_dimension=1, t...  251 us
    all_gather x1, waiting for transfers between devices, carried_in(): lax.all_gather(part.astype(kind), axis)  250 us
    all_gather x1, waiting for transfers between devices, entering(): lax.all_gather(part.astype(kind), axis)  218 us
    all_gather x1, waiting for transfers between devices, body(): lax.all_gather(gate_up, ('head', 'seq'), axis=0, tiled=True)  191 us
    reduce_scatter x1, waiting for transfers between devices, body(): lax.psum_scatter(weight_grads[1], ('head', 'seq'), scatter_dimension=0, t...  164 us
  transfers between devices with their start and end apart: 23, of which 16 were waited for; matrix products, arithmetic and copies ran while one was open for 8% of the time, Pallas kernels for 0%

commit v1 on v0

--- a/solution.py
+++ b/solution.py
@@ -1,8 +1,11 @@
+import functools
 import math
 
 import jax
 import jax.numpy as jnp
 from jax import lax
+from jax.experimental import pallas as pl
+from jax.experimental.pallas import tpu as pltpu
 from jax.sharding import PartitionSpec as P
 
 FF = 4096
@@ -630,9 +633,1225 @@
     )
 
 
+BLOCK = 128
+BIT_C, BIT_ZH, BIT_ZL, BIT_Y, BIT_X = 16, 8, 4, 2, 1
+DEVICES = 32
+BOTH = ("head", "seq")
+CUBE_ORDERS = ((0, 1, 2), (1, 2, 0), (2, 0, 1))
+CUBE_BITS = (BIT_ZL, BIT_Y, BIT_X)
+bf16 = jnp.bfloat16
+f32 = jnp.float32
+
+
+def flip(value, mask):
+    return lax.ppermute(value, BOTH, [(i, i ^ mask) for i in range(DEVICES)])
+
+
+def swap_sequences(value):
+    pairs = []
+    for i in range(DEVICES):
+        core, half = (i // BIT_C) % 2, (i // BIT_ZH) % 2
+        pairs.append((i, i - core * BIT_C - half * BIT_ZH + half * BIT_C + core * BIT_ZH))
+    return lax.ppermute(value, BOTH, pairs)
+
+
+def column_parts(width):
+    lanes = width // 128
+    first = -(-lanes // 3)
+    second = -(-(lanes - first) // 2)
+    edges = (0, first * 128, (first + second) * 128, width)
+    return [(edges[i], edges[i + 1]) for i in range(3)]
+
+
+def joint(*values):
+    return lax.optimization_barrier(values)
+
+
+def column_parts(width):
+    lanes = width // 128
+    first = -(-lanes // 3)
+    second = -(-(lanes - first) // 2)
+    edges = (0, first * 128, (first + second) * 128, width)
+    return [(edges[i], edges[i + 1]) for i in range(3)]
+
+
+def assemble(pieces, moves, shape, info):
+    count = len(pieces)
+
+    def kernel(info_ref, *refs):
+        out, sems = refs[count], refs[count + 1]
+        copies = []
+        for at, (number, source, target) in enumerate(moves):
+            copies.append(
+                pltpu.make_async_copy(
+                    refs[number].at[source(info_ref)], out.at[target(info_ref)], sems.at[at]
+                )
+            )
+        for copy in copies:
+            copy.start()
+        for copy in copies:
+            copy.wait()
+
+    size = math.prod(shape) * 2
+    return pl.pallas_call(
+        kernel,
+        in_specs=[pl.BlockSpec(memory_space=pltpu.SMEM)]
+        + [pl.BlockSpec(memory_space=pl.ANY)] * count,
+        out_specs=pl.BlockSpec(memory_space=pltpu.VMEM),
+        out_shape=jax.ShapeDtypeStruct(shape, bf16),
+        scratch_shapes=[pltpu.SemaphoreType.DMA((len(moves),))],
+        compiler_params=pltpu.CompilerParams(vmem_limit_bytes=2 * size + 8 * 1024 * 1024),
+        cost_estimate=LITTLE,
+        name="assemble",
+    )(info, *pieces)
+
+
+def fixed(row, rows, column, columns):
+    return lambda info: (pl.ds(row, rows), pl.ds(column, columns))
+
+
+class Gather:
+    def __init__(self, value, edges):
+        self.rows, self.step = value.shape[0], 0
+        self.state = ([value[None, None, None, :, a:b] for a, b in edges], None)
+
+    def hop(self):
+        parts, received = self.state
+        if received is not None:
+            parts = [
+                jnp.concatenate([part, got], axis=order[self.step - 1])
+                for part, got, order in zip(parts, received, CUBE_ORDERS)
+            ]
+        sent = [
+            flip(part, CUBE_BITS[order[self.step]]) for part, order in zip(parts, CUBE_ORDERS)
+        ]
+        self.state = (parts, sent)
+        self.step += 1
+
+    def pieces(self):
+        while self.step < 3:
+            self.hop()
+        near, far = [[part.reshape(4 * self.rows, -1) for part in parts] for parts in self.state]
+        crossed = [flip(jnp.concatenate(parts, axis=1), BIT_C) for parts in (near, far)]
+        return near + far + crossed
+
+
+def piece_blocks(part, far):
+    last = CUBE_ORDERS[part][2]
+    if last == 0:
+        return [(0, 4 * far, 4)]
+    if last == 1:
+        return [(2 * z, 4 * z + 2 * far, 2) for z in range(2)]
+    return [(i, 2 * i + far, 1) for i in range(4)]
+
+
+def gathered(gather, width, info):
+    rows = gather.rows
+    pieces = gather.pieces()
+    moves = []
+    for group in range(4):
+        half, far = group // 2, group % 2
+        for part, (a, b) in enumerate(column_parts(width)):
+            number = 3 * group + part if half == 0 else 6 + far
+            for first, place, blocks in piece_blocks(part, far):
+                moves.append(
+                    (
+                        number,
+                        fixed(first * rows, blocks * rows, a * half, b - a),
+                        fixed((half * 8 + place) * rows, blocks * rows, a, b - a),
+                    )
+                )
+    return assemble(pieces, moves, (16 * rows, width), info)
+
+
+def gather_start(value):
+    return Gather(value, column_parts(value.shape[1]))
+
+
+class Scatter:
+    def __init__(self, own_half, other_half):
+        self.total_rows, self.width = own_half.shape
+        self.step = 0
+        self.state = (own_half, flip(other_half.astype(bf16), BIT_C))
+
+    def summed(self):
+        kept, received = self.state
+        if self.step == 0:
+            value = kept.astype(f32) + received.astype(f32)
+            shape = (2, 2, 2, self.total_rows // 8, self.width)
+            value = value.reshape(shape)
+            return [value[..., a:b] for a, b in column_parts(self.width)]
+        return [near.astype(f32) + got.astype(f32) for near, got in zip(kept, received)]
+
+    def hop(self):
+        near, sent = [], []
+        for part, order in zip(self.summed(), CUBE_ORDERS):
+            axis = order[self.step]
+            part = part.astype(bf16)
+            near.append(lax.slice_in_dim(part, 0, 1, axis=axis))
+            sent.append(flip(lax.slice_in_dim(part, 1, 2, axis=axis), CUBE_BITS[axis]))
+        self.state = (near, sent)
+        self.step += 1
+
+    def result(self):
+        while self.step < 3:
+            self.hop()
+        rows = self.total_rows // 8
+        return jnp.concatenate([part.reshape(rows, -1) for part in self.summed()], axis=1)
+
+
+def group_sum(value):
+    for masks in ((BIT_C, BIT_X, BIT_C + BIT_X), (BIT_Y, BIT_ZL, BIT_Y + BIT_ZL)):
+        first, second, third = [flip(value, mask) for mask in masks]
+        value = (value + first) + (second + third)
+    return value
+
+
+def exchange(value):
+    return lax.all_to_all(value, BOTH, split_axis=0, concat_axis=0, tiled=True)
+
+
+def mm(a, b):
+    return jnp.dot(a, b, preferred_element_type=f32)
+
+
+def mm_nt(a, b):
+    return lax.dot_general(a, b, (((1,), (1,)), ((), ())), preferred_element_type=f32)
+
+
+def mm_tn(a, b):
+    return lax.dot_general(a, b, (((0,), (0,)), ((), ())), preferred_element_type=f32)
+
+
+VMEM_ASK = 40 * 1024 * 1024
+LITTLE = pl.CostEstimate(flops=1000, bytes_accessed=1000, transcendentals=0)
+
+
+def params():
+    return pltpu.CompilerParams(
+        dimension_semantics=("arbitrary",), vmem_limit_bytes=VMEM_ASK
+    )
+
+
+def k_nt(a, b, precision=None):
+    return lax.dot_general(
+        a, b, (((1,), (1,)), ((), ())), preferred_element_type=f32, precision=precision
+    )
+
+
+def k_tn(a, b):
+    return lax.dot_general(a, b, (((0,), (0,)), ((), ())), preferred_element_type=f32)
+
+
+def k_mm(a, b, precision=None):
+    return lax.dot_general(
+        a, b, (((1,), (0,)), ((), ())), preferred_element_type=f32, precision=precision
+    )
+
+
+def logistic(value):
+    return 1.0 / (1.0 + jnp.exp(-value))
+
+
+def by_head(columns, lane):
+    spread = columns[:, 0:1]
+    for head in range(1, HEADS_HERE):
+        spread = jnp.where(lane >= head * MP, columns[:, head : head + 1], spread)
+    return spread
+
+
+def shifted_sum(padded, taps, start, step):
+    total = None
+    for tap in range(KC):
+        at = start + step * tap
+        term = taps[tap : tap + 1] * padded[at : at + BLOCK]
+        total = term if total is None else total + term
+    return total
+
+
+HEADS_HERE = 3
+OWN = HEADS_HERE * MP
+TAIL = 8
+KEYS_AT = 2 * NS
+
+
+def block_decays(cum_col, cum_row, lane):
+    cum = by_head(cum_col, lane)
+    last = cum[BLOCK - 1 : BLOCK]
+    row = lax.broadcasted_iota(jnp.int32, (BLOCK, BLOCK), 0)
+    col = lax.broadcasted_iota(jnp.int32, (BLOCK, BLOCK), 1)
+    reach = []
+    for head in range(HEADS_HERE):
+        spread = cum_col[:, head : head + 1] - cum_row[head : head + 1, :]
+        reach.append(jnp.where(row >= col, jnp.exp(jnp.minimum(spread, 0.0)), 0.0))
+    return cum, last, reach
+
+
+def step_lanes(place, lane):
+    source = lax.broadcasted_iota(jnp.int32, (128, OWN), 0)
+    head = lax.broadcasted_iota(jnp.int32, (128, OWN), 1) // MP
+    return jnp.where(source == place * HEADS_HERE + head, 1.0, 0.0)
+
+
+def mix_forward(
+    info,
+    own_ref,
+    s_ref,
+    cos_ref,
+    sin_ref,
+    cum_col_ref,
+    cum_row_ref,
+    taps_x_ref,
+    taps_m_ref,
+    vec_ref,
+    y_ref,
+    gained_ref,
+    square_ref,
+    state_ref,
+    q_ref,
+    k_ref,
+    v_ref,
+    state,
+    last_x,
+    last_m,
+):
+    @pl.when(pl.program_id(0) == 0)
+    def _():
+        state[...] = jnp.zeros_like(state)
+        last_x[...] = jnp.zeros_like(last_x)
+        last_m[...] = jnp.zeros_like(last_m)
+
+    lane = lax.broadcasted_iota(jnp.int32, (1, OWN), 1)
+    gate = own_ref[:, :OWN]
+    x_raw = own_ref[:, OWN : 2 * OWN]
+    m_raw = s_ref[:, : 2 * NS]
+    cosine, sine = cos_ref[...], sin_ref[...]
+
+    def turned(value):
+        return (value * cosine + pltpu.roll(value, HD // 2, 1) * sine).astype(bf16)
+
+    q_ref[...] = turned(own_ref[:, 2 * OWN :])
+    k_ref[...] = turned(s_ref[:, KEYS_AT : KEYS_AT + HD])
+    v_ref[...] = s_ref[:, KEYS_AT + HD : KEYS_AT + 2 * HD].astype(bf16)
+
+    s_x = shifted_sum(
+        jnp.concatenate([last_x[...], x_raw], axis=0), taps_x_ref, TAIL - KC + 1, 1
+    ) + taps_x_ref[KC : KC + 1]
+    s_m = shifted_sum(
+        jnp.concatenate([last_m[...], m_raw], axis=0), taps_m_ref, TAIL - KC + 1, 1
+    ) + taps_m_ref[KC : KC + 1]
+    last_x[...] = x_raw[BLOCK - TAIL :]
+    last_m[...] = m_raw[BLOCK - TAIL :]
+    x = (s_x * logistic(s_x)).astype(bf16).astype(f32)
+    maps = (s_m * logistic(s_m)).astype(bf16)
+    b_map, c_map = maps[:, :NS], maps[:, NS:]
+
+    place = info[0]
+    picked = k_mm(s_ref[:, KEYS_AT + 2 * HD :].astype(bf16), step_lanes(place, lane).astype(bf16))
+    raised = picked + vec_ref[0:1]
+    step = jnp.maximum(raised, 0.0) + jnp.log(1.0 + jnp.exp(-jnp.abs(raised)))
+    cum, last, reach = block_decays(cum_col_ref[...], cum_row_ref[0], lane)
+    scaled = step * x
+    inter = k_nt(c_map, b_map)
+    total = vec_ref[1:2] * x
+    for head in range(HEADS_HERE):
+        here = (lane >= head * MP) & (lane < (head + 1) * MP)
+        total += k_mm(
+            (reach[head] * inter).astype(bf16), jnp.where(here, scaled, 0.0).astype(bf16)
+        )
+    before = state[...]
+    state_ref[0] = before.astype(bf16)
+    total += jnp.exp(cum) * k_mm(c_map, before.astype(bf16))
+    tail = (jnp.exp(last - cum) * scaled).astype(bf16)
+    state[...] = jnp.exp(last) * before + k_tn(b_map, tail)
+    y = total.astype(bf16)
+    y_ref[...] = y
+    gated = y.astype(f32) * (gate * logistic(gate))
+    gained_ref[...] = (gated * vec_ref[2:3]).astype(bf16)
+    square_ref[0] = k_nt(jnp.ones((8, OWN), f32), gated * gated, HIGHEST)
+
+
+def mix_backward(
+    info,
+    own_ref,
+    s_ref,
+    own_tail_ref,
+    s_tail_ref,
+    cos_ref,
+    sin_ref,
+    cum_col_ref,
+    cum_row_ref,
+    taps_x_ref,
+    taps_m_ref,
+    vec_ref,
+    lanes_ref,
+    y_ref,
+    g_inner_ref,
+    scales_ref,
+    state_ref,
+    dq_ref,
+    dk_ref,
+    dv_ref,
+    g_all_ref,
+    acc_x_ref,
+    acc_m_ref,
+    acc_v_ref,
+    acc_s_ref,
+    g_state,
+    next_x,
+    next_m,
+):
+    step_id = pl.program_id(0)
+    block = pl.num_programs(0) - 1 - step_id
+    place = info[0]
+
+    @pl.when(step_id == 0)
+    def _():
+        g_state[...] = jnp.zeros_like(g_state)
+        next_x[...] = jnp.zeros_like(next_x)
+        next_m[...] = jnp.zeros_like(next_m)
+        acc_x_ref[...] = jnp.zeros_like(acc_x_ref)
+        acc_m_ref[...] = jnp.zeros_like(acc_m_ref)
+        acc_v_ref[...] = jnp.zeros_like(acc_v_ref)
+        acc_s_ref[...] = jnp.zeros_like(acc_s_ref)
+
+    lane = lax.broadcasted_iota(jnp.int32, (1, OWN), 1)
+    cosine, sine = cos_ref[...], sin_ref[...]
+
+    def unturned(value):
+        return value * cosine - pltpu.roll(value, HD // 2, 1) * sine
+
+    gate = own_ref[:, :OWN]
+    x_raw = own_ref[:, OWN : 2 * OWN]
+    m_raw = s_ref[:, : 2 * NS]
+    first = block == 0
+    x_pad = jnp.concatenate(
+        [jnp.where(first, 0.0, own_tail_ref[:, OWN : 2 * OWN]), x_raw], axis=0
+    )
+    m_pad = jnp.concatenate([jnp.where(first, 0.0, s_tail_ref[:, : 2 * NS]), m_raw], axis=0)
+    s_x = shifted_sum(x_pad, taps_x_ref, TAIL - KC + 1, 1) + taps_x_ref[KC : KC + 1]
+    s_m = shifted_sum(m_pad, taps_m_ref, TAIL - KC + 1, 1) + taps_m_ref[KC : KC + 1]
+    sig_x, sig_m = logistic(s_x), logistic(s_m)
+    x = (s_x * sig_x).astype(bf16).astype(f32)
+    maps = (s_m * sig_m).astype(bf16)
+    b_map, c_map = maps[:, :NS], maps[:, NS:]
+    select = step_lanes(place, lane)
+    step_raw = s_ref[:, KEYS_AT + 2 * HD :].astype(bf16)
+    raised = k_mm(step_raw, select.astype(bf16)) + vec_ref[0:1]
+    step = jnp.maximum(raised, 0.0) + jnp.log(1.0 + jnp.exp(-jnp.abs(raised)))
+    cum, last, reach = block_decays(cum_col_ref[...], cum_row_ref[0], lane)
+    scaled = step * x
+
+    inv, dots = scales_ref[:, 0:1], scales_ref[:, 1:2]
+    y = y_ref[...].astype(f32)
+    g_inner = g_inner_ref[...]
+    gate_sig = logistic(gate)
+    gate_silu = gate * gate_sig
+    normed = y * gate_silu * inv
+    g_gated = inv * (vec_ref[2:3] * g_inner - normed * dots)
+    g_y = (g_gated * gate_silu).astype(bf16).astype(f32)
+    g_z = g_gated * y * gate_sig * (1.0 + gate * (1.0 - gate_sig))
+
+    inter = k_nt(c_map, b_map)
+    g_inter = jnp.zeros((BLOCK, BLOCK), f32)
+    g_scaled = jnp.zeros((BLOCK, OWN), f32)
+    scaled_b = scaled.astype(bf16)
+    for head in range(HEADS_HERE):
+        here = (lane >= head * MP) & (lane < (head + 1) * MP)
+        g_head = jnp.where(here, g_y, 0.0).astype(bf16)
+        g_inter += reach[head] * k_nt(g_head, scaled_b)
+        g_scaled += k_tn((reach[head] * inter).astype(bf16), g_head)
+    before = state_ref[0]
+    g_after = g_state[...]
+    g_after_b = g_after.astype(bf16)
+    tail_w = jnp.exp(last - cum)
+    reached = (jnp.exp(cum) * g_y).astype(bf16)
+    g_inter_b = g_inter.astype(bf16)
+    g_c = k_mm(g_inter_b, b_map) + k_nt(reached, before)
+    g_b = k_tn(g_inter_b, c_map) + k_nt((tail_w * scaled).astype(bf16), g_after_b)
+    g_scaled += tail_w * k_mm(b_map, g_after_b)
+    g_state[...] = jnp.exp(last) * g_after + k_tn(c_map, reached)
+    g_x = step * g_scaled + vec_ref[1:2] * g_y
+    g_step = k_nt(x * g_scaled, select, HIGHEST) * logistic(
+        step_raw.astype(f32) + lanes_ref[0:1]
+    )
+
+    gs_x = g_x.astype(bf16).astype(f32) * (sig_x * (1.0 + s_x * (1.0 - sig_x)))
+    g_maps = jnp.concatenate([g_b, g_c], axis=1).astype(bf16).astype(f32)
+    gs_m = g_maps * (sig_m * (1.0 + s_m * (1.0 - sig_m)))
+    gs_x_pad = jnp.concatenate([gs_x, next_x[...]], axis=0)
+    gs_m_pad = jnp.concatenate([gs_m, next_m[...]], axis=0)
+    g_x_raw = shifted_sum(gs_x_pad, taps_x_ref, KC - 1, -1)
+    g_m_raw = shifted_sum(gs_m_pad, taps_m_ref, KC - 1, -1)
+    next_x[...] = gs_x[:TAIL]
+    next_m[...] = gs_m[:TAIL]
+    for tap in range(KC):
+        at = TAIL - KC + 1 + tap
+        acc_x_ref[tap : tap + 1] += jnp.sum(gs_x * x_pad[at : at + BLOCK], axis=0, keepdims=True)
+        acc_m_ref[tap : tap + 1] += jnp.sum(gs_m * m_pad[at : at + BLOCK], axis=0, keepdims=True)
+    acc_x_ref[KC : KC + 1] += jnp.sum(gs_x, axis=0, keepdims=True)
+    acc_m_ref[KC : KC + 1] += jnp.sum(gs_m, axis=0, keepdims=True)
+    acc_v_ref[0:1] += jnp.sum(normed * g_inner, axis=0, keepdims=True)
+    acc_v_ref[1:2] += jnp.sum(g_y * x, axis=0, keepdims=True)
+    acc_s_ref[0:1] += jnp.sum(g_step, axis=0, keepdims=True)
+
+    here = (block // 8) == info[1]
+    g_q = jnp.where(here, unturned(dq_ref[...]), 0.0)
+    at = 2 * OWN
+    g_all_ref[:, :at] = jnp.concatenate([g_z, g_x_raw], axis=1).astype(bf16)
+    for piece in (g_q, g_m_raw, unturned(dk_ref[...]), dv_ref[...], g_step):
+        g_all_ref[:, at : at + piece.shape[1]] = piece.astype(bf16)
+        at += piece.shape[1]
+
+
+def masked_scores(info, keys, queries, length):
+    scores = k_nt(keys, queries) * (HD**-0.5)
+    start = (info[1] * 8 + pl.program_id(0)) * BLOCK
+    key_at = lax.broadcasted_iota(jnp.int32, (length, BLOCK), 0)
+    query_at = lax.broadcasted_iota(jnp.int32, (length, BLOCK), 1) + start
+    return scores, key_at <= query_at
+
+
+def attend_forward(info, q_ref, k_ref, v_ref, out_ref, out_f_ref, log_ref):
+    scores, allowed = masked_scores(info, k_ref[...], q_ref[...], k_ref.shape[0])
+    scores = jnp.where(allowed, scores, NEGATIVE)
+    top = jnp.max(scores, axis=0, keepdims=True)
+    weights = jnp.exp(scores - top)
+    total = jnp.sum(weights, axis=0, keepdims=True)
+    result = jnp.transpose(k_tn(v_ref[...], weights.astype(bf16)) / total)
+    out_ref[...] = result.astype(bf16)
+    out_f_ref[...] = result
+    log_ref[0] = jnp.broadcast_to(top + jnp.log(total), (8, BLOCK))
+
+
+def attend_backward(info, q_ref, k_ref, v_ref, out_f_ref, log_ref, g_ref, dq_ref, dk_ref, dv_ref):
+    @pl.when(pl.program_id(0) == 0)
+    def _():
+        dk_ref[...] = jnp.zeros_like(dk_ref)
+        dv_ref[...] = jnp.zeros_like(dv_ref)
+
+    keys, queries, grads = k_ref[...], q_ref[...], g_ref[...]
+    scores, allowed = masked_scores(info, keys, queries, k_ref.shape[0])
+    probs = jnp.where(allowed, jnp.exp(scores - log_ref[0, 0:1]), 0.0)
+    delta = k_nt(jnp.ones((8, HD), f32), grads.astype(f32) * out_f_ref[...], HIGHEST)[0:1]
+    g_scores = (probs * (k_nt(v_ref[...], grads) - delta)).astype(bf16)
+    dv_ref[...] += k_mm(probs.astype(bf16), grads)
+    dk_ref[...] += k_mm(g_scores, queries) * (HD**-0.5)
+    dq_ref[...] = (k_tn(g_scores, keys) * (HD**-0.5)).astype(bf16).astype(f32)
+
+
+def rows_at(width, column=0):
+    return pl.BlockSpec((BLOCK, width), lambda i, s: (i ^ s[0], column))
+
+
+def rows_back(count, width, column=0):
+    return pl.BlockSpec((BLOCK, width), lambda i, s: ((count - 1 - i) ^ s[0], column))
+
+
+def whole(*shape):
+    return pl.BlockSpec(shape, lambda i, s: (0,) * len(shape))
+
+
+def run_mix_forward(info, own, shared, cosine, sine, cum_col, cum_row, taps_x, taps_m, vec):
+    length = own.shape[0]
+    count = length // BLOCK
+
+    def plain(width):
+        return pl.BlockSpec((BLOCK, width), lambda i, s: (i, 0))
+
+    def plain3(rows, width):
+        return pl.BlockSpec((1, rows, width), lambda i, s: (i, 0, 0))
+
+    return pl.pallas_call(
+        mix_forward,
+        grid_spec=pltpu.PrefetchScalarGridSpec(
+            num_scalar_prefetch=1,
+            grid=(count,),
+            in_specs=[
+                rows_at(own.shape[1]),
+                rows_at(shared.shape[1]),
+                plain(HD),
+                plain(HD),
+                plain(8),
+                plain3(8, BLOCK),
+                whole(8, OWN),
+                whole(8, 2 * NS),
+                whole(8, OWN),
+            ],
+            out_specs=[
+                rows_at(OWN),
+                rows_at(OWN),
+                plain3(8, BLOCK),
+                plain3(NS, OWN),
+                plain(HD),
+                plain(HD),
+                plain(HD),
+            ],
+            scratch_shapes=[
+                pltpu.VMEM((NS, OWN), f32),
+                pltpu.VMEM((TAIL, OWN), f32),
+                pltpu.VMEM((TAIL, 2 * NS), f32),
+            ],
+        ),
+        out_shape=[
+            jax.ShapeDtypeStruct((length, OWN), bf16),
+            jax.ShapeDtypeStruct((length, OWN), bf16),
+            jax.ShapeDtypeStruct((count, 8, BLOCK), f32),
+            jax.ShapeDtypeStruct((count, NS, OWN), bf16),
+            jax.ShapeDtypeStruct((length, HD), bf16),
+            jax.ShapeDtypeStruct((length, HD), bf16),
+            jax.ShapeDtypeStruct((length, HD), bf16),
+        ],
+        compiler_params=params(),
+        cost_estimate=LITTLE,
+        name="mix_forward",
+    )(info, own, shared, cosine, sine, cum_col, cum_row, taps_x, taps_m, vec)
+
+
+def run_mix_backward(
+    info,
+    own,
+    shared,
+    cosine,
+    sine,
+    cum_col,
+    cum_row,
+    taps_x,
+    taps_m,
+    vec,
+    lanes,
+    y,
+    g_inner,
+    scales,
+    states,
+    dq,
+    dk,
+    dv,
+):
+    length = own.shape[0]
+    count = length // BLOCK
+    tails = BLOCK // TAIL
+    all_width = own.shape[1] + shared.shape[1]
+
+    def plain(width):
+        return pl.BlockSpec((BLOCK, width), lambda i, s: (count - 1 - i, 0))
+
+    def plain3(rows, width):
+        return pl.BlockSpec((1, rows, width), lambda i, s: (count - 1 - i, 0, 0))
+
+    def tail_of(width):
+        def where(i, s):
+            before = jnp.maximum(count - 2 - i, 0)
+            return ((before ^ s[0]) * tails + tails - 1, 0)
+
+        return pl.BlockSpec((TAIL, width), where)
+
+    def query_rows(i, s):
+        return ((count - 1 - i) % 8, 0)
+
+    return pl.pallas_call(
+        mix_backward,
+        grid_spec=pltpu.PrefetchScalarGridSpec(
+            num_scalar_prefetch=1,
+            grid=(count,),
+            in_specs=[
+                rows_back(count, own.shape[1]),
+                rows_back(count, shared.shape[1]),
+                tail_of(own.shape[1]),
+                tail_of(shared.shape[1]),
+                plain(HD),
+                plain(HD),
+                plain(8),
+                plain3(8, BLOCK),
+                whole(8, OWN),
+                whole(8, 2 * NS),
+                whole(8, OWN),
+                whole(8, 128),
+                rows_back(count, OWN),
+                rows_back(count, OWN),
+                plain(8),
+                plain3(NS, OWN),
+                pl.BlockSpec((BLOCK, HD), query_rows),
+                plain(HD),
+                plain(HD),
+            ],
+            out_specs=[
+                rows_back(count, all_width),
+                whole(8, OWN),
+                whole(8, 2 * NS),
+                whole(8, OWN),
+                whole(8, 128),
+            ],
+            scratch_shapes=[
+                pltpu.VMEM((NS, OWN), f32),
+                pltpu.VMEM((TAIL, OWN), f32),
+                pltpu.VMEM((TAIL, 2 * NS), f32),
+            ],
+        ),
+        out_shape=[
+            jax.ShapeDtypeStruct((length, all_width), bf16),
+            jax.ShapeDtypeStruct((8, OWN), f32),
+            jax.ShapeDtypeStruct((8, 2 * NS), f32),
+            jax.ShapeDtypeStruct((8, OWN), f32),
+            jax.ShapeDtypeStruct((8, 128), f32),
+        ],
+        compiler_params=params(),
+        cost_estimate=LITTLE,
+        name="mix_backward",
+    )(
+        info,
+        own,
+        shared,
+        own,
+        shared,
+        cosine,
+        sine,
+        cum_col,
+        cum_row,
+        taps_x,
+        taps_m,
+        vec,
+        lanes,
+        y,
+        g_inner,
+        scales,
+        states,
+        dq,
+        dk,
+        dv,
+    )
+
+
+def own_queries(width):
+    return pl.BlockSpec((BLOCK, width), lambda i, s: (s[1] * 8 + i, 0))
+
+
+def own_rows(width):
+    return pl.BlockSpec((BLOCK, width), lambda i, s: (i ^ s[2], 0))
+
+
+def run_attend_forward(info, queries, keys, values):
+    length = keys.shape[0]
+    half = length // 2
+    count = half // BLOCK
+    return pl.pallas_call(
+        attend_forward,
+        grid_spec=pltpu.PrefetchScalarGridSpec(
+            num_scalar_prefetch=1,
+            grid=(count,),
+            in_specs=[own_queries(HD), whole(length, HD), whole(length, HD)],
+            out_specs=[
+                own_rows(HD),
+                pl.BlockSpec((BLOCK, HD), lambda i, s: (i, 0)),
+                pl.BlockSpec((1, 8, BLOCK), lambda i, s: (i, 0, 0)),
+            ],
+        ),
+        out_shape=[
+            jax.ShapeDtypeStruct((half, HD), bf16),
+            jax.ShapeDtypeStruct((half, HD), f32),
+            jax.ShapeDtypeStruct((count, 8, BLOCK), f32),
+        ],
+        compiler_params=params(),
+        cost_estimate=LITTLE,
+        name="attend_forward",
+    )(info, queries, keys, values)
+
+
+def run_attend_backward(info, queries, keys, values, out_f, logs, grads):
+    length = keys.shape[0]
+    half = length // 2
+    count = half // BLOCK
+    return pl.pallas_call(
+        attend_backward,
+        grid_spec=pltpu.PrefetchScalarGridSpec(
+            num_scalar_prefetch=1,
+            grid=(count,),
+            in_specs=[
+                own_queries(HD),
+                whole(length, HD),
+                whole(length, HD),
+                pl.BlockSpec((BLOCK, HD), lambda i, s: (i, 0)),
+                pl.BlockSpec((1, 8, BLOCK), lambda i, s: (i, 0, 0)),
+                own_rows(HD),
+            ],
+            out_specs=[
+                pl.BlockSpec((BLOCK, HD), lambda i, s: (i, 0)),
+                whole(length, HD),
+                whole(length, HD),
+            ],
+        ),
+        out_shape=[
+            jax.ShapeDtypeStruct((half, HD), f32),
+            jax.ShapeDtypeStruct((length, HD), f32),
+            jax.ShapeDtypeStruct((length, HD), f32),
+        ],
+        compiler_params=params(),
+        cost_estimate=LITTLE,
+        name="attend_backward",
+    )(info, queries, keys, values, out_f, logs, grads)
+
+
+def cube_body(
+    tokens,
+    log_decay,
+    norm_gain,
+    qkv_proj,
+    attn_proj,
+    inner_proj,
+    conv_weight,
+    conv_bias,
+    step_bias,
+    skip_gain,
+    inner_gain,
+    inner_out,
+    ff_gain,
+    gate_up,
+    down_proj,
+    cotangent,
+):
+    core = lax.axis_index("head")
+    chip = lax.axis_index("seq")
+    member = chip % 8
+    bits = (member // 4, (member // 2) % 2, member % 2)
+    zl = bits[0]
+    place = core * 8 + member
+    info = jnp.stack([place, core, member]).astype(jnp.int32)
+    width = tokens.shape[-1]
+    rows = tokens.shape[1]
+    shard = width // DEVICES
+    inner_width = MH * MP
+    conv_width = inner_width + 2 * NS
+    heads = MH // 16
+    mine = heads * MP
+    length = rows * 16
+    half_rows = rows * 8
+    ffc = FF // 16
+
+    x_bf = swap_sequences(tokens[0])
+
+    gain_rows = norm_gain.astype(f32)[:, None]
+    qkv_s = (qkv_proj.astype(f32) * gain_rows).astype(bf16)
+    inner_s = (inner_proj.astype(f32) * gain_rows).astype(bf16)
+    gate_up_s = (gate_up.astype(f32) * ff_gain.astype(f32)[:, None]).astype(bf16)
+
+    def to_places(value):
+        return jnp.moveaxis(value.reshape(shard, 16, -1), 1, 0)
+
+    def to_members(value):
+        parts = jnp.moveaxis(value.reshape(shard, 8, -1), 1, 0)
+        return jnp.concatenate([parts, parts], axis=0)
+
+    def for_devices(value):
+        split = value.reshape((2, 1, 8) + value.shape[1:])
+        return jnp.broadcast_to(split, (2, 2, 8) + value.shape[1:]).reshape(
+            (DEVICES,) + value.shape[1:]
+        )
+
+    kv_width = KVH * HD
+    conv_shard = conv_weight.shape[1]
+    smalls = jnp.concatenate([conv_weight.reshape(-1), conv_bias, inner_gain])
+    decay_rows = jnp.moveaxis(log_decay, 1, 2).reshape(2, -1)
+    decay_high = lax.optimization_barrier(decay_rows.astype(bf16))
+    decay_low = (decay_rows - decay_high.astype(f32)).astype(bf16)
+    decay_rows = jnp.concatenate([decay_high, decay_low], axis=1)
+    extra_size = shard * 128
+    extra_pad = jnp.zeros((extra_size - smalls.shape[0] - decay_rows.shape[1],), bf16)
+    seq_half = chip // 8
+
+    def shared_for(half):
+        mine_rows = lax.dynamic_index_in_dim(decay_rows, half, 0, keepdims=False)
+        extra = jnp.concatenate([smalls, mine_rows, extra_pad]).reshape(shard, 128)
+        return jnp.concatenate([shared_send, extra], axis=1)
+
+    shared_send = jnp.concatenate(
+        [
+            inner_s[:, 2 * inner_width : inner_width + conv_width],
+            qkv_s[:, QH * HD : QH * HD + kv_width],
+            inner_s[:, inner_width + conv_width :],
+            jnp.zeros((shard, -MH % 128), bf16),
+            qkv_s[:, QH * HD + kv_width :],
+        ],
+        axis=1,
+    )
+    shared_other = flip(shared_for(1 - seq_half), BIT_ZH)
+    send_in = jnp.concatenate(
+        [
+            to_places(inner_s[:, :inner_width]),
+            to_places(inner_s[:, inner_width : 2 * inner_width]),
+            to_members(qkv_s[:, : QH * HD]),
+        ],
+        axis=2,
+    )
+    send_in, x_bf, shared_other = joint(for_devices(send_in), x_bf, shared_other)
+    w_own = exchange(send_in).reshape(width, 2 * mine + HD)
+    x_rows = x_bf.astype(f32)
+    inv_in = lax.rsqrt(jnp.mean(x_rows * x_rows, axis=-1, keepdims=True) + EPSILON)
+    shared_mine = shared_for(seq_half)
+    shared_both = jnp.where(
+        seq_half == 0,
+        jnp.concatenate([shared_mine, shared_other], axis=0),
+        jnp.concatenate([shared_other, shared_mine], axis=0),
+    )
+    normed_mine = (x_rows * inv_in).astype(bf16)
+    shared_edges = ((0, 2 * NS), (2 * NS, 2 * NS + kv_width + 128), (2 * NS + kv_width + 128, None))
+    lanes_all = (shared_both.shape[1] + width) // 128
+    goals = (-(-lanes_all // 3), -(-lanes_all // 3), lanes_all - 2 * -(-lanes_all // 3))
+    edges, normed_edges, joined, at, done = [], [], [], 0, 0
+    for (a, b), lanes_here in zip(shared_edges, goals):
+        part = shared_both[:, a:b]
+        taken = lanes_here * 128 - part.shape[1]
+        joined += [part, normed_mine[:, done : done + taken]]
+        edges.append((at, at + lanes_here * 128))
+        normed_edges.append((part.shape[1], done, taken))
+        at += lanes_here * 128
+        done += taken
+    pieces = Gather(jnp.concatenate(joined, axis=1), edges).pieces()
+    shared_width = 2 * NS + 2 * HD + 128
+    picks = (
+        ((0, 0, 0, 2 * NS),),
+        ((0, HD, 2 * NS, HD), (kv_width, 0, 2 * NS + 2 * HD, 128)),
+        ((0, HD, 2 * NS + HD, HD),),
+    )
+    moves, extra_moves, normed_moves = [], [], []
+    for group in range(4):
+        half, far = group // 2, group % 2
+        for part in range(3):
+            number = 3 * group + part if half == 0 else 6 + far
+            start = edges[part][0] * half
+            skip, normed_at, taken = normed_edges[part]
+            for first, cube_place, count in piece_blocks(part, far):
+                normed_moves.append(
+                    (
+                        number,
+                        fixed(first * rows, count * rows, start + skip, taken),
+                        fixed((half * 8 + cube_place) * rows, count * rows, normed_at, taken),
+                    )
+                )
+                for block, zh in ((i, j) for i in range(count) for j in range(2)):
+                    row = (first + block) * 2 * shard + zh * shard
+                    position = half * 8 + cube_place + block
+
+                    def goal(ref, position=position, zh=zh, target=0, columns=128):
+                        place = ref[0] ^ position
+                        to = (place // 8) * 16 + zh * 8 + place % 8
+                        to = pl.multiple_of(to * shard, shard)
+                        return (pl.ds(to, shard), pl.ds(target, columns))
+
+                    for column, by_zl, target, columns in picks[part]:
+
+                        def source(ref, row=row, at=start + column, by_zl=by_zl, columns=columns):
+                            if by_zl:
+                                at = pl.multiple_of(at + (ref[2] // 4) * by_zl, 128)
+                            return (pl.ds(row, shard), pl.ds(at, columns))
+
+                        moves.append(
+                            (
+                                number,
+                                source,
+                                functools.partial(goal, target=target, columns=columns),
+                            )
+                        )
+                    if part == 2:
+                        extra_moves.append(
+                            (number, fixed(row, shard, start + kv_width, 128), goal)
+                        )
+    normed = assemble(pieces, normed_moves, (length, width), info)
+    w_s = assemble(pieces, moves, (width, shared_width), info)
+    small_got = assemble(pieces, extra_moves, (width, 128), info).reshape(DEVICES, -1)
+    at = smalls.shape[0]
+    decay = lax.dynamic_slice_in_dim(small_got[:, at : at + decay_rows.shape[1]], core * 16, 16, 0)
+    decay = decay.astype(f32).reshape(16, 2, 8, heads, rows)
+    decay = lax.dynamic_index_in_dim(decay[:, 0] + decay[:, 1], member, 1, keepdims=False)
+    at = 0
+    conv_w = jnp.moveaxis(
+        small_got[:, at : at + KC * conv_shard].reshape(DEVICES, KC, conv_shard), 1, 0
+    ).reshape(KC, conv_width)
+    at += KC * conv_shard
+    conv_b = small_got[:, at : at + conv_shard].reshape(1, conv_width)
+    at += conv_shard
+    gain_all = small_got[:, at : at + inner_gain.shape[0]].reshape(1, inner_width)
+    conv_all = jnp.concatenate([conv_w, conv_b], axis=0).astype(f32)
+    conv_all = jnp.concatenate([conv_all, jnp.zeros((8 - KC - 1, conv_width), f32)], axis=0)
+    taps_x = lax.dynamic_slice_in_dim(conv_all[:, :inner_width], place * mine, mine, 1)
+    taps_m = conv_all[:, inner_width:]
+    gain_mine = lax.dynamic_slice_in_dim(gain_all, place * mine, mine, 1)[0].astype(f32)
+
+    send_mix = jnp.concatenate(
+        [to_places(inner_out.T), to_members(attn_proj.T)], axis=2
+    )
+    send_mix, w_own = joint(for_devices(send_mix), w_own)
+    w_mix = exchange(send_mix).reshape(width, mine + HD)
+    send_gu = jnp.concatenate([to_places(gate_up_s[:, :FF]), to_places(gate_up_s[:, FF:])], axis=2)
+    send_down, w_mix = joint(for_devices(to_places(down_proj.T)), w_mix)
+    w_down = exchange(send_down).reshape(width, ffc)
+    send_gu, w_down = joint(for_devices(send_gu), w_down)
+    w_gu = exchange(send_gu).reshape(width, 2 * ffc)
+
+    bias_mine = lax.dynamic_slice_in_dim(step_bias, member * heads, heads, 0)
+    skip_mine = lax.dynamic_slice_in_dim(skip_gain, member * heads, heads, 0)
+    vec = jnp.concatenate(
+        [
+            jnp.repeat(bias_mine, MP)[None],
+            jnp.repeat(skip_mine, MP)[None],
+            gain_mine[None],
+            jnp.zeros((5, mine), f32),
+        ],
+        axis=0,
+    )
+    lanes = lax.dynamic_update_slice(
+        jnp.zeros((8, 128), f32), bias_mine[None], (0, place * heads)
+    )
+    cum_row = jnp.cumsum(decay, axis=2)
+    cum_row = jnp.concatenate([cum_row, jnp.zeros((16, 8 - heads, rows), f32)], axis=1)
+    cum_col = jnp.moveaxis(cum_row, 1, 2).reshape(length, 8)
+    w_all = jnp.concatenate([w_own, w_s], axis=1)
+
+    order = jnp.arange(16, dtype=jnp.int32) ^ place
+
+    def reordered(value):
+        return jnp.take(value, order, axis=0, unique_indices=True, mode="clip")
+
+    cotangent_mine, normed = joint(cotangent[0], normed)
+    g_out_bf = swap_sequences(cotangent_mine)
+    raw_s = mm(normed, w_s)
+    g_out_bf, raw_s = joint(g_out_bf, raw_s)
+    g_out = gather_start(g_out_bf)
+    g_out.hop()
+    raw_own = mm(normed, w_own)
+    raw_own, w_mix = joint(raw_own, w_mix)
+    w_out, w_att = w_mix[:, :mine], w_mix[:, mine:]
+
+    positions = jnp.arange(length, dtype=f32)
+    frequency = ROPE_BASE ** (-2.0 * jnp.arange(HD // 2, dtype=f32) / HD)
+    angle = positions[:, None] * frequency[None, :]
+    cosine, sine = jnp.cos(angle), jnp.sin(angle)
+    cosine = jnp.concatenate([cosine, cosine], axis=1)
+    sine = jnp.concatenate([-sine, sine], axis=1)
+
+    tables = (cosine, sine, cum_col, cum_row, taps_x, taps_m, vec)
+    y, gained, squares, states, queries, keys, values = run_mix_forward(
+        info, raw_own, raw_s, *tables
+    )
+    g_out.state, queries = joint(g_out.state, queries)
+    g_out.hop()
+    squares = group_sum(squares[:, 0])
+    inv_mix = lax.rsqrt(squares / inner_width + EPSILON)
+    inv_mix_rows = reordered(inv_mix).reshape(length, 1)
+    keys, w_down = joint(keys, w_down)
+    attended, attended_f, logs = run_attend_forward(info, queries, keys, values)
+    g_out.state, attended = joint(g_out.state, attended)
+    g_out.hop()
+    part_other = inv_mix_rows[half_rows:] * mm_nt(gained[half_rows:], w_out)
+    part_own = inv_mix_rows[:half_rows] * mm_nt(gained[:half_rows], w_out) + mm_nt(attended, w_att)
+    sums = Scatter(part_own.astype(bf16), part_other)
+    sums.hop()
+    sums.state, w_gu = joint(sums.state, w_gu)
+    hidden = x_rows + sums.result()
+    g_out = gathered(g_out, width, info)
+
+    inv_ff = lax.rsqrt(jnp.mean(hidden * hidden, axis=-1, keepdims=True) + EPSILON)
+    normed_ff = gathered(gather_start((hidden * inv_ff).astype(bf16)), width, info)
+    gate_vals = mm(normed_ff, w_gu)
+    gate, up = gate_vals[:, :ffc], gate_vals[:, ffc:]
+    sig = jax.nn.sigmoid(gate)
+    mixed = (gate * sig * up).astype(bf16)
+    g_mixed = mm(g_out, w_down)
+    g_vals = jnp.concatenate(
+        [g_mixed * up * sig * (1.0 + gate * (1.0 - sig)), g_mixed * gate * sig], axis=1
+    ).astype(bf16)
+    g_ff_other = mm_nt(g_vals[half_rows:], w_gu).astype(bf16)
+    sums = Scatter(mm_nt(g_vals[:half_rows], w_gu).astype(bf16), g_ff_other)
+    g_ff_own, g_ff_got = sums.state
+    g_ff_own, mixed_late, g_vals_late = joint(g_ff_own, mixed, g_vals)
+    sums.state = (g_ff_own, g_ff_got)
+    out_other = mm_nt(mixed_late[half_rows:], w_down).astype(bf16)
+    out_own = mm_nt(mixed_late[:half_rows], w_down).astype(bf16)
+    d_gu = mm_tn(normed_ff, g_vals_late).astype(bf16)
+    d_down = mm_tn(g_out, mixed_late).astype(bf16)
+    sums.hop()
+    sums.state, out_other, out_own, d_gu, d_down = joint(
+        sums.state, out_other, out_own, d_gu, d_down
+    )
+    g_ff = sums.result()
+
+    def to_owners(value):
+        return exchange(value.astype(bf16).reshape(DEVICES, shard, -1))
+
+    def owned(got):
+        got = got.astype(f32).reshape((2, 2, 8) + got.shape[1:])
+        return (got[:, 0] + got[:, 1]).reshape((16,) + got.shape[3:])
+
+    def from_places(value):
+        return jnp.moveaxis(value, 0, 1).reshape(shard, -1)
+
+    g_hidden = (
+        g_out_bf.astype(f32)
+        + inv_ff * g_ff
+        - hidden * inv_ff**3 * jnp.mean(hidden * g_ff, axis=-1, keepdims=True)
+    )
+    g_branch = gathered(gather_start(g_hidden.astype(bf16)), width, info)
+    g_branch, d_gu, out_own, out_other = joint(g_branch, d_gu, out_own, out_other)
+    d_gu_got = to_owners(d_gu)
+
+    g_branch_own = g_branch[:half_rows]
+    inner_normed = (gained.astype(f32) * inv_mix_rows).astype(bf16)
+    g_inner = mm(g_branch, w_out)
+    g_att = mm(g_branch_own, w_att).astype(bf16)
+    dots = jnp.sum(inner_normed.astype(f32) * g_inner, axis=-1).reshape(16, rows)
+    dots = group_sum(reordered(dots))
+    d_out = mm_tn(g_branch, inner_normed).astype(bf16)
+    d_att = mm_tn(g_branch_own, attended).astype(bf16)
+    out_part = Scatter(out_own, out_other).result()
+
+    d_q, d_k, d_v = run_attend_backward(
+        info, queries, keys, values, attended_f, logs, g_att
+    )
+    scales = jnp.stack([inv_mix, dots / inner_width], axis=-1).reshape(length, 2)
+    scales = jnp.concatenate([scales, jnp.zeros((length, 6), f32)], axis=1)
+    scales, out_part = joint(scales, out_part)
+    g_all, acc_x, acc_m, acc_v, acc_s = run_mix_backward(
+        info,
+        raw_own,
+        raw_s,
+        *tables,
+        lanes,
+        y,
+        g_inner,
+        scales,
+        states,
+        d_q,
+        d_k,
+        d_v,
+    )
+    output = swap_sequences((hidden + out_part).astype(bf16))[None]
+    conv_grads = jnp.concatenate([acc_x[: KC + 1], acc_m[: KC + 1]], axis=1)
+    g_bias = lax.dynamic_slice_in_dim(acc_s[0], place * heads, heads, 0)
+    g_skip = jnp.sum(acc_v[1].reshape(heads, MP), axis=1)
+    small_grads = jnp.concatenate([conv_grads.reshape(-1), acc_v[0], g_bias, g_skip])
+    small_grads = jnp.pad(small_grads, (0, -small_grads.shape[0] % shard)).astype(bf16)
+    small_grads = jnp.broadcast_to(
+        small_grads.reshape(1, shard, -1), (DEVICES, shard, small_grads.shape[0] // shard)
+    ).reshape(width, -1)
+    d_mix = jnp.concatenate([d_down, d_out, d_att, small_grads], axis=1)
+    d_mix, g_all, d_gu_got = joint(d_mix, g_all, d_gu_got)
+    d_mix_got = to_owners(d_mix)
+    g_in_other = mm_nt(g_all[half_rows:], w_all).astype(bf16)
+    g_in_own = mm_nt(g_all[:half_rows], w_all).astype(bf16)
+    g_late = g_all
+    own_width = 2 * mine + HD
+    d_own = mm_tn(normed, g_late[:, :own_width]).astype(bf16)
+    d_own, d_mix_got = joint(d_own, d_mix_got)
+    d_own_got = to_owners(d_own)
+    d_shared = mm_tn(normed, g_late[:, own_width:]).astype(bf16)
+    def only_mine(value):
+        empty = jnp.zeros((width, KVH * HD), bf16)
+        return lax.dynamic_update_slice_in_dim(empty, value, zl * HD, 1)
+
+    d_shared = jnp.concatenate(
+        [
+            d_shared[:, : 2 * NS],
+            only_mine(d_shared[:, 2 * NS : 2 * NS + HD]),
+            only_mine(d_shared[:, 2 * NS + HD : 2 * NS + 2 * HD]),
+            d_shared[:, 2 * NS + 2 * HD :],
+        ],
+        axis=1,
+    )
+    moves = []
+    for block in range(DEVICES):
+
+        def goal(ref, block=block):
+            position = ref[0] ^ (block // 16 * 8 + block % 8)
+            row = position * 2 + block // 8 % 2
+            return (pl.ds(pl.multiple_of(row * shard, shard), shard), slice(None))
+
+        moves.append((0, fixed(block * shard, shard, 0, d_shared.shape[1]), goal))
+    d_shared = assemble([d_shared], moves, d_shared.shape, info)
+    sums = Scatter(
+        jnp.concatenate([g_in_own, d_shared[:half_rows]], axis=1),
+        jnp.concatenate([g_in_other, d_shared[half_rows:]], axis=1),
+    ).result()
+    sums, d_mix_got = joint(sums, d_mix_got)
+    g_in = sums[:, :width]
+    d_cube = sums[:, width:].reshape(2, shard, -1)
+    d_shared_own = lax.dynamic_index_in_dim(d_cube, seq_half, 0, keepdims=False) + flip(
+        lax.dynamic_index_in_dim(d_cube, 1 - seq_half, 0, keepdims=False).astype(bf16), BIT_ZH
+    ).astype(f32)
+    d_gu_own = owned(d_gu_got)
+    d_gate_up = jnp.concatenate(
+        [from_places(d_gu_own[..., :ffc]), from_places(d_gu_own[..., ffc:])], axis=1
+    )
+    grad_gate_up = d_gate_up * ff_gain.astype(f32)[:, None]
+    grad_ff_gain = jnp.sum(d_gate_up * gate_up.astype(f32), axis=1)
+    d_mix_own = owned(d_mix_got)
+    grad_down = jnp.moveaxis(d_mix_own[..., :ffc], 1, 2).reshape(FF, shard)
+    grad_inner_out = jnp.moveaxis(d_mix_own[..., ffc : ffc + mine], 1, 2).reshape(
+        inner_width, shard
+    )
+    at = ffc + mine + HD
+    d_att = d_mix_own[..., ffc + mine : at].reshape(2, 8, shard, HD)
+    grad_attn = jnp.moveaxis(d_att[0] + d_att[1], 1, 2).reshape(QH * HD, shard)
+    d_own = owned(d_own_got)
+    d_z = from_places(d_own[..., :mine])
+    d_x = from_places(d_own[..., mine : 2 * mine])
+    d_qw = d_own[..., 2 * mine :].reshape(2, 8, shard, HD)
+    d_qw = from_places(d_qw[0] + d_qw[1])
+
+    got = d_mix_own[..., at:].reshape(16, -1)
+    at = 0
+    taps_width = mine + 2 * NS
+    conv_grads = got[:, at : at + (KC + 1) * taps_width].reshape(16, KC + 1, taps_width)
+    at += (KC + 1) * taps_width
+    conv_full = jnp.concatenate(
+        [
+            jnp.moveaxis(conv_grads[..., :mine], 0, 1).reshape(KC + 1, inner_width),
+            jnp.sum(conv_grads[..., mine:], axis=0),
+        ],
+        axis=1,
+    )
+    device = core * 16 + chip
+    conv_own = lax.dynamic_slice_in_dim(conv_full, device * conv_shard, conv_shard, 1)
+    gain_full = got[:, at : at + mine].reshape(inner_width)
+    gain_shard = inner_gain.shape[0]
+    grad_inner_gain = lax.dynamic_slice_in_dim(gain_full, device * gain_shard, gain_shard, 0)
+    at += mine
+    local = lax.dynamic_slice_in_dim(got[:, at : at + 2 * heads], core * 8, 8, 0)
+    grad_step_bias = local[:, :heads].reshape(-1)
+    grad_skip_gain = local[:, heads:].reshape(-1)
+
+    at = 2 * NS + 2 * kv_width
+    d_qkv = jnp.concatenate([d_qw, d_shared_own[:, 2 * NS : at]], axis=1)
+    d_inner = jnp.concatenate(
+        [d_z, d_x, d_shared_own[:, : 2 * NS], d_shared_own[:, at : at + MH]], axis=1
+    )
+    grad_norm_gain = jnp.sum(d_qkv * qkv_proj.astype(f32), axis=1) + jnp.sum(
+        d_inner * inner_proj.astype(f32), axis=1
+    )
+    g_x_rows = (
+        inv_in * g_in - x_rows * inv_in**3 * jnp.mean(x_rows * g_in, axis=-1, keepdims=True)
+    )
+    grad_tokens = swap_sequences((g_hidden + g_x_rows).astype(bf16)).astype(f32)[None]
+    return (
+        output,
+        grad_tokens,
+        grad_norm_gain,
+        d_qkv * gain_rows,
+        grad_attn,
+        d_inner * gain_rows,
+        conv_own[:KC],
+        conv_own[KC],
+        grad_step_bias,
+        grad_skip_gain,
+        grad_inner_gain,
+        grad_inner_out,
+        grad_ff_gain,
+        grad_gate_up,
+        grad_down,
+    )
+
+
 def solution(mesh):
     return jax.shard_map(
-        body,
+        cube_body if mesh.shape["seq"] == 16 else body,
         mesh=mesh,
         in_specs=(
             P("head", "seq", None),

time: 5600 us -> 950 us (0.17)
  waiting for transfers between devices: 4710 us -> 309 us
  blocking collectives: 294 us -> 0 us
  starting transfers between devices: 17.5 us -> 189 us
  matrix products: 281 us -> 139 us
  Pallas kernels: 0 us -> 89.8 us
  other arithmetic: 177 us -> 98.1 us
    reduce_scatter x7 -> x0, waiting for transfers between devices: 3760 us -> none  [the longest x1 1410 us: body(): lax.psum_scatter(weight_grads[9], ('head', 'seq'), scatter_dimension=0, t...]
    all_gather x10 -> x0, waiting for transfers between devices: 943 us -> none  [the longest x1 250 us: carried_in(): lax.all_gather(part.astype(kind), axis)]
    ppermute x2 -> x102, waiting for transfers between devices: 0.01 us -> 283 us  [the longest x98 283 us: flip(): return lax.ppermute(value, BOTH, [(i, i ^ mask) for i in range(DEVICES)])]
    ppermute x2 -> x102, starting transfers between devices: 5.04 us -> 152 us  [the longest x98 133 us: flip(): return lax.ppermute(value, BOTH, [(i, i ^ mask) for i in range(DEVICES)])]
    dot_general x37 -> x21, matrix products: 281 us -> 139 us  [the longest x9 48.2 us: mm_nt(): lax.dot_general(a, b, (((1,), (1,)), ((), ())), preferred_element_type=f32)]
    all_gather x2 -> x0, blocking collectives: 103 us -> none  [the longest x1 66.9 us: body(): lax.all_gather(conv_weight, ('head', 'seq'), axis=1, tiled=True)]
    select_n x32 -> x1, other arithmetic: 96.7 us -> 0.06 us  [cube_body(): jnp.where(seq_half == 0, jnp.concatenate([shared_mine, shared_other], axi...]
    pallas_call x0 -> x11, Pallas kernels: none -> 89.8 us  [the longest x1 30.9 us: run_mix_backward(): pl.pallas_call(mix_backward, grid_spec=pltpu.PrefetchScalarGridSpec(num_s...]
  transfers between devices with their start and end apart: 23 -> 109, of which waited for: 16 -> 51; matrix products, arithmetic and copies ran while one was open for 8% -> 27% of each run, Pallas kernels for 0% -> 6%
where the time goes in v1:
time: 950 us; the launch traced here: 941 us
  waiting for transfers between devices  309 us (33%)
  starting transfers between devices  189 us (20%)
  matrix products  139 us (15%)
  local copies, waits for them, and re-layouts  113 us (12%)
  other arithmetic  98.1 us (10%)
  Pallas kernels  89.8 us (9%)
    ppermute x98, waiting for transfers between devices, flip(): return lax.ppermute(value, BOTH, [(i, i ^ mask) for i in range(DEVICES)])  283 us
    ppermute x98, starting transfers between devices, flip(): return lax.ppermute(value, BOTH, [(i, i ^ mask) for i in range(DEVICES)])  133 us
    dot_general x9, matrix products, mm_nt(): lax.dot_general(a, b, (((1,), (1,)), ((), ())), preferred_element_type=f32)  48.2 us
    dot_general x6, matrix products, mm(): return jnp.dot(a, b, preferred_element_type=f32)  46.6 us
    dot_general x6, matrix products, mm_tn(): lax.dot_general(a, b, (((0,), (0,)), ((), ())), preferred_element_type=f32)  44.2 us
    all_to_all x7, starting transfers between devices, exchange(): return lax.all_to_all(value, BOTH, split_axis=0, concat_axis=0, tiled=True)  37.5 us
    unnamed x201, local copies, waits for them, and re-layouts  33.1 us
    pallas_call x1, Pallas kernels, run_mix_backward(): pl.pallas_call(mix_backward, grid_spec=pltpu.PrefetchScalarGridSpec(num_s...  30.9 us
  transfers between devices with their start and end apart: 109, of which 51 were waited for; matrix products, arithmetic and copies ran while one was open for 27% of the time, Pallas kernels for 6%

profile of v1, /device:TPU:0, one launch (start us, length us, event | category | flops | bytes accessed | tf_op | source)
XLA Modules:
  0.0 941.2 jit_solution(4621666934042644624)
XLA Ops:
  14.8 9.1 collective-permute-done.1
  37.3 14.3 %collective-permute-done.6 = bf16[1,1,1,128,1024]{4,3,2,1,0:T(8,128)(2,1)S(1)} collective-permute-done((bf16[1,1,1,128,1024]{4,3,2,1,0:T(8,128)(2,1)S(1)}, bf16[1,1,1,128,1024]{4,3,2,1,0:T(8,128)(2,1)S(1)}, u32[]{:S(2)}, u32[]{:S(2)}) %collective-permute-start.6) | collective-permute-done | bytes 262176 | tf_op jit(solution)/shard_map/ppermute | solution.py:647
  66.6 11.7 %all-to-all-start = ((bf16[32,64,512]{2,1,0:T(8,128)(2,1)}), bf16[32,64,512]{2,1,0:T(8,128)(2,1)}, u32[]{:S(2)}, u32[]{:S(2)}) async-start(bf16[32,64,512]{2,1,0:T(8,128)(2,1)} %bitcast.4), calls=%async_computation | async-start | bytes 4194304 | tf_op jit(solution)/shard_map/all_to_all | solution.py:811
  81.9 7.5 collective-permute-done.10
  98.3 12.6 %collective-permute-start.12 = (bf16[512,3328]{1,0:T(8,128)(2,1)}, bf16[512,3328]{1,0:T(8,128)(2,1)}, u32[]{:S(2)}, u32[]{:S(2)}) collective-permute-start(bf16[512,3328]{1,0:T(8,128)(2,1)} %pad_maximum_fusion.6), channel_id=1, source_target_pairs={{0,16},{1,17},{2,18},{3,19},{4,20},{5,21},{6,22},{7,23},{8,24},{9,... | collective-permute-start | bytes 10223624 | tf_op jit(solution)/shard_map/ppermute | solution.py:647
  160.0 7.6 fusion.87.own_ref.own_tail_ref
  171.2 10.9 %fusion.88.s_ref.s_tail_ref = f32[2048,896]{1,0:T(8,128)} fusion(bf16[2048,2048]{1,0:T(8,128)(2,1)S(1)} %assemble.7, bf16[2048,896]{1,0:T(8,128)(2,1)S(1)} %assemble.8), kind=kOutput, calls=%fused_computation.292 | convolution fusion | flops 7516192768 | bytes 19398656 | tf_op jit(solution)/shard_map/dot_general | solution.py:815
  187.8 17.9 %mix_forward.1 = (bf16[2048,192]{1,0:T(8,128)(2,1)S(1)}, bf16[2048,192]{1,0:T(8,128)(2,1)S(1)}, f32[16,8,128]{2,1,0:T(8,128)S(1)}, bf16[16,256,192]{2,1,0:T(8,12...) custom-call(s32[3]{0:T(128)S(1)} %pad_add_fusion.info_ref.info, ...), custom_call_target="tpu_custom_call" | custom-call | flops 1000 | bytes 1000 | tf_op jit(solution)/shard_map/mix_forward/pallas_call | solution.py:1165
  232.9 20.1 %all-to-all-done.2 = bf16[32,64,256]{2,1,0:T(8,128)(2,1)} async-done(((bf16[32,64,256]{2,1,0:T(8,128)(2,1)}), bf16[32,64,256]{2,1,0:T(8,128)(2,1)}, u32[]{:S(2)}, u32[]{:S(2)}) %all-to-all-start.2) | async-done | bytes 1048608 | tf_op jit(solution)/shard_map/all_to_all | solution.py:811
  266.7 9.9 %collective-permute-done.21 = bf16[1,1,1,128,640]{4,3,2,1,0:T(8,128)(2,1)S(1)} collective-permute-done((bf16[1,1,1,128,640]{4,3,2,1,0:T(8,128)(2,1)S(1)}, bf16[1,1,1,128,640]{4,3,2,1,0:T(8,128)(2,1)S(1)}, u32[]{:S(2)}, u32[]{:S(2)}) %collective-permute-start.21) | collective-permute-done | bytes 163872 | tf_op jit(solution)/shard_map/ppermute | solution.py:647
  277.5 20.7 %collective-permute-done.20 = bf16[1,1,1,128,768]{4,3,2,1,0:T(8,128)(2,1)S(1)} collective-permute-done((bf16[1,1,1,128,768]{4,3,2,1,0:T(8,128)(2,1)S(1)}, bf16[1,1,1,128,768]{4,3,2,1,0:T(8,128)(2,1)S(1)}, u32[]{:S(2)}, u32[]{:S(2)}) %collective-permute-start.20) | collective-permute-done | bytes 196640 | tf_op jit(solution)/shard_map/ppermute | solution.py:647
  307.0 8.9 attend_forward.1
  328.6 12.1 %collective-permute-done.28 = bf16[2,1,2,128,640]{4,3,2,1,0:T(8,128)(2,1)S(1)} collective-permute-done((bf16[2,1,2,128,640]{4,3,2,1,0:T(8,128)(2,1)S(1)}, bf16[2,1,2,128,640]{4,3,2,1,0:T(8,128)(2,1)S(1)}, u32[]{:S(2)}, u32[]{:S(2)}) %collective-permute-start.28) | collective-permute-done | bytes 655392 | tf_op jit(solution)/shard_map/ppermute | solution.py:647
  354.6 8.2 collective-permute-done.30
  396.2 9.6 %collective-permute-done.37 = bf16[1,2,2,128,640]{4,3,2,1,0:T(8,128)(2,1)S(1)} collective-permute-done((bf16[1,2,2,128,640]{4,3,2,1,0:T(8,128)(2,1)S(1)}, bf16[1,2,2,128,640]{4,3,2,1,0:T(8,128)(2,1)S(1)}, u32[]{:S(2)}, u32[]{:S(2)}) %collective-permute-start.37) | collective-permute-done | bytes 655392 | tf_op jit(solution)/shard_map/ppermute | solution.py:647
  426.8 10.6 %fusion.89 = f32[2048,512]{0,1:T(8,128)} fusion(bf16[2048,2048]{1,0:T(8,128)(2,1)} %copy-done.6, bf16[2048,512]{1,0:T(8,128)(2,1)} %bitcast.51), kind=kOutput, calls=%fused_computation.293 | convolution fusion | flops 4294967296 | bytes 14680064 | tf_op jit(solution)/shard_map/dot_general | solution.py:815
  481.5 11.7 %collective-permute-done.54 = bf16[2,1,2,128,640]{4,3,2,1,0:T(8,128)(2,1)S(1)} collective-permute-done((bf16[2,1,2,128,640]{4,3,2,1,0:T(8,128)(2,1)S(1)}, bf16[2,1,2,128,640]{4,3,2,1,0:T(8,128)(2,1)S(1)}, u32[]{:S(2)}, u32[]{:S(2)}) %collective-permute-start.54) | collective-permute-done | bytes 655392 | tf_op jit(solution)/shard_map/ppermute | solution.py:647
  538.3 6.6 collective-permute-done.65
  547.6 8.1 collective-permute-done.69
  567.5 8.3 multiply_reduce_fusion
  579.7 7.0 convolution_convert_fusion.9
  614.4 8.9 attend_backward.1
  640.8 12.4 %collective-permute-done.86 = bf16[2,2,1,128,640]{4,3,2,1,0:T(8,128)(2,1)} collective-permute-done((bf16[2,2,1,128,640]{4,3,2,1,0:T(8,128)(2,1)}, bf16[2,2,1,128,640]{4,3,2,1,0:T(8,128)(2,1)}, u32[]{:S(2)}, u32[]{:S(2)}) %collective-permute-start.86) | collective-permute-done | bytes 655392 | tf_op jit(solution)/shard_map/ppermute | solution.py:647
  677.7 30.9 %mix_backward.1 = (bf16[2048,1408]{1,0:T(8,128)(2,1)}, f32[8,192]{1,0:T(8,128)S(1)}, f32[8,512]{1,0:T(8,128)S(1)}, f32[8,192]{1,0:T(8,128)S(1)}, f32[8,128]{1,0:T(8,128)S(1)}) custom-call(s32[3]{0:T(128)S(1)} %pad_add_fusion.info_ref.info, f32[2048,512]{1,0:T(8,128)} %fusion.87.own_ref.own_tail_ref, f32[2048,896]{1,0:T(8,128)} %fusion.88.s_ref.s_tail_ref, ...), custom_call_target="tpu_custom_call" | custom-call | flops 1000 | bytes 1000 | tf_op jit(solution)/shard_map/mix_backward/pallas_call | solution.py:1252
  713.7 12.7 %fusion.6 = bf16[2048,896]{1,0:T(8,128)(2,1)S(1)} fusion(bf16[2048,2048]{1,0:T(8,128)(2,1)} %copy-done.3, bf16[2048,1408]{1,0:T(8,128)(2,1)} %get-tuple-element.172), kind=kOutput, calls=%fused_computation.23 | convolution fusion | flops 7518027776 | bytes 15728640 | tf_op jit(solution)/shard_map/dot_general | solution.py:823
  730.7 8.1 convolution_convert_fusion
  738.9 7.0 assemble.13
  761.0 10.1 %convolution_convert_fusion.6 = bf16[2048,512]{1,0:T(8,128)(2,1)} fusion(bf16[2048,2048]{1,0:T(8,128)(2,1)} %copy-done.3, bf16[2048,1408]{1,0:T(8,128)(2,1)} %get-tuple-element.172), kind=kOutput, calls=%fused_computation.26 | convolution fusion | flops 4296015872 | bytes 12582912 | tf_op jit(solution)/shard_map/dot_general | solution.py:823
  771.1 9.2 convolution_convert_fusion.1
  791.6 27.7 %collective-permute-done.94 = bf16[2,1,2,128,1024]{4,3,2,1,0:T(8,128)(2,1)S(1)} collective-permute-done((bf16[2,1,2,128,1024]{4,3,2,1,0:T(8,128)(2,1)S(1)}, bf16[2,1,2,128,1024]{4,3,2,1,0:T(8,128)(2,1)S(1)}, u32[]{:S(2)}, u32[]{:S(2)}) %collective-permute-start.94) | collective-permute-done | bytes 1048608 | tf_op jit(solution)/shard_map/ppermute | solution.py:647
  849.9 11.7 %collective-permute-done.92 = bf16[1,1,2,128,1152]{4,3,2,1,0:T(8,128)(2,1)S(1)} collective-permute-done((bf16[1,1,2,128,1152]{4,3,2,1,0:T(8,128)(2,1)}, bf16[1,1,2,128,1152]{4,3,2,1,0:T(8,128)(2,1)S(1)}, u32[]{:S(2)}, u32[]{:S(2)}) %collective-permute-start.92) | collective-permute-done | bytes 589856 | tf_op jit(solution)/shard_map/ppermute | solution.py:647
  864.3 19.1 %collective-permute-done.96 = bf16[1,1,1,128,1024]{4,3,2,1,0:T(8,128)(2,1)S(1)} collective-permute-done((bf16[1,1,1,128,1024]{4,3,2,1,0:T(8,128)(2,1)S(1)}, bf16[1,1,1,128,1024]{4,3,2,1,0:T(8,128)(2,1)S(1)}, u32[]{:S(2)}, u32[]{:S(2)}) %collective-permute-start.96) | collective-permute-done | bytes 262176 | tf_op jit(solution)/shard_map/ppermute | solution.py:647
  (716 shorter events, 546.7 us)
Async XLA Ops:
  53.4 41.6 %collective-permute-start.9 = (bf16[1,2,2,128,1152]{4,3,2,1,0:T(8,128)(2,1)}, bf16[1,2,2,128,1152]{4,3,2,1,0:T(8,128)(2,1)}, u32[]{:S(2)}, u32[]{:S(2)}) collective-permute-start(bf16[1,2,2,128,1152]{4,3,2,1,0:T(8,128)(2,1)} %pad_maximum_fusion.18), channel_id=1, source_target_pairs={{0,4},{1,5},{2,6},{3,7},{4,0},{5,1},{6,2},{7,3},{8,12},{9,13},{10,... | collective-permute-start | bytes 3538952 | tf_op jit(solution)/shard_map/ppermute | solution.py:647
  56.1 38.9 %collective-permute-start.8 = (bf16[2,2,1,128,1152]{4,3,2,1,0:T(8,128)(2,1)}, bf16[2,2,1,128,1152]{4,3,2,1,0:T(8,128)(2,1)}, u32[]{:S(2)}, u32[]{:S(2)}) collective-permute-start(bf16[2,2,1,128,1152]{4,3,2,1,0:T(8,128)(2,1)} %pad_maximum_fusion.17), channel_id=1, source_target_pairs={{0,1},{1,0},{2,3},{3,2},{4,5},{5,4},{6,7},{7,6},{8,9},{9,8},{10,11... | collective-permute-start | bytes 3538952 | tf_op jit(solution)/shard_map/ppermute | solution.py:647
  65.0 24.4 %collective-permute-start.10 = (bf16[2,1,2,128,1024]{4,3,2,1,0:T(8,128)(2,1)}, bf16[2,1,2,128,1024]{4,3,2,1,0:T(8,128)(2,1)}, u32[]{:S(2)}, u32[]{:S(2)}) collective-permute-start(bf16[2,1,2,128,1024]{4,3,2,1,0:T(8,128)(2,1)} %pad_maximum_fusion.19), channel_id=1, source_target_pairs={{0,2},{1,3},{2,0},{3,1},{4,6},{5,7},{6,4},{7,5},{8,10},{9,11},{10,... | collective-permute-start | bytes 3145736 | tf_op jit(solution)/shard_map/ppermute | solution.py:647
  66.6 62.2 %all-to-all-start = ((bf16[32,64,512]{2,1,0:T(8,128)(2,1)}), bf16[32,64,512]{2,1,0:T(8,128)(2,1)}, u32[]{:S(2)}, u32[]{:S(2)}) async-start(bf16[32,64,512]{2,1,0:T(8,128)(2,1)} %bitcast.4), calls=%async_computation | async-start | bytes 4194304 | tf_op jit(solution)/shard_map/all_to_all | solution.py:811
  81.5 53.2 %collective-permute-start.11 = (bf16[512,3328]{1,0:T(8,128)(2,1)}, bf16[512,3328]{1,0:T(8,128)(2,1)S(1)}, u32[]{:S(2)}, u32[]{:S(2)}) collective-permute-start(bf16[512,3328]{1,0:T(8,128)(2,1)} %pad_maximum_fusion.5), channel_id=1, source_target_pairs={{0,16},{1,17},{2,18},{3,19},{4,20},{5,21},{6,22},{7,23},{8,24},{9,... | collective-permute-start | bytes 10223624 | tf_op jit(solution)/shard_map/ppermute | solution.py:647
  98.3 36.4 %collective-permute-start.12 = (bf16[512,3328]{1,0:T(8,128)(2,1)}, bf16[512,3328]{1,0:T(8,128)(2,1)}, u32[]{:S(2)}, u32[]{:S(2)}) collective-permute-start(bf16[512,3328]{1,0:T(8,128)(2,1)} %pad_maximum_fusion.6), channel_id=1, source_target_pairs={{0,16},{1,17},{2,18},{3,19},{4,20},{5,21},{6,22},{7,23},{8,24},{9,... | collective-permute-start | bytes 10223624 | tf_op jit(solution)/shard_map/ppermute | solution.py:647
  131.3 52.2 %all-to-all-start.1 = ((bf16[32,64,320]{2,1,0:T(8,128)(2,1)}), bf16[32,64,320]{2,1,0:T(8,128)(2,1)}, u32[]{:S(2)}, u32[]{:S(2)}) async-start(bf16[32,64,320]{2,1,0:T(8,128)(2,1)} %bitcast.307), calls=%async_computation.1 | async-start | bytes 3145728 | tf_op jit(solution)/shard_map/all_to_all | solution.py:811
  153.5 30.0 %collective-permute-start.13 = (bf16[128,2048]{1,0:T(8,128)(2,1)}, bf16[128,2048]{1,0:T(8,128)(2,1)}, u32[]{:S(2)}, u32[]{:S(2)}) collective-permute-start(bf16[128,2048]{1,0:T(8,128)(2,1)} %bitcast.11), channel_id=1, source_target_pairs={{0,0},{1,1},{2,2},{3,3},{4,4},{5,5},{6,6},{7,7},{8,16},{9,17},{10,... | collective-permute-start | bytes 1572872 | tf_op jit(solution)/shard_map/ppermute | solution.py:655
  219.8 33.2 %all-to-all-start.2 = ((bf16[32,64,256]{2,1,0:T(8,128)(2,1)}), bf16[32,64,256]{2,1,0:T(8,128)(2,1)}, u32[]{:S(2)}, u32[]{:S(2)}) async-start(bf16[32,64,256]{2,1,0:T(8,128)(2,1)} %bitcast.308), calls=%async_computation.2 | async-start | bytes 2097152 | tf_op jit(solution)/shard_map/all_to_all | solution.py:811
  230.4 85.6 %collective-permute-start.26 = (bf16[1024,2048]{1,0:T(8,128)(2,1)}, bf16[1024,2048]{1,0:T(8,128)(2,1)}, u32[]{:S(2)}, u32[]{:S(2)}) collective-permute-start(bf16[1024,2048]{1,0:T(8,128)(2,1)} %multiply_convert_fusion), channel_id=1, source_target_pairs={{0,16},{1,17},{2,18},{3,19},{4,20},{5,21},{6,22},{7,23},{8,24},{9,... | collective-permute-start | bytes 12582920 | tf_op jit(solution)/shard_map/ppermute | solution.py:647
  255.8 86.7 %all-to-all-start.3 = ((bf16[32,64,512]{2,1,0:T(8,128)(2,1)}), bf16[32,64,512]{2,1,0:T(8,128)(2,1)}, u32[]{:S(2)}, u32[]{:S(2)}) async-start(bf16[32,64,512]{2,1,0:T(8,128)(2,1)} %bitcast.305), calls=%async_computation.3 | async-start | bytes 4194304 | tf_op jit(solution)/shard_map/all_to_all | solution.py:811
  260.8 37.5 %collective-permute-start.20 = (bf16[1,1,1,128,768]{4,3,2,1,0:T(8,128)(2,1)S(1)}, bf16[1,1,1,128,768]{4,3,2,1,0:T(8,128)(2,1)S(1)}, u32[]{:S(2)}, u32[]{:S(2)}) collective-permute-start(bf16[1,1,1,128,768]{4,3,2,1,0:T(8,128)(2,1)S(1)} %slice_bitcast_fusion.8), channel_id=1, source_target_pairs={{0,4},{1,5},{2,6},{3,7},{4,0},{5,1},{6,2},{7,3},{8,12},{9,13},{10,... | collective-permute-start | bytes 589832 | tf_op jit(solution)/shard_map/ppermute | solution.py:647
  325.4 68.8 %collective-permute-start.38 = (bf16[2,1,2,128,640]{4,3,2,1,0:T(8,128)(2,1)}, bf16[2,1,2,128,640]{4,3,2,1,0:T(8,128)(2,1)}, u32[]{:S(2)}, u32[]{:S(2)}) collective-permute-start(bf16[2,1,2,128,640]{4,3,2,1,0:T(8,128)(2,1)} %constant_dynamic-update-slice_fusion.10), channel_id=1, source_target_pairs={{0,2},{1,3},{2,0},{3,1},{4,6},{5,7},{6,4},{7,5},{8,10},{9,11},{10,... | collective-permute-start | bytes 1966088 | tf_op jit(solution)/shard_map/ppermute | solution.py:647
  380.6 27.0 %collective-permute-start.36 = (bf16[2,2,1,128,768]{4,3,2,1,0:T(8,128)(2,1)}, bf16[2,2,1,128,768]{4,3,2,1,0:T(8,128)(2,1)S(1)}, u32[]{:S(2)}, u32[]{:S(2)}) collective-permute-start(bf16[2,2,1,128,768]{4,3,2,1,0:T(8,128)(2,1)} %constant_dynamic-update-slice_fusion.6), channel_id=1, source_target_pairs={{0,1},{1,0},{2,3},{3,2},{4,5},{5,4},{6,7},{7,6},{8,9},{9,8},{10,11... | collective-permute-start | bytes 2359304 | tf_op jit(solution)/shard_map/ppermute | solution.py:647
  565.7 34.0 %collective-permute-start.79 = (bf16[1024,2048]{1,0:T(8,128)(2,1)}, bf16[1024,2048]{1,0:T(8,128)(2,1)}, u32[]{:S(2)}, u32[]{:S(2)}) collective-permute-start(bf16[1024,2048]{1,0:T(8,128)(2,1)} %convolution_convert_fusion.3), channel_id=1, source_target_pairs={{0,16},{1,17},{2,18},{3,19},{4,20},{5,21},{6,22},{7,23},{8,24},{9,... | collective-permute-start | bytes 12582920 | tf_op jit(solution)/shard_map/ppermute | solution.py:647
  590.0 123.7 %all-to-all-start.4 = ((bf16[32,64,512]{2,1,0:T(8,128)(2,1)}), bf16[32,64,512]{2,1,0:T(8,128)(2,1)}, u32[]{:S(2)}, u32[]{:S(2)}) async-start(bf16[32,64,512]{2,1,0:T(8,128)(2,1)} %bitcast.315), calls=%async_computation.4 | async-start | bytes 4194304 | tf_op jit(solution)/shard_map/all_to_all | solution.py:811
  596.2 37.6 %collective-permute-start.76 = (f32[16,128]{1,0:T(8,128)}, f32[16,128]{1,0:T(8,128)}, u32[]{:S(2)}, u32[]{:S(2)}) collective-permute-start(f32[16,128]{1,0:T(8,128)} %add_add_fusion), channel_id=1, source_target_pairs={{0,2},{1,3},{2,0},{3,1},{4,6},{5,7},{6,4},{7,5},{8,10},{9,11},{10,... | collective-permute-start | bytes 24584 | tf_op jit(solution)/shard_map/ppermute | solution.py:647
  598.1 37.2 %collective-permute-start.77 = (f32[16,128]{1,0:T(8,128)}, f32[16,128]{1,0:T(8,128)}, u32[]{:S(2)}, u32[]{:S(2)}) collective-permute-start(f32[16,128]{1,0:T(8,128)} %add_add_fusion), channel_id=1, source_target_pairs={{0,4},{1,5},{2,6},{3,7},{4,0},{5,1},{6,2},{7,3},{8,12},{9,13},{10,... | collective-permute-start | bytes 24584 | tf_op jit(solution)/shard_map/ppermute | solution.py:647
  599.5 35.7 %collective-permute-start.78 = (f32[16,128]{1,0:T(8,128)}, f32[16,128]{1,0:T(8,128)}, u32[]{:S(2)}, u32[]{:S(2)}) collective-permute-start(f32[16,128]{1,0:T(8,128)} %add_add_fusion), channel_id=1, source_target_pairs={{0,6},{1,7},{2,4},{3,5},{4,2},{5,3},{6,0},{7,1},{8,14},{9,15},{10,... | collective-permute-start | bytes 24584 | tf_op jit(solution)/shard_map/ppermute | solution.py:647
  608.1 30.5 %collective-permute-start.83 = (bf16[2,1,2,128,640]{4,3,2,1,0:T(8,128)(2,1)}, bf16[2,1,2,128,640]{4,3,2,1,0:T(8,128)(2,1)}, u32[]{:S(2)}, u32[]{:S(2)}) collective-permute-start(bf16[2,1,2,128,640]{4,3,2,1,0:T(8,128)(2,1)} %slice.809), channel_id=1, source_target_pairs={{0,2},{1,3},{2,0},{3,1},{4,6},{5,7},{6,4},{7,5},{8,10},{9,11},{10,... | collective-permute-start | bytes 1966088 | tf_op jit(solution)/shard_map/ppermute | solution.py:647
  632.3 24.2 %collective-permute-start.80 = (bf16[1,2,2,128,768]{4,3,2,1,0:T(8,128)(2,1)}, bf16[1,2,2,128,768]{4,3,2,1,0:T(8,128)(2,1)}, u32[]{:S(2)}, u32[]{:S(2)}) collective-permute-start(bf16[1,2,2,128,768]{4,3,2,1,0:T(8,128)(2,1)} %slice.803), channel_id=1, source_target_pairs={{0,4},{1,5},{2,6},{3,7},{4,0},{5,1},{6,2},{7,3},{8,12},{9,13},{10,... | collective-permute-start | bytes 2359304 | tf_op jit(solution)/shard_map/ppermute | solution.py:647
  750.9 29.4 %collective-permute-start.90 = (bf16[1024,3200]{1,0:T(8,128)(2,1)}, bf16[1024,3200]{1,0:T(8,128)(2,1)}, u32[]{:S(2)}, u32[]{:S(2)}) collective-permute-start(bf16[1024,3200]{1,0:T(8,128)(2,1)} %pad_maximum_fusion), channel_id=1, source_target_pairs={{0,16},{1,17},{2,18},{3,19},{4,20},{5,21},{6,22},{7,23},{8,24},{9,... | collective-permute-start | bytes 19660808 | tf_op jit(solution)/shard_map/ppermute | solution.py:647
  756.2 83.7 %all-to-all-start.5 = ((bf16[32,64,635]{2,1,0:T(8,128)(2,1)}), bf16[32,64,635]{2,1,0:T(8,128)(2,1)S(1)}, u32[]{:S(2)}, u32[]{:S(2)}) async-start(bf16[32,64,635]{2,1,0:T(8,128)(2,1)} %bitcast.101), calls=%async_computation.5 | async-start | bytes 5242880 | tf_op jit(solution)/shard_map/all_to_all | solution.py:811
  784.9 34.5 %collective-permute-start.94 = (bf16[2,1,2,128,1024]{4,3,2,1,0:T(8,128)(2,1)S(1)}, bf16[2,1,2,128,1024]{4,3,2,1,0:T(8,128)(2,1)S(1)}, u32[]{:S(2)}, u32[]{:S(2)}) collective-permute-start(bf16[2,1,2,128,1024]{4,3,2,1,0:T(8,128)(2,1)S(1)} %slice.836), channel_id=1, source_target_pairs={{0,2},{1,3},{2,0},{3,1},{4,6},{5,7},{6,4},{7,5},{8,10},{9,11},{10,... | collective-permute-start | bytes 3145736 | tf_op jit(solution)/shard_map/ppermute | solution.py:647
  787.9 45.8 %collective-permute-start.91 = (bf16[1,2,2,128,1152]{4,3,2,1,0:T(8,128)(2,1)S(1)}, bf16[1,2,2,128,1152]{4,3,2,1,0:T(8,128)(2,1)S(1)}, u32[]{:S(2)}, u32[]{:S(2)}) collective-permute-start(bf16[1,2,2,128,1152]{4,3,2,1,0:T(8,128)(2,1)S(1)} %slice.830), channel_id=1, source_target_pairs={{0,4},{1,5},{2,6},{3,7},{4,0},{5,1},{6,2},{7,3},{8,12},{9,13},{10,... | collective-permute-start | bytes 3538952 | tf_op jit(solution)/shard_map/ppermute | solution.py:647
  789.4 35.8 %collective-permute-start.97 = (bf16[2,2,1,128,1024]{4,3,2,1,0:T(8,128)(2,1)S(1)}, bf16[2,2,1,128,1024]{4,3,2,1,0:T(8,128)(2,1)S(1)}, u32[]{:S(2)}, u32[]{:S(2)}) collective-permute-start(bf16[2,2,1,128,1024]{4,3,2,1,0:T(8,128)(2,1)S(1)} %slice.842), channel_id=1, source_target_pairs={{0,1},{1,0},{2,3},{3,2},{4,5},{5,4},{6,7},{7,6},{8,9},{9,8},{10,11... | collective-permute-start | bytes 3145736 | tf_op jit(solution)/shard_map/ppermute | solution.py:647
  835.8 25.7 %collective-permute-start.92 = (bf16[1,1,2,128,1152]{4,3,2,1,0:T(8,128)(2,1)}, bf16[1,1,2,128,1152]{4,3,2,1,0:T(8,128)(2,1)S(1)}, u32[]{:S(2)}, u32[]{:S(2)}) collective-permute-start(bf16[1,1,2,128,1152]{4,3,2,1,0:T(8,128)(2,1)} %slice.832), channel_id=1, source_target_pairs={{0,2},{1,3},{2,0},{3,1},{4,6},{5,7},{6,4},{7,5},{8,10},{9,11},{10,... | collective-permute-start | bytes 1769480 | tf_op jit(solution)/shard_map/ppermute | solution.py:647
  839.8 85.0 %all-to-all-start.6 = ((bf16[32,64,512]{2,1,0:T(8,128)(2,1)}), bf16[32,64,512]{2,1,0:T(8,128)(2,1)}, u32[]{:S(2)}, u32[]{:S(2)}) async-start(bf16[32,64,512]{2,1,0:T(8,128)(2,1)} %bitcast.316), calls=%async_computation.6 | async-start | bytes 4194304 | tf_op jit(solution)/shard_map/all_to_all | solution.py:811
  845.0 38.4 %collective-permute-start.96 = (bf16[1,1,1,128,1024]{4,3,2,1,0:T(8,128)(2,1)S(1)}, bf16[1,1,1,128,1024]{4,3,2,1,0:T(8,128)(2,1)S(1)}, u32[]{:S(2)}, u32[]{:S(2)}) collective-permute-start(bf16[1,1,1,128,1024]{4,3,2,1,0:T(8,128)(2,1)S(1)} %slice.840), channel_id=1, source_target_pairs={{0,4},{1,5},{2,6},{3,7},{4,0},{5,1},{6,2},{7,3},{8,12},{9,13},{10,... | collective-permute-start | bytes 786440 | tf_op jit(solution)/shard_map/ppermute | solution.py:647
  848.3 35.1 %collective-permute-start.99 = (bf16[1,1,1,128,1024]{4,3,2,1,0:T(8,128)(2,1)S(1)}, bf16[1,1,1,128,1024]{4,3,2,1,0:T(8,128)(2,1)S(1)}, u32[]{:S(2)}, u32[]{:S(2)}) collective-permute-start(bf16[1,1,1,128,1024]{4,3,2,1,0:T(8,128)(2,1)S(1)} %slice.846), channel_id=1, source_target_pairs={{0,2},{1,3},{2,0},{3,1},{4,6},{5,7},{6,4},{7,5},{8,10},{9,11},{10,... | collective-permute-start | bytes 786440 | tf_op jit(solution)/shard_map/ppermute | solution.py:647
  891.8 31.1 %collective-permute-start.101 = (bf16[64,1152]{1,0:T(8,128)(2,1)}, bf16[64,1152]{1,0:T(8,128)(2,1)}, u32[]{:S(2)}, u32[]{:S(2)}) collective-permute-start(bf16[64,1152]{1,0:T(8,128)(2,1)} %fusion.53), channel_id=1, source_target_pairs={{0,8},{1,9},{2,10},{3,11},{4,12},{5,13},{6,14},{7,15},{8,0},{9,1},... | collective-permute-start | bytes 442376 | tf_op jit(solution)/shard_map/ppermute | solution.py:647
  909.5 27.5 %collective-permute-start.100 = (bf16[128,2048]{1,0:T(8,128)(2,1)}, bf16[128,2048]{1,0:T(8,128)(2,1)}, u32[]{:S(2)}, u32[]{:S(2)}) collective-permute-start(bf16[128,2048]{1,0:T(8,128)(2,1)} %get-tuple-element.214), channel_id=1, source_target_pairs={{0,0},{1,1},{2,2},{3,3},{4,4},{5,5},{6,6},{7,7},{8,16},{9,17},{10,... | collective-permute-start | bytes 1572872 | tf_op jit(solution)/shard_map/ppermute | solution.py:655
  (171 other events, 1756.6 us)

commit v2 on v1

--- a/solution.py
+++ b/solution.py
@@ -636,7 +636,8 @@
 BLOCK = 128
 BIT_C, BIT_ZH, BIT_ZL, BIT_Y, BIT_X = 16, 8, 4, 2, 1
 DEVICES = 32
-BOTH = ("head", "seq")
+BOTH = ("head", "half", "cube")
+GROUP = ("head", "cube")
 CUBE_ORDERS = ((0, 1, 2), (1, 2, 0), (2, 0, 1))
 CUBE_BITS = (BIT_ZL, BIT_Y, BIT_X)
 bf16 = jnp.bfloat16
@@ -651,8 +652,14 @@
     pairs = []
     for i in range(DEVICES):
         core, half = (i // BIT_C) % 2, (i // BIT_ZH) % 2
-        pairs.append((i, i - core * BIT_C - half * BIT_ZH + half * BIT_C + core * BIT_ZH))
-    return lax.ppermute(value, BOTH, pairs)
+        if core != half:
+            pairs.append((i, i ^ (BIT_C + BIT_ZH)))
+    stays = lax.axis_index("head") == lax.axis_index("half")
+    return jnp.where(stays, value, lax.ppermute(value, BOTH, pairs))
+
+
+def joint(*values):
+    return lax.optimization_barrier(values)
 
 
 def column_parts(width):
@@ -663,28 +670,19 @@
     return [(edges[i], edges[i + 1]) for i in range(3)]
 
 
-def joint(*values):
-    return lax.optimization_barrier(values)
-
-
-def column_parts(width):
-    lanes = width // 128
-    first = -(-lanes // 3)
-    second = -(-(lanes - first) // 2)
-    edges = (0, first * 128, (first + second) * 128, width)
-    return [(edges[i], edges[i + 1]) for i in range(3)]
-
-
-def assemble(pieces, moves, shape, info):
-    count = len(pieces)
+def assemble(pieces, outputs, info):
+    count, made = len(pieces), len(outputs)
+    moves = [(to, *move) for to, (_, _, out_moves) in enumerate(outputs) for move in out_moves]
 
     def kernel(info_ref, *refs):
-        out, sems = refs[count], refs[count + 1]
+        sems = refs[count + made]
         copies = []
-        for at, (number, source, target) in enumerate(moves):
+        for at, (to, number, source, target) in enumerate(moves):
             copies.append(
                 pltpu.make_async_copy(
-                    refs[number].at[source(info_ref)], out.at[target(info_ref)], sems.at[at]
+                    refs[number].at[source(info_ref)],
+                    refs[count + to].at[target(info_ref)],
+                    sems.at[at],
                 )
             )
         for copy in copies:
@@ -692,13 +690,13 @@
         for copy in copies:
             copy.wait()
 
-    size = math.prod(shape) * 2
+    size = sum(math.prod(shape) * jnp.dtype(kind).itemsize for shape, kind, _ in outputs)
     return pl.pallas_call(
         kernel,
         in_specs=[pl.BlockSpec(memory_space=pltpu.SMEM)]
-        + [pl.BlockSpec(memory_space=pl.ANY)] * count,
-        out_specs=pl.BlockSpec(memory_space=pltpu.VMEM),
-        out_shape=jax.ShapeDtypeStruct(shape, bf16),
+        + [pl.BlockSpec(memory_space=pltpu.HBM)] * count,
+        out_specs=[pl.BlockSpec(memory_space=pltpu.VMEM)] * made,
+        out_shape=[jax.ShapeDtypeStruct(shape, kind) for shape, kind, _ in outputs],
         scratch_shapes=[pltpu.SemaphoreType.DMA((len(moves),))],
         compiler_params=pltpu.CompilerParams(vmem_limit_bytes=2 * size + 8 * 1024 * 1024),
         cost_estimate=LITTLE,
@@ -706,43 +704,72 @@
     )(info, *pieces)
 
 
+def reordered_rows(value, info):
+    moves = []
+    for block in range(value.shape[0] // BLOCK):
+
+        def goal(ref, block=block):
+            row = pl.multiple_of((ref[2] ^ block) * BLOCK, BLOCK)
+            return (pl.ds(row, BLOCK), slice(None))
+
+        moves.append((0, fixed(block * BLOCK, BLOCK, 0, value.shape[1]), goal))
+    return assemble([value], [(value.shape, value.dtype, moves)], info)[0]
+
+
 def fixed(row, rows, column, columns):
     return lambda info: (pl.ds(row, rows), pl.ds(column, columns))
 
 
 class Gather:
-    def __init__(self, value, edges):
-        self.rows, self.step = value.shape[0], 0
-        self.state = ([value[None, None, None, :, a:b] for a, b in edges], None)
+    def __init__(self, value, edges, info):
+        self.rows, self.width, self.step = value.shape[0], value.shape[1], 0
+        self.edges, self.info = edges, info
+        self.joined = None
+        self.state = ([value[:, a:b] for a, b in edges], None)
 
     def hop(self):
         parts, received = self.state
         if received is not None:
-            parts = [
-                jnp.concatenate([part, got], axis=order[self.step - 1])
-                for part, got, order in zip(parts, received, CUBE_ORDERS)
-            ]
+            parts = self.stacked(parts, received)
         sent = [
             flip(part, CUBE_BITS[order[self.step]]) for part, order in zip(parts, CUBE_ORDERS)
         ]
         self.state = (parts, sent)
         self.step += 1
 
+    def stacked(self, parts, received):
+        rows = parts[0].shape[0]
+        outputs, side = [], []
+        for i, (a, b) in enumerate(self.edges):
+            own, got = fixed(0, rows, 0, b - a), fixed(rows, rows, 0, b - a)
+            outputs.append(((2 * rows, b - a), bf16, [(i, own, own), (3 + i, own, got)]))
+            side.append((i, own, fixed(0, rows, a, b - a)))
+            side.append((3 + i, own, fixed(rows, rows, a, b - a)))
+        if self.step == 2:
+            outputs.append(((2 * rows, self.width), bf16, side))
+        result = assemble(parts + received, outputs, self.info)
+        if self.step == 2:
+            self.joined = result[3]
+        return list(result[:3])
+
     def pieces(self):
         while self.step < 3:
             self.hop()
-        near, far = [[part.reshape(4 * self.rows, -1) for part in parts] for parts in self.state]
-        crossed = [flip(jnp.concatenate(parts, axis=1), BIT_C) for parts in (near, far)]
+        near, far = self.state
+        side = [(i, fixed(0, 4 * self.rows, 0, b - a), fixed(0, 4 * self.rows, a, b - a)) for i, (a, b) in enumerate(self.edges)]
+        (far_joined,) = assemble(
+            far, [((4 * self.rows, self.width), bf16, side)], self.info
+        )
+        crossed = [flip(self.joined, BIT_C), flip(far_joined, BIT_C)]
         return near + far + crossed
 
 
 def piece_blocks(part, far):
-    last = CUBE_ORDERS[part][2]
-    if last == 0:
-        return [(0, 4 * far, 4)]
-    if last == 1:
-        return [(2 * z, 4 * z + 2 * far, 2) for z in range(2)]
-    return [(i, 2 * i + far, 1) for i in range(4)]
+    axes = [CUBE_BITS[axis] for axis in CUBE_ORDERS[part]]
+    return [
+        (block, (block % 2) * axes[0] + (block // 2) * axes[1] + far * axes[2], 1)
+        for block in range(4)
+    ]
 
 
 def gathered(gather, width, info):
@@ -761,11 +788,11 @@
                         fixed((half * 8 + place) * rows, blocks * rows, a, b - a),
                     )
                 )
-    return assemble(pieces, moves, (16 * rows, width), info)
-
-
-def gather_start(value):
-    return Gather(value, column_parts(value.shape[1]))
+    return assemble(pieces, [((16 * rows, width), bf16, moves)], info)[0]
+
+
+def gather_start(value, info):
+    return Gather(value, column_parts(value.shape[1]), info)
 
 
 class Scatter:
@@ -774,30 +801,53 @@
         self.step = 0
         self.state = (own_half, flip(other_half.astype(bf16), BIT_C))
 
-    def summed(self):
+    def pairs(self):
         kept, received = self.state
         if self.step == 0:
-            value = kept.astype(f32) + received.astype(f32)
             shape = (2, 2, 2, self.total_rows // 8, self.width)
-            value = value.reshape(shape)
-            return [value[..., a:b] for a, b in column_parts(self.width)]
-        return [near.astype(f32) + got.astype(f32) for near, got in zip(kept, received)]
+            edges = column_parts(self.width)
+            kept = [kept.reshape(shape)[..., a:b] for a, b in edges]
+            received = [received.reshape(shape)[..., a:b] for a, b in edges]
+        halves = []
+        for part, got, order in zip(kept, received, CUBE_ORDERS):
+            axis = order[self.step]
+            halves.append(
+                [
+                    (
+                        lax.slice_in_dim(part, i, i + 1, axis=axis).astype(f32)
+                        + lax.slice_in_dim(got, i, i + 1, axis=axis).astype(f32)
+                    ).astype(bf16)
+                    for i in (0, 1)
+                ]
+            )
+        return halves
 
     def hop(self):
-        near, sent = [], []
-        for part, order in zip(self.summed(), CUBE_ORDERS):
-            axis = order[self.step]
-            part = part.astype(bf16)
-            near.append(lax.slice_in_dim(part, 0, 1, axis=axis))
-            sent.append(flip(lax.slice_in_dim(part, 1, 2, axis=axis), CUBE_BITS[axis]))
+        halves = self.pairs()
+        sent = [
+            flip(far, CUBE_BITS[order[self.step]])
+            for (_, far), order in zip(halves, CUBE_ORDERS)
+        ]
+        self.state = ([near for near, _ in halves], sent)
+        self.step += 1
+
+    def then(self, *values):
+        near, sent = self.state
+        near, values = joint(near, values)
         self.state = (near, sent)
-        self.step += 1
+        return values
 
     def result(self):
         while self.step < 3:
             self.hop()
         rows = self.total_rows // 8
-        return jnp.concatenate([part.reshape(rows, -1) for part in self.summed()], axis=1)
+        return jnp.concatenate(
+            [
+                (near.astype(f32) + got.astype(f32)).reshape(rows, -1)
+                for near, got in zip(*self.state)
+            ],
+            axis=1,
+        )
 
 
 def group_sum(value):
@@ -808,7 +858,7 @@
 
 
 def exchange(value):
-    return lax.all_to_all(value, BOTH, split_axis=0, concat_axis=0, tiled=True)
+    return lax.all_to_all(value, GROUP, split_axis=0, concat_axis=0, tiled=True)
 
 
 def mm(a, b):
@@ -985,9 +1035,8 @@
     taps_m_ref,
     vec_ref,
     lanes_ref,
-    y_ref,
-    g_inner_ref,
-    scales_ref,
+    g_y_ref,
+    g_z_ref,
     state_ref,
     dq_ref,
     dk_ref,
@@ -1021,7 +1070,6 @@
     def unturned(value):
         return value * cosine - pltpu.roll(value, HD // 2, 1) * sine
 
-    gate = own_ref[:, :OWN]
     x_raw = own_ref[:, OWN : 2 * OWN]
     m_raw = s_ref[:, : 2 * NS]
     first = block == 0
@@ -1042,15 +1090,7 @@
     cum, last, reach = block_decays(cum_col_ref[...], cum_row_ref[0], lane)
     scaled = step * x
 
-    inv, dots = scales_ref[:, 0:1], scales_ref[:, 1:2]
-    y = y_ref[...].astype(f32)
-    g_inner = g_inner_ref[...]
-    gate_sig = logistic(gate)
-    gate_silu = gate * gate_sig
-    normed = y * gate_silu * inv
-    g_gated = inv * (vec_ref[2:3] * g_inner - normed * dots)
-    g_y = (g_gated * gate_silu).astype(bf16).astype(f32)
-    g_z = g_gated * y * gate_sig * (1.0 + gate * (1.0 - gate_sig))
+    g_y = g_y_ref[...].astype(f32)
 
     inter = k_nt(c_map, b_map)
     g_inter = jnp.zeros((BLOCK, BLOCK), f32)
@@ -1091,14 +1131,13 @@
         acc_m_ref[tap : tap + 1] += jnp.sum(gs_m * m_pad[at : at + BLOCK], axis=0, keepdims=True)
     acc_x_ref[KC : KC + 1] += jnp.sum(gs_x, axis=0, keepdims=True)
     acc_m_ref[KC : KC + 1] += jnp.sum(gs_m, axis=0, keepdims=True)
-    acc_v_ref[0:1] += jnp.sum(normed * g_inner, axis=0, keepdims=True)
-    acc_v_ref[1:2] += jnp.sum(g_y * x, axis=0, keepdims=True)
+    acc_v_ref[0:1] += jnp.sum(g_y * x, axis=0, keepdims=True)
     acc_s_ref[0:1] += jnp.sum(g_step, axis=0, keepdims=True)
 
     here = (block // 8) == info[1]
-    g_q = jnp.where(here, unturned(dq_ref[...]), 0.0)
+    g_q = jnp.where(here, dq_ref[...].astype(f32), 0.0)
     at = 2 * OWN
-    g_all_ref[:, :at] = jnp.concatenate([g_z, g_x_raw], axis=1).astype(bf16)
+    g_all_ref[:, :at] = jnp.concatenate([g_z_ref[...].astype(f32), g_x_raw], axis=1).astype(bf16)
     for piece in (g_q, g_m_raw, unturned(dk_ref[...]), dv_ref[...], g_step):
         g_all_ref[:, at : at + piece.shape[1]] = piece.astype(bf16)
         at += piece.shape[1]
@@ -1124,7 +1163,9 @@
     log_ref[0] = jnp.broadcast_to(top + jnp.log(total), (8, BLOCK))
 
 
-def attend_backward(info, q_ref, k_ref, v_ref, out_f_ref, log_ref, g_ref, dq_ref, dk_ref, dv_ref):
+def attend_backward(
+    info, q_ref, k_ref, v_ref, out_f_ref, log_ref, g_ref, cos_ref, sin_ref, dq_ref, dk_ref, dv_ref
+):
     @pl.when(pl.program_id(0) == 0)
     def _():
         dk_ref[...] = jnp.zeros_like(dk_ref)
@@ -1137,7 +1178,8 @@
     g_scores = (probs * (k_nt(v_ref[...], grads) - delta)).astype(bf16)
     dv_ref[...] += k_mm(probs.astype(bf16), grads)
     dk_ref[...] += k_mm(g_scores, queries) * (HD**-0.5)
-    dq_ref[...] = (k_tn(g_scores, keys) * (HD**-0.5)).astype(bf16).astype(f32)
+    dq = (k_tn(g_scores, keys) * (HD**-0.5)).astype(bf16).astype(f32)
+    dq_ref[...] = (dq * cos_ref[...] - pltpu.roll(dq, HD // 2, 1) * sin_ref[...]).astype(bf16)
 
 
 def rows_at(width, column=0):
@@ -1220,9 +1262,8 @@
     taps_m,
     vec,
     lanes,
-    y,
-    g_inner,
-    scales,
+    g_y,
+    g_z,
     states,
     dq,
     dk,
@@ -1247,7 +1288,7 @@
         return pl.BlockSpec((TAIL, width), where)
 
     def query_rows(i, s):
-        return ((count - 1 - i) % 8, 0)
+        return (((count - 1 - i) ^ s[0]) % 8, 0)
 
     return pl.pallas_call(
         mix_backward,
@@ -1269,7 +1310,6 @@
                 whole(8, 128),
                 rows_back(count, OWN),
                 rows_back(count, OWN),
-                plain(8),
                 plain3(NS, OWN),
                 pl.BlockSpec((BLOCK, HD), query_rows),
                 plain(HD),
@@ -1312,9 +1352,8 @@
         taps_m,
         vec,
         lanes,
-        y,
-        g_inner,
-        scales,
+        g_y,
+        g_z,
         states,
         dq,
         dk,
@@ -1357,7 +1396,7 @@
     )(info, queries, keys, values)
 
 
-def run_attend_backward(info, queries, keys, values, out_f, logs, grads):
+def run_attend_backward(info, queries, keys, values, out_f, logs, grads, cosine, sine):
     length = keys.shape[0]
     half = length // 2
     count = half // BLOCK
@@ -1373,22 +1412,24 @@
                 pl.BlockSpec((BLOCK, HD), lambda i, s: (i, 0)),
                 pl.BlockSpec((1, 8, BLOCK), lambda i, s: (i, 0, 0)),
                 own_rows(HD),
+                own_queries(HD),
+                own_queries(HD),
             ],
             out_specs=[
-                pl.BlockSpec((BLOCK, HD), lambda i, s: (i, 0)),
+                own_rows(HD),
                 whole(length, HD),
                 whole(length, HD),
             ],
         ),
         out_shape=[
-            jax.ShapeDtypeStruct((half, HD), f32),
+            jax.ShapeDtypeStruct((half, HD), bf16),
             jax.ShapeDtypeStruct((length, HD), f32),
             jax.ShapeDtypeStruct((length, HD), f32),
         ],
         compiler_params=params(),
         cost_estimate=LITTLE,
         name="attend_backward",
-    )(info, queries, keys, values, out_f, logs, grads)
+    )(info, queries, keys, values, out_f, logs, grads, cosine, sine)
 
 
 def cube_body(
@@ -1410,12 +1451,13 @@
     cotangent,
 ):
     core = lax.axis_index("head")
-    chip = lax.axis_index("seq")
-    member = chip % 8
+    seq_half = lax.axis_index("half")
+    member = lax.axis_index("cube")
+    chip = seq_half * 8 + member
     bits = (member // 4, (member // 2) % 2, member % 2)
     zl = bits[0]
     place = core * 8 + member
-    info = jnp.stack([place, core, member]).astype(jnp.int32)
+    info = jnp.stack([place, core, member, seq_half]).astype(jnp.int32)
     width = tokens.shape[-1]
     rows = tokens.shape[1]
     shard = width // DEVICES
@@ -1427,7 +1469,24 @@
     half_rows = rows * 8
     ffc = FF // 16
 
-    x_bf = swap_sequences(tokens[0])
+    def to_local(value):
+        parts = [value[:, i * width // 4 : (i + 1) * width // 4] for i in range(4)]
+        return jnp.where(
+            seq_half == 0,
+            jnp.concatenate([parts[i] for i in (0, 2, 1, 3)], axis=1),
+            jnp.concatenate([parts[i] for i in (1, 3, 0, 2)], axis=1),
+        )
+
+    def to_natural(value):
+        parts = [value[:, i * width // 4 : (i + 1) * width // 4] for i in range(4)]
+        return jnp.where(
+            seq_half == 0,
+            jnp.concatenate([parts[i] for i in (0, 2, 1, 3)], axis=1),
+            jnp.concatenate([parts[i] for i in (2, 0, 3, 1)], axis=1),
+        )
+
+    swapped = swap_sequences(jnp.concatenate([tokens[0], cotangent[0]], axis=0))
+    x_bf, g_out_bf = to_local(swapped[:rows]), to_local(swapped[rows:])
 
     gain_rows = norm_gain.astype(f32)[:, None]
     qkv_s = (qkv_proj.astype(f32) * gain_rows).astype(bf16)
@@ -1441,11 +1500,8 @@
         parts = jnp.moveaxis(value.reshape(shard, 8, -1), 1, 0)
         return jnp.concatenate([parts, parts], axis=0)
 
-    def for_devices(value):
-        split = value.reshape((2, 1, 8) + value.shape[1:])
-        return jnp.broadcast_to(split, (2, 2, 8) + value.shape[1:]).reshape(
-            (DEVICES,) + value.shape[1:]
-        )
+    def both_halves(value, other):
+        return jnp.concatenate([value, other], axis=0)
 
     kv_width = KVH * HD
     conv_shard = conv_weight.shape[1]
@@ -1456,7 +1512,6 @@
     decay_rows = jnp.concatenate([decay_high, decay_low], axis=1)
     extra_size = shard * 128
     extra_pad = jnp.zeros((extra_size - smalls.shape[0] - decay_rows.shape[1],), bf16)
-    seq_half = chip // 8
 
     def shared_for(half):
         mine_rows = lax.dynamic_index_in_dim(decay_rows, half, 0, keepdims=False)
@@ -1474,7 +1529,7 @@
         axis=1,
     )
     shared_other = flip(shared_for(1 - seq_half), BIT_ZH)
-    send_in = jnp.concatenate(
+    send_own = jnp.concatenate(
         [
             to_places(inner_s[:, :inner_width]),
             to_places(inner_s[:, inner_width : 2 * inner_width]),
@@ -1482,16 +1537,11 @@
         ],
         axis=2,
     )
-    send_in, x_bf, shared_other = joint(for_devices(send_in), x_bf, shared_other)
-    w_own = exchange(send_in).reshape(width, 2 * mine + HD)
+    got_own = exchange(send_own).reshape(width // 2, -1)
     x_rows = x_bf.astype(f32)
     inv_in = lax.rsqrt(jnp.mean(x_rows * x_rows, axis=-1, keepdims=True) + EPSILON)
     shared_mine = shared_for(seq_half)
-    shared_both = jnp.where(
-        seq_half == 0,
-        jnp.concatenate([shared_mine, shared_other], axis=0),
-        jnp.concatenate([shared_other, shared_mine], axis=0),
-    )
+    shared_both = jnp.concatenate([shared_mine, shared_other], axis=0)
     normed_mine = (x_rows * inv_in).astype(bf16)
     shared_edges = ((0, 2 * NS), (2 * NS, 2 * NS + kv_width + 128), (2 * NS + kv_width + 128, None))
     lanes_all = (shared_both.shape[1] + width) // 128
@@ -1505,7 +1555,36 @@
         normed_edges.append((part.shape[1], done, taken))
         at += lanes_here * 128
         done += taken
-    pieces = Gather(jnp.concatenate(joined, axis=1), edges).pieces()
+    first = Gather(jnp.concatenate(joined, axis=1), edges, info)
+    first.state, got_own = joint(first.state, got_own)
+    own_width = 2 * mine + HD
+    other_own = [flip(got_own[:, : own_width // 2], BIT_ZH), None]
+    first.hop()
+    send_rest = jnp.concatenate(
+        [
+            to_places(inner_out.T),
+            to_members(attn_proj.T),
+            to_places(gate_up_s[:, :FF]),
+            to_places(gate_up_s[:, FF:]),
+            to_places(down_proj.T),
+        ],
+        axis=2,
+    )
+    positions = jnp.arange(length, dtype=f32)
+    frequency = ROPE_BASE ** (-2.0 * jnp.arange(HD // 2, dtype=f32) / HD)
+    angle = positions[:, None] * frequency[None, :]
+    cosine, sine = jnp.cos(angle), jnp.sin(angle)
+    cosine = jnp.concatenate([cosine, cosine], axis=1)
+    sine = jnp.concatenate([-sine, sine], axis=1)
+    first.hop()
+    first.state, other_own[0], got_own = joint(first.state, other_own[0], got_own)
+    other_own[1] = flip(got_own[:, own_width // 2 :], BIT_ZH)
+    first.hop()
+    first.state, send_rest, other_own[1], cosine, sine = joint(
+        first.state, send_rest, other_own[1], cosine, sine
+    )
+    got = exchange(send_rest).reshape(width // 2, -1)
+    pieces = first.pieces()
     shared_width = 2 * NS + 2 * HD + 128
     picks = (
         ((0, 0, 0, 2 * NS),),
@@ -1519,23 +1598,28 @@
             number = 3 * group + part if half == 0 else 6 + far
             start = edges[part][0] * half
             skip, normed_at, taken = normed_edges[part]
-            for first, cube_place, count in piece_blocks(part, far):
+            for begin, cube_place, count in piece_blocks(part, far):
                 normed_moves.append(
                     (
                         number,
-                        fixed(first * rows, count * rows, start + skip, taken),
+                        fixed(begin * rows, count * rows, start + skip, taken),
                         fixed((half * 8 + cube_place) * rows, count * rows, normed_at, taken),
                     )
                 )
                 for block, zh in ((i, j) for i in range(count) for j in range(2)):
-                    row = (first + block) * 2 * shard + zh * shard
+                    row = (begin + block) * 2 * shard + zh * shard
                     position = half * 8 + cube_place + block
 
                     def goal(ref, position=position, zh=zh, target=0, columns=128):
-                        place = ref[0] ^ position
-                        to = (place // 8) * 16 + zh * 8 + place % 8
+                        to = zh * 16 + (ref[0] ^ position)
                         to = pl.multiple_of(to * shard, shard)
                         return (pl.ds(to, shard), pl.ds(target, columns))
+
+                    def extra_goal(ref, position=position, zh=zh):
+                        place = ref[0] ^ position
+                        to = (place // 8) * 16 + (zh ^ ref[3]) * 8 + place % 8
+                        to = pl.multiple_of(to * shard, shard)
+                        return (pl.ds(to, shard), pl.ds(0, 128))
 
                     for column, by_zl, target, columns in picks[part]:
 
@@ -1553,11 +1637,18 @@
                         )
                     if part == 2:
                         extra_moves.append(
-                            (number, fixed(row, shard, start + kv_width, 128), goal)
+                            (number, fixed(row, shard, start + kv_width, 128), extra_goal)
                         )
-    normed = assemble(pieces, normed_moves, (length, width), info)
-    w_s = assemble(pieces, moves, (width, shared_width), info)
-    small_got = assemble(pieces, extra_moves, (width, 128), info).reshape(DEVICES, -1)
+    normed, w_s, small_got = assemble(
+        pieces,
+        [
+            ((length, width), bf16, normed_moves),
+            ((width, shared_width), bf16, moves),
+            ((width, 128), bf16, extra_moves),
+        ],
+        info,
+    )
+    small_got = small_got.reshape(DEVICES, -1)
     at = smalls.shape[0]
     decay = lax.dynamic_slice_in_dim(small_got[:, at : at + decay_rows.shape[1]], core * 16, 16, 0)
     decay = decay.astype(f32).reshape(16, 2, 8, heads, rows)
@@ -1576,17 +1667,7 @@
     taps_m = conv_all[:, inner_width:]
     gain_mine = lax.dynamic_slice_in_dim(gain_all, place * mine, mine, 1)[0].astype(f32)
 
-    send_mix = jnp.concatenate(
-        [to_places(inner_out.T), to_members(attn_proj.T)], axis=2
-    )
-    send_mix, w_own = joint(for_devices(send_mix), w_own)
-    w_mix = exchange(send_mix).reshape(width, mine + HD)
-    send_gu = jnp.concatenate([to_places(gate_up_s[:, :FF]), to_places(gate_up_s[:, FF:])], axis=2)
-    send_down, w_mix = joint(for_devices(to_places(down_proj.T)), w_mix)
-    w_down = exchange(send_down).reshape(width, ffc)
-    send_gu, w_down = joint(for_devices(send_gu), w_down)
-    w_gu = exchange(send_gu).reshape(width, 2 * ffc)
-
+    (w_own,) = joint(both_halves(got_own, jnp.concatenate(other_own, axis=1)))
     bias_mine = lax.dynamic_slice_in_dim(step_bias, member * heads, heads, 0)
     skip_mine = lax.dynamic_slice_in_dim(skip_gain, member * heads, heads, 0)
     vec = jnp.concatenate(
@@ -1604,53 +1685,58 @@
     cum_row = jnp.cumsum(decay, axis=2)
     cum_row = jnp.concatenate([cum_row, jnp.zeros((16, 8 - heads, rows), f32)], axis=1)
     cum_col = jnp.moveaxis(cum_row, 1, 2).reshape(length, 8)
-    w_all = jnp.concatenate([w_own, w_s], axis=1)
+    (w_all,) = joint(jnp.concatenate([w_own, w_s], axis=1))
 
     order = jnp.arange(16, dtype=jnp.int32) ^ place
 
     def reordered(value):
         return jnp.take(value, order, axis=0, unique_indices=True, mode="clip")
 
-    cotangent_mine, normed = joint(cotangent[0], normed)
-    g_out_bf = swap_sequences(cotangent_mine)
+    g_out_bf, normed = joint(g_out_bf, normed)
+    g_out = gather_start(g_out_bf, info)
+    g_out.hop()
     raw_s = mm(normed, w_s)
-    g_out_bf, raw_s = joint(g_out_bf, raw_s)
-    g_out = gather_start(g_out_bf)
+    g_out.state, raw_s, got, normed = joint(g_out.state, raw_s, got, normed)
+    cuts = [0, mine + HD] + [mine + HD + i * ffc for i in (1, 2, 3)]
+    got = [got[:, a:b] for a, b in zip(cuts[:-1], cuts[1:])]
+    other = [flip(got[0], BIT_ZH), None, None, None]
     g_out.hop()
     raw_own = mm(normed, w_own)
-    raw_own, w_mix = joint(raw_own, w_mix)
-    w_out, w_att = w_mix[:, :mine], w_mix[:, mine:]
-
-    positions = jnp.arange(length, dtype=f32)
-    frequency = ROPE_BASE ** (-2.0 * jnp.arange(HD // 2, dtype=f32) / HD)
-    angle = positions[:, None] * frequency[None, :]
-    cosine, sine = jnp.cos(angle), jnp.sin(angle)
-    cosine = jnp.concatenate([cosine, cosine], axis=1)
-    sine = jnp.concatenate([-sine, sine], axis=1)
+    g_out.state, raw_own = joint(g_out.state, raw_own)
+    g_out.hop()
 
     tables = (cosine, sine, cum_col, cum_row, taps_x, taps_m, vec)
     y, gained, squares, states, queries, keys, values = run_mix_forward(
         info, raw_own, raw_s, *tables
     )
-    g_out.state, queries = joint(g_out.state, queries)
-    g_out.hop()
+    squares, other[0] = joint(squares, other[0])
+    other[3] = flip(got[3], BIT_ZH)
+    (w_mix,) = joint(both_halves(got[0], other[0]))
+    w_out, w_att = w_mix[:, :mine], w_mix[:, mine:]
     squares = group_sum(squares[:, 0])
+    squares, queries, other[3], got[1] = joint(squares, queries, other[3], got[1])
+    other[1] = flip(got[1], BIT_ZH)
+    (w_down,) = joint(both_halves(got[3], other[3]))
+    attended, attended_f, logs = run_attend_forward(info, queries, keys, values)
     inv_mix = lax.rsqrt(squares / inner_width + EPSILON)
     inv_mix_rows = reordered(inv_mix).reshape(length, 1)
-    keys, w_down = joint(keys, w_down)
-    attended, attended_f, logs = run_attend_forward(info, queries, keys, values)
-    g_out.state, attended = joint(g_out.state, attended)
-    g_out.hop()
     part_other = inv_mix_rows[half_rows:] * mm_nt(gained[half_rows:], w_out)
     part_own = inv_mix_rows[:half_rows] * mm_nt(gained[:half_rows], w_out) + mm_nt(attended, w_att)
     sums = Scatter(part_own.astype(bf16), part_other)
+    sums.state, other[1], got[2] = joint(sums.state, other[1], got[2])
+    other[2] = flip(got[2], BIT_ZH)
     sums.hop()
-    sums.state, w_gu = joint(sums.state, w_gu)
+    sums.hop()
+    sums.state, other[2] = joint(sums.state, other[2])
+    (w_gu,) = joint(
+        jnp.concatenate([both_halves(got[i], other[i]) for i in (1, 2)], axis=1)
+    )
     hidden = x_rows + sums.result()
     g_out = gathered(g_out, width, info)
 
     inv_ff = lax.rsqrt(jnp.mean(hidden * hidden, axis=-1, keepdims=True) + EPSILON)
-    normed_ff = gathered(gather_start((hidden * inv_ff).astype(bf16)), width, info)
+    gather = gather_start((hidden * inv_ff).astype(bf16), info)
+    normed_ff = gathered(gather, width, info)
     gate_vals = mm(normed_ff, w_gu)
     gate, up = gate_vals[:, :ffc], gate_vals[:, ffc:]
     sig = jax.nn.sigmoid(gate)
@@ -1661,25 +1747,32 @@
     ).astype(bf16)
     g_ff_other = mm_nt(g_vals[half_rows:], w_gu).astype(bf16)
     sums = Scatter(mm_nt(g_vals[:half_rows], w_gu).astype(bf16), g_ff_other)
-    g_ff_own, g_ff_got = sums.state
-    g_ff_own, mixed_late, g_vals_late = joint(g_ff_own, mixed, g_vals)
-    sums.state = (g_ff_own, g_ff_got)
-    out_other = mm_nt(mixed_late[half_rows:], w_down).astype(bf16)
-    out_own = mm_nt(mixed_late[:half_rows], w_down).astype(bf16)
+    sums.hop()
+    def crossing(value):
+        return flip(value[width // 2 :], BIT_ZH)
+
+    def to_owners(values, crossed):
+        total = [
+            value[: width // 2].astype(f32) + got.astype(f32)
+            for value, got in zip(values, crossed)
+        ]
+        total = jnp.concatenate([part.astype(bf16) for part in total], axis=1)
+        return exchange(total.reshape(16, shard, -1))
+
+    mixed_late, g_vals_late = sums.then(mixed, g_vals)
+    mixed_cube = reordered_rows(mixed_late, info)
+    out_other = mm_nt(mixed_cube[half_rows:], w_down).astype(bf16)
+    out_own = mm_nt(mixed_cube[:half_rows], w_down).astype(bf16)
     d_gu = mm_tn(normed_ff, g_vals_late).astype(bf16)
+    d_gate, d_up = d_gu[:, :ffc], d_gu[:, ffc:]
+    sums.state, out_other, out_own, d_gate = joint(sums.state, out_other, out_own, d_gate)
+    out_got = flip(out_other, BIT_C)
+    gate_got = crossing(d_gate)
+    sums.hop()
+    mixed_late, g_out = sums.then(mixed_late, g_out)
     d_down = mm_tn(g_out, mixed_late).astype(bf16)
-    sums.hop()
-    sums.state, out_other, out_own, d_gu, d_down = joint(
-        sums.state, out_other, out_own, d_gu, d_down
-    )
+    sums.state, d_down = joint(sums.state, d_down)
     g_ff = sums.result()
-
-    def to_owners(value):
-        return exchange(value.astype(bf16).reshape(DEVICES, shard, -1))
-
-    def owned(got):
-        got = got.astype(f32).reshape((2, 2, 8) + got.shape[1:])
-        return (got[:, 0] + got[:, 1]).reshape((16,) + got.shape[3:])
 
     def from_places(value):
         return jnp.moveaxis(value, 0, 1).reshape(shard, -1)
@@ -1689,60 +1782,98 @@
         + inv_ff * g_ff
         - hidden * inv_ff**3 * jnp.mean(hidden * g_ff, axis=-1, keepdims=True)
     )
-    g_branch = gathered(gather_start(g_hidden.astype(bf16)), width, info)
-    g_branch, d_gu, out_own, out_other = joint(g_branch, d_gu, out_own, out_other)
-    d_gu_got = to_owners(d_gu)
-
-    g_branch_own = g_branch[:half_rows]
+    gather = gather_start(g_hidden.astype(bf16), info)
+    gather.state, gate_got, d_up = joint(gather.state, gate_got, d_up)
+    up_got = crossing(d_up)
+    gather.hop()
+    gather.hop()
+    out_sum = (out_own.astype(f32) + out_got.astype(f32)).astype(bf16)
+    gather.state, up_got, d_down, out_sum, w_all = joint(
+        gather.state, up_got, d_down, out_sum, w_all
+    )
+    down_got = crossing(d_down)
+    g_branch = gathered(gather, width, info)
+
     inner_normed = (gained.astype(f32) * inv_mix_rows).astype(bf16)
     g_inner = mm(g_branch, w_out)
+    g_branch_own = g_branch[:half_rows]
     g_att = mm(g_branch_own, w_att).astype(bf16)
     dots = jnp.sum(inner_normed.astype(f32) * g_inner, axis=-1).reshape(16, rows)
     dots = group_sum(reordered(dots))
-    d_out = mm_tn(g_branch, inner_normed).astype(bf16)
-    d_att = mm_tn(g_branch_own, attended).astype(bf16)
-    out_part = Scatter(out_own, out_other).result()
-
+    g_branch_own = g_branch[:half_rows]
+    g_att = mm(g_branch_own, w_att).astype(bf16)
+    d_mix_early = jnp.concatenate(
+        [
+            mm_tn(g_branch, inner_normed).astype(bf16),
+            mm_tn(g_branch_own, attended).astype(bf16),
+        ],
+        axis=1,
+    )
+    d_mix_early, g_att = joint(d_mix_early, g_att)
+    early_got = crossing(d_mix_early)
     d_q, d_k, d_v = run_attend_backward(
-        info, queries, keys, values, attended_f, logs, g_att
-    )
-    scales = jnp.stack([inv_mix, dots / inner_width], axis=-1).reshape(length, 2)
-    scales = jnp.concatenate([scales, jnp.zeros((length, 6), f32)], axis=1)
-    scales, out_part = joint(scales, out_part)
+        info, queries, keys, values, attended_f, logs, g_att, cosine, sine
+    )
+    gate = raw_own[:, :mine]
+    gate_sig = jax.nn.sigmoid(gate)
+    y_rows = y.astype(f32)
+    normed_mix = y_rows * (gate * gate_sig) * inv_mix_rows
+    g_gated = inv_mix_rows * (
+        gain_mine * g_inner - normed_mix * (reordered(dots).reshape(length, 1) / inner_width)
+    )
+    g_y = (g_gated * gate * gate_sig).astype(bf16)
+    g_z = (g_gated * y_rows * gate_sig * (1.0 + gate * (1.0 - gate_sig))).astype(bf16)
+    grad_gain_mine = jnp.sum(normed_mix * g_inner, axis=0)
+    d_q, down_got, dots = joint(d_q, down_got, dots)
+    d_ff_got = to_owners((d_gate, d_up, d_down), (gate_got, up_got, down_got))
+    d_mix_late = jnp.concatenate(
+        [
+            mm_tn(normed, g_z).astype(bf16),
+            mm_tn(normed[:half_rows], d_q).astype(bf16),
+        ],
+        axis=1,
+    )
+    d_mix_late, early_got = joint(d_mix_late, early_got)
+    late_got = crossing(d_mix_late)
+    g_y, d_ff_got, out_sum, d_mix_late = joint(g_y, d_ff_got, out_sum, d_mix_late)
+    out_got = lax.all_to_all(
+        out_sum.reshape(8, rows, width), "cube", split_axis=0, concat_axis=0, tiled=True
+    )
     g_all, acc_x, acc_m, acc_v, acc_s = run_mix_backward(
         info,
         raw_own,
         raw_s,
         *tables,
         lanes,
-        y,
-        g_inner,
-        scales,
+        g_y,
+        g_z,
         states,
         d_q,
         d_k,
         d_v,
     )
-    output = swap_sequences((hidden + out_part).astype(bf16))[None]
     conv_grads = jnp.concatenate([acc_x[: KC + 1], acc_m[: KC + 1]], axis=1)
     g_bias = lax.dynamic_slice_in_dim(acc_s[0], place * heads, heads, 0)
-    g_skip = jnp.sum(acc_v[1].reshape(heads, MP), axis=1)
-    small_grads = jnp.concatenate([conv_grads.reshape(-1), acc_v[0], g_bias, g_skip])
+    g_skip = jnp.sum(acc_v[0].reshape(heads, MP), axis=1)
+    small_grads = jnp.concatenate([conv_grads.reshape(-1), grad_gain_mine, g_bias, g_skip])
     small_grads = jnp.pad(small_grads, (0, -small_grads.shape[0] % shard)).astype(bf16)
     small_grads = jnp.broadcast_to(
         small_grads.reshape(1, shard, -1), (DEVICES, shard, small_grads.shape[0] // shard)
     ).reshape(width, -1)
-    d_mix = jnp.concatenate([d_down, d_out, d_att, small_grads], axis=1)
-    d_mix, g_all, d_gu_got = joint(d_mix, g_all, d_gu_got)
-    d_mix_got = to_owners(d_mix)
     g_in_other = mm_nt(g_all[half_rows:], w_all).astype(bf16)
-    g_in_own = mm_nt(g_all[:half_rows], w_all).astype(bf16)
-    g_late = g_all
-    own_width = 2 * mine + HD
-    d_own = mm_tn(normed, g_late[:, :own_width]).astype(bf16)
-    d_own, d_mix_got = joint(d_own, d_mix_got)
-    d_own_got = to_owners(d_own)
-    d_shared = mm_tn(normed, g_late[:, own_width:]).astype(bf16)
+    sums = Scatter(mm_nt(g_all[:half_rows], w_all).astype(bf16), g_in_other)
+    sums.state, out_got = joint(sums.state, out_got)
+    sums.hop()
+    (g_all,) = sums.then(g_all)
+    d_own = mm_tn(normed, g_all[:, mine : 2 * mine]).astype(bf16)
+    d_own = jnp.concatenate([d_own, small_grads], axis=1)
+    d_shared = mm_tn(normed, g_all[:, own_width:]).astype(bf16)
+    sums.state, d_own, d_shared = joint(sums.state, d_own, d_shared)
+    sums.hop()
+    d_shared, d_ff_got, out_got = sums.then(d_shared, d_ff_got, out_got)
+    out_part = jnp.sum(out_got.astype(f32), axis=0)
+    out_rows = (hidden + out_part).astype(bf16)
+
     def only_mine(value):
         empty = jnp.zeros((width, KVH * HD), bf16)
         return lax.dynamic_update_slice_in_dim(empty, value, zl * HD, 1)
@@ -1760,43 +1891,53 @@
     for block in range(DEVICES):
 
         def goal(ref, block=block):
-            position = ref[0] ^ (block // 16 * 8 + block % 8)
-            row = position * 2 + block // 8 % 2
+            row = (ref[0] ^ (block % 16)) * 2 + block // 16
             return (pl.ds(pl.multiple_of(row * shard, shard), shard), slice(None))
 
         moves.append((0, fixed(block * shard, shard, 0, d_shared.shape[1]), goal))
-    d_shared = assemble([d_shared], moves, d_shared.shape, info)
-    sums = Scatter(
-        jnp.concatenate([g_in_own, d_shared[:half_rows]], axis=1),
-        jnp.concatenate([g_in_other, d_shared[half_rows:]], axis=1),
-    ).result()
-    sums, d_mix_got = joint(sums, d_mix_got)
-    g_in = sums[:, :width]
-    d_cube = sums[:, width:].reshape(2, shard, -1)
-    d_shared_own = lax.dynamic_index_in_dim(d_cube, seq_half, 0, keepdims=False) + flip(
-        lax.dynamic_index_in_dim(d_cube, 1 - seq_half, 0, keepdims=False).astype(bf16), BIT_ZH
-    ).astype(f32)
-    d_gu_own = owned(d_gu_got)
+    d_shared = assemble([d_shared], [(d_shared.shape, bf16, moves)], info)[0]
+    sums.state, d_shared = joint(sums.state, d_shared)
+    shared_sums = Scatter(d_shared[:half_rows], d_shared[half_rows:])
+    sums.hop()
+    g_in, d_own = joint(sums.result(), d_own)
+    own_back = crossing(d_own)
+    g_x_rows = (
+        inv_in * g_in - x_rows * inv_in**3 * jnp.mean(x_rows * g_in, axis=-1, keepdims=True)
+    )
+    both = jnp.concatenate(
+        [to_natural(out_rows), to_natural((g_hidden + g_x_rows).astype(bf16))], axis=0
+    )
+    both = swap_sequences(both)
+    output, grad_tokens = both[None, :rows], both[None, rows:].astype(f32)
+    shared_sums.hop()
+    shared_sums.state, own_back = joint(shared_sums.state, own_back)
+    shared_sums.hop()
+    shared_sums.hop()
+    shared_sums.state, own_back, late_got, early_got = joint(
+        shared_sums.state, own_back, late_got, early_got
+    )
+    d_own_got = to_owners((d_own, d_mix_late, d_mix_early), (own_back, late_got, early_got))
+    d_cube = shared_sums.result().reshape(2, shard, -1)
+    d_shared_own = d_cube[0] + flip(d_cube[1].astype(bf16), BIT_ZH).astype(f32)
+    d_ff_own = d_ff_got.astype(f32)
     d_gate_up = jnp.concatenate(
-        [from_places(d_gu_own[..., :ffc]), from_places(d_gu_own[..., ffc:])], axis=1
+        [from_places(d_ff_own[..., :ffc]), from_places(d_ff_own[..., ffc : 2 * ffc])], axis=1
     )
     grad_gate_up = d_gate_up * ff_gain.astype(f32)[:, None]
     grad_ff_gain = jnp.sum(d_gate_up * gate_up.astype(f32), axis=1)
-    d_mix_own = owned(d_mix_got)
-    grad_down = jnp.moveaxis(d_mix_own[..., :ffc], 1, 2).reshape(FF, shard)
-    grad_inner_out = jnp.moveaxis(d_mix_own[..., ffc : ffc + mine], 1, 2).reshape(
-        inner_width, shard
-    )
-    at = ffc + mine + HD
-    d_att = d_mix_own[..., ffc + mine : at].reshape(2, 8, shard, HD)
+    grad_down = jnp.moveaxis(d_ff_own[..., 2 * ffc : 3 * ffc], 1, 2).reshape(FF, shard)
+    d_own = d_own_got.astype(f32)
+    small_end = d_own.shape[-1] - 2 * mine - 2 * HD
+    d_mix_own = d_own[..., small_end + mine + HD :]
+    grad_inner_out = jnp.moveaxis(d_mix_own[..., :mine], 1, 2).reshape(inner_width, shard)
+    d_att = d_mix_own[..., mine:].reshape(2, 8, shard, HD)
     grad_attn = jnp.moveaxis(d_att[0] + d_att[1], 1, 2).reshape(QH * HD, shard)
-    d_own = owned(d_own_got)
-    d_z = from_places(d_own[..., :mine])
-    d_x = from_places(d_own[..., mine : 2 * mine])
-    d_qw = d_own[..., 2 * mine :].reshape(2, 8, shard, HD)
+    d_x = from_places(d_own[..., :mine])
+    d_z = from_places(d_own[..., small_end : small_end + mine])
+    d_qw = d_own[..., small_end + mine : small_end + mine + HD].reshape(2, 8, shard, HD)
     d_qw = from_places(d_qw[0] + d_qw[1])
 
-    got = d_mix_own[..., at:].reshape(16, -1)
+    got = d_own[..., mine:small_end].reshape(16, -1)
     at = 0
     taps_width = mine + 2 * NS
     conv_grads = got[:, at : at + (KC + 1) * taps_width].reshape(16, KC + 1, taps_width)
@@ -1826,10 +1967,6 @@
     grad_norm_gain = jnp.sum(d_qkv * qkv_proj.astype(f32), axis=1) + jnp.sum(
         d_inner * inner_proj.astype(f32), axis=1
     )
-    g_x_rows = (
-        inv_in * g_in - x_rows * inv_in**3 * jnp.mean(x_rows * g_in, axis=-1, keepdims=True)
-    )
-    grad_tokens = swap_sequences((g_hidden + g_x_rows).astype(bf16)).astype(f32)[None]
     return (
         output,
         grad_tokens,
@@ -1849,9 +1986,60 @@
     )
 
 
+def cube_solution(mesh):
+    cubes = jax.sharding.Mesh(mesh.devices.reshape(2, 2, 8), BOTH)
+    tokens = P("head", ("half", "cube"), None)
+    lines = P(BOTH)
+    rows = P(BOTH, None)
+    columns = P(None, BOTH)
+    head = P("head")
+    return jax.shard_map(
+        cube_body,
+        mesh=cubes,
+        in_specs=(
+            tokens,
+            P(None, ("half", "cube"), "head"),
+            lines,
+            rows,
+            columns,
+            rows,
+            columns,
+            lines,
+            head,
+            head,
+            lines,
+            columns,
+            lines,
+            rows,
+            columns,
+            tokens,
+        ),
+        out_specs=(
+            tokens,
+            tokens,
+            lines,
+            rows,
+            columns,
+            rows,
+            columns,
+            lines,
+            head,
+            head,
+            lines,
+            columns,
+            lines,
+            rows,
+            columns,
+        ),
+        check_vma=False,
+    )
+
+
 def solution(mesh):
+    if mesh.shape["seq"] == 16:
+        return cube_solution(mesh)
     return jax.shard_map(
-        cube_body if mesh.shape["seq"] == 16 else body,
+        body,
         mesh=mesh,
         in_specs=(
             P("head", "seq", None),

time: 950 us -> 875 us (0.921)
  starting transfers between devices: 189 us -> 153 us
  Pallas kernels: 89.8 us -> 120 us
  local copies, waits for them, and re-layouts: 113 us -> 86.5 us
  waiting for transfers between devices: 309 us -> 290 us
  matrix products: 139 us -> 121 us
    pallas_call x7 -> x18, Pallas kernels: 23.2 us -> 53.6 us  [assemble(): pl.pallas_call(kernel, in_specs=[pl.BlockSpec(memory_space=pltpu.SMEM)] +...]
    convert_element_type x27 -> x49, other arithmetic: 18.8 us -> 40 us  [the longest x36 18.8 us: pairs(): halves.append([(lax.slice_in_dim(part, i, i + 1, axis=axis).astype(f32) +...]
    ppermute x4 -> x2, starting transfers between devices: 18.8 us -> 3.3 us  [swap_sequences(): return jnp.where(stays, value, lax.ppermute(value, BOTH, pairs))]
    broadcast_in_dim x14 -> x0, local copies, waits for them, and re-layouts: 15.4 us -> none  [the longest x8 13.2 us: for_devices(): jnp.broadcast_to(split, (2, 2, 8) + value.shape[1:])]
    another operation x5 -> x1, other arithmetic: 15.3 us -> 0.08 us  [cube_body(): info = jnp.stack([place, core, member, seq_half]).astype(jnp.int32)]
    ppermute x98 -> x111, starting transfers between devices: 133 us -> 120 us  [flip(): return lax.ppermute(value, BOTH, [(i, i ^ mask) for i in range(DEVICES)])]
    all_to_all x7 -> x5, waiting for transfers between devices: 25.5 us -> 16.1 us  [the longest x4 16.1 us: exchange(): return lax.all_to_all(value, GROUP, split_axis=0, concat_axis=0, tiled=True)]
    ppermute x98 -> x111, waiting for transfers between devices: 283 us -> 274 us  [flip(): return lax.ppermute(value, BOTH, [(i, i ^ mask) for i in range(DEVICES)])]
  transfers between devices with their start and end apart: 109 -> 118, of which waited for: 51 -> 50; matrix products, arithmetic and copies ran while one was open for 27% -> 25% of each run, Pallas kernels for 6% -> 12%
where the time goes in v2:
time: 875 us; the launch traced here: 865 us
  waiting for transfers between devices  290 us (33%)
  starting transfers between devices  153 us (17%)
  matrix products  121 us (14%)
  Pallas kernels  120 us (14%)
  other arithmetic  90.9 us (10%)
  local copies, waits for them, and re-layouts  86.5 us (10%)
    ppermute x111, waiting for transfers between devices, flip(): return lax.ppermute(value, BOTH, [(i, i ^ mask) for i in range(DEVICES)])  274 us
    ppermute x111, starting transfers between devices, flip(): return lax.ppermute(value, BOTH, [(i, i ^ mask) for i in range(DEVICES)])  120 us
    pallas_call x18, Pallas kernels, assemble(): pl.pallas_call(kernel, in_specs=[pl.BlockSpec(memory_space=pltpu.SMEM)] +...  53.6 us
    dot_general x9, matrix products, mm_nt(): lax.dot_general(a, b, (((1,), (1,)), ((), ())), preferred_element_type=f32)  42.7 us
    dot_general x6, matrix products, mm(): return jnp.dot(a, b, preferred_element_type=f32)  42.5 us
    dot_general x8, matrix products, mm_tn(): lax.dot_general(a, b, (((0,), (0,)), ((), ())), preferred_element_type=f32)  35.4 us
    pallas_call x1, Pallas kernels, run_mix_backward(): pl.pallas_call(mix_backward, grid_spec=pltpu.PrefetchScalarGridSpec(num_s...  29.5 us
    unnamed x249, local copies, waits for them, and re-layouts  26.6 us
  transfers between devices with their start and end apart: 118, of which 50 were waited for; matrix products, arithmetic and copies ran while one was open for 25% of the time, Pallas kernels for 12%

profile of v2, /device:TPU:0, one launch (start us, length us, event | category | flops | bytes accessed | tf_op | source)
XLA Modules:
  0.0 864.5 jit_solution(6109192056977338928)
XLA Ops:
  18.4 22.0 %collective-permute-done.1 = bf16[64,1280]{1,0:T(8,128)(2,1)S(1)} collective-permute-done((bf16[64,1280]{1,0:T(8,128)(2,1)S(1)}, bf16[64,1280]{1,0:T(8,128)(2,1)S(1)}, u32[]{:S(2)}, u32[]{:S(2)}) %collective-permute-start.1) | collective-permute-done | bytes 163872 | tf_op jit(solution)/shard_map/ppermute | solution.py:648
  61.2 16.8 %collective-permute-done.8 = bf16[1024,256]{1,0:T(8,128)(2,1)S(1)} collective-permute-done((bf16[1024,256]{1,0:T(8,128)(2,1)S(1)}, bf16[1024,256]{1,0:T(8,128)(2,1)S(1)}, u32[]{:S(2)}, u32[]{:S(2)}) %collective-permute-start.8) | collective-permute-done | bytes 524320 | tf_op jit(solution)/shard_map/ppermute | solution.py:648
  112.8 6.6 collective-permute-done.12
  131.6 8.1 all-to-all-start.1
  139.7 10.3 %assemble.21 = (bf16[2048,2048]{1,0:T(8,128)(2,1)}, bf16[2048,896]{1,0:T(8,128)(2,1)S(1)}, bf16[2048,128]{1,0:T(8,128)(2,1)S(1)}) custom-call(s32[4]{0:T(128)S(1)} %pad_add_fusion.info_ref.info, bf16[512,1152]{1,0:T(8,128)(2,1)} %get-tuple-element.235.refs_0_, bf16[512,1152]{1,0:T(8,128)(2,1)} %get-tuple-element.236.refs_1_, ...), custom_call_target="tpu_custom_call" | custom-call | flops 1000 | bytes 1000 | tf_op jit(solution)/shard_map/assemble/pallas_call | solution.py:694
  164.1 14.2 %fusion.96.s_ref.s_tail_ref = f32[2048,896]{1,0:T(8,128)} fusion(bf16[2048,2048]{1,0:T(8,128)(2,1)} %get-tuple-element.256, bf16[2048,896]{1,0:T(8,128)(2,1)} %copy-done.10), kind=kOutput, calls=%fused_computation.333 | convolution fusion | flops 7516192768 | bytes 19398656 | tf_op jit(solution)/shard_map/dot_general | solution.py:865
  190.3 7.5 fusion.97.own_ref.own_tail_ref
  197.9 18.5 %mix_forward.1 = (bf16[2048,192]{1,0:T(8,128)(2,1)S(1)}, bf16[2048,192]{1,0:T(8,128)(2,1)S(1)}, f32[16,8,128]{2,1,0:T(8,128)S(1)}, bf16[16,256,192]{2,1,0:T(8,12...) custom-call(s32[4]{0:T(128)S(1)} %pad_add_fusion.info_ref.info, ...), custom_call_target="tpu_custom_call" | custom-call | flops 1000 | bytes 1000 | tf_op jit(solution)/shard_map/mix_forward/pallas_call | solution.py:1207
  241.8 13.0 %collective-permute-done.28 = bf16[1024,256]{1,0:T(8,128)(2,1)} collective-permute-done((bf16[1024,256]{1,0:T(8,128)(2,1)}, bf16[1024,256]{1,0:T(8,128)(2,1)}, u32[]{:S(2)}, u32[]{:S(2)}) %collective-permute-start.28) | collective-permute-done | bytes 524320 | tf_op jit(solution)/shard_map/ppermute | solution.py:648
  260.4 8.9 %attend_forward.1 = (bf16[1024,128]{1,0:T(8,128)(2,1)S(1)}, f32[1024,128]{1,0:T(8,128)S(1)}, f32[8,8,128]{2,1,0:T(8,128)S(1)}) custom-call(s32[4]{0:T(128)S(1)} %pad_add_fusion.info_ref.info, bf16[2048,128]{1,0:T(8,128)(2,1)S(1)} %copy-done.15, bf16[2048,128]{1,0:T(8,128)(2,1)S(1)} %copy-done.18, bf16[2048,128]{1,0:T(8,128)(2,1)S(1)} %copy-done.21), custom_call_target="tpu_custom_call" | custom-call | flops 1000 | bytes 1000 | tf_op jit(solution)/shard_map/attend_forward/pallas_call | solution.py:1376
  272.2 14.1 %collective-permute-done.30 = bf16[1024,256]{1,0:T(8,128)(2,1)S(1)} collective-permute-done((bf16[1024,256]{1,0:T(8,128)(2,1)S(1)}, bf16[1024,256]{1,0:T(8,128)(2,1)S(1)}, u32[]{:S(2)}, u32[]{:S(2)}) %collective-permute-start.30) | collective-permute-done | bytes 524320 | tf_op jit(solution)/shard_map/ppermute | solution.py:648
  297.7 7.5 collective-permute-done.33
  305.4 18.4 %collective-permute-done.31 = bf16[1,2,2,128,768]{4,3,2,1,0:T(8,128)(2,1)S(1)} collective-permute-done((bf16[1,2,2,128,768]{4,3,2,1,0:T(8,128)(2,1)S(1)}, bf16[1,2,2,128,768]{4,3,2,1,0:T(8,128)(2,1)S(1)}, u32[]{:S(2)}, u32[]{:S(2)}) %collective-permute-start.31) | collective-permute-done | bytes 786464 | tf_op jit(solution)/shard_map/ppermute | solution.py:648
  356.9 7.3 collective-permute-done.50.refs_4_
  372.5 8.9 %collective-permute-done.43.refs_2_.refs_5_ = bf16[512,640]{1,0:T(8,128)(2,1)S(1)} collective-permute-done((bf16[512,640]{1,0:T(8,128)(2,1)S(1)}, bf16[512,640]{1,0:T(8,128)(2,1)S(1)}, u32[]{:S(2)}, u32[]{:S(2)}) %collective-permute-start.43) | collective-permute-done | bytes 655392 | tf_op jit(solution)/shard_map/ppermute | solution.py:648
  426.3 6.4 convolution_convert_fusion.6
  443.9 9.4 %collective-permute-done.60 = bf16[2,2,1,128,640]{4,3,2,1,0:T(8,128)(2,1)S(1)} collective-permute-done((bf16[2,2,1,128,640]{4,3,2,1,0:T(8,128)(2,1)S(1)}, bf16[2,2,1,128,640]{4,3,2,1,0:T(8,128)(2,1)S(1)}, u32[]{:S(2)}, u32[]{:S(2)}) %collective-permute-start.60) | collective-permute-done | bytes 655392 | tf_op jit(solution)/shard_map/ppermute | solution.py:648
  466.2 6.6 collective-permute-done.63
  475.2 6.6 collective-permute-done.65
  510.8 6.4 collective-permute-done.74
  521.1 14.8 %collective-permute-done.77.refs_1_.refs_4_ = bf16[512,640]{1,0:T(8,128)(2,1)S(1)} collective-permute-done((bf16[512,640]{1,0:T(8,128)(2,1)S(1)}, bf16[512,640]{1,0:T(8,128)(2,1)S(1)}, u32[]{:S(2)}, u32[]{:S(2)}) %collective-permute-start.77) | collective-permute-done | bytes 655392 | tf_op jit(solution)/shard_map/ppermute | solution.py:648
  565.0 9.4 %attend_backward.1 = (bf16[1024,128]{1,0:T(8,128)(2,1)S(1)}, f32[2048,128]{1,0:T(8,128)S(1)}, f32[2048,128]{1,0:T(8,128)S(1)}) custom-call(s32[4]{0:T(128)S(1)} %pad_add_fusion.info_ref.info, bf16[2048,128]{1,0:T(8,128)(2,1)S(1)} %copy-done.16, bf16[2048,128]{1,0:T(8,128)(2,1)S(1)} %copy-done.19, bf16[2048,128]{1,0:T(8,128)(2,1)S(1)} %copy-done.22, ...), custom_call_target="tpu_custom_call" | custom-call | flops 1000 | bytes 1000 | tf_op jit(solution)/shard_map/attend_backward/pallas_call | solution.py:1403
  599.0 16.4 %collective-permute-done.88 = bf16[1024,320]{0,1:T(8,128)(2,1)} collective-permute-done((bf16[1024,320]{0,1:T(8,128)(2,1)}, bf16[1024,320]{0,1:T(8,128)(2,1)}, u32[]{:S(2)}, u32[]{:S(2)}) %collective-permute-start.88) | collective-permute-done | bytes 655392 | tf_op jit(solution)/shard_map/ppermute | solution.py:648
  632.7 29.5 %mix_backward.1 = (bf16[2048,1408]{1,0:T(8,128)(2,1)}, f32[8,192]{1,0:T(8,128)S(1)}, f32[8,512]{1,0:T(8,128)S(1)}, f32[8,192]{1,0:T(8,128)S(1)}, f32[8,128]{1,0:T(8,128)S(1)}) custom-call(s32[4]{0:T(128)S(1)} %pad_add_fusion.info_ref.info, f32[2048,512]{1,0:T(8,128)S(1)} %copy-done.4, f32[2048,896]{1,0:T(8,128)} %fusion.96.s_ref.s_tail_ref, ...), custom_call_target="tpu_custom_call" | custom-call | flops 1000 | bytes 1000 | tf_op jit(solution)/shard_map/mix_backward/pallas_call | solution.py:1293
  662.2 11.1 %convolution_convert_fusion = bf16[1024,2048]{1,0:T(8,128)(2,1)} fusion(bf16[2048,1408]{1,0:T(8,128)(2,1)} %pad_maximum_fusion, bf16[2048,1408]{1,0:T(8,128)(2,1)} %get-tuple-element.373), kind=kOutput, calls=%fused_computation.11 | convolution fusion | flops 5907677184 | bytes 12845056 | tf_op jit(solution)/shard_map/dot_general | solution.py:869
  677.1 11.0 %convolution_convert_fusion.1 = bf16[1024,2048]{1,0:T(8,128)(2,1)} fusion(bf16[2048,1408]{1,0:T(8,128)(2,1)} %pad_maximum_fusion, bf16[2048,1408]{1,0:T(8,128)(2,1)} %get-tuple-element.373), kind=kOutput, calls=%fused_computation.12 | convolution fusion | flops 5907677184 | bytes 12845056 | tf_op jit(solution)/shard_map/dot_general | solution.py:869
  694.6 12.8 %fusion.8 = bf16[2048,896]{1,0:T(8,128)(2,1)S(1)} fusion(bf16[2048,2048]{1,0:T(8,128)(2,1)} %get-tuple-element.256, bf16[2048,1408]{1,0:T(8,128)(2,1)} %get-tuple-element.373), kind=kOutput, calls=%fused_computation.23 | convolution fusion | flops 7518027776 | bytes 15728640 | tf_op jit(solution)/shard_map/dot_general | solution.py:873
  716.0 8.7 %collective-permute-done.92 = bf16[2,2,1,128,640]{4,3,2,1,0:T(8,128)(2,1)S(1)} collective-permute-done((bf16[2,2,1,128,640]{4,3,2,1,0:T(8,128)(2,1)S(1)}, bf16[2,2,1,128,640]{4,3,2,1,0:T(8,128)(2,1)S(1)}, u32[]{:S(2)}, u32[]{:S(2)}) %collective-permute-start.92) | collective-permute-done | bytes 655392 | tf_op jit(solution)/shard_map/ppermute | solution.py:648
  737.7 8.5 assemble.35
  767.1 17.8 %collective-permute-done.104 = bf16[1024,251]{0,1:T(8,128)(2,1)S(1)} collective-permute-done((bf16[1024,251]{0,1:T(8,128)(2,1)S(1)}, bf16[1024,251]{0,1:T(8,128)(2,1)S(1)}, u32[]{:S(2)}, u32[]{:S(2)}) %collective-permute-start.104) | collective-permute-done | bytes 514080 | tf_op jit(solution)/shard_map/ppermute | solution.py:648
  815.3 11.4 %collective-permute-start.112 = (bf16[64,1152]{1,0:T(8,128)(2,1)S(1)}, bf16[64,1152]{1,0:T(8,128)(2,1)S(1)}, u32[]{:S(2)}, u32[]{:S(2)}) collective-permute-start(bf16[64,1152]{1,0:T(8,128)(2,1)S(1)} %slice.1611), channel_id=1, source_target_pairs={{0,8},{1,9},{2,10},{3,11},{4,12},{5,13},{6,14},{7,15},{8,0},{9,1},... | collective-permute-start | bytes 442376 | tf_op jit(solution)/shard_map/ppermute | solution.py:648
  835.0 11.6 %all-to-all-done.4 = bf16[16,64,891]{2,1,0:T(8,128)(2,1)S(1)} async-done(((bf16[16,64,891]{2,1,0:T(8,128)(2,1)}), bf16[16,64,891]{2,1,0:T(8,128)(2,1)S(1)}, u32[]{:S(2)}, u32[]{:S(2)}) %all-to-all-start.4) | async-done | bytes 1824800 | tf_op jit(solution)/shard_map/all_to_all | solution.py:861
  (770 shorter events, 480.1 us)
Async XLA Ops:
  3.1 37.3 %collective-permute-start = (bf16[256,2048]{1,0:T(8,128)(2,1)}, bf16[256,2048]{1,0:T(8,128)(2,1)}, u32[]{:S(2)}, u32[]{:S(2)}) collective-permute-start(bf16[256,2048]{1,0:T(8,128)(2,1)} %pad_maximum_fusion.9), channel_id=1, source_target_pairs={{8,16},{9,17},{10,18},{11,19},{12,20},{13,21},{14,22},{15,23},{16,... | collective-permute-start | bytes 3145736 | tf_op jit(solution)/shard_map/ppermute | solution.py:658
  5.7 34.7 %collective-permute-start.1 = (bf16[64,1280]{1,0:T(8,128)(2,1)S(1)}, bf16[64,1280]{1,0:T(8,128)(2,1)S(1)}, u32[]{:S(2)}, u32[]{:S(2)}) collective-permute-start(bf16[64,1280]{1,0:T(8,128)(2,1)S(1)} %concatenate.183), channel_id=1, source_target_pairs={{0,8},{1,9},{2,10},{3,11},{4,12},{5,13},{6,14},{7,15},{8,0},{9,1},... | collective-permute-start | bytes 491528 | tf_op jit(solution)/shard_map/ppermute | solution.py:648
  13.2 33.4 %all-to-all-start = ((bf16[16,64,512]{2,1,0:T(8,128)(2,1)}), bf16[16,64,512]{2,1,0:T(8,128)(2,1)S(1)}, u32[]{:S(2)}, u32[]{:S(2)}) async-start(bf16[16,64,512]{2,1,0:T(8,128)(2,1)} %maximum_maximum_fusion.2), calls=%async_computation | async-start | bytes 2097152 | tf_op jit(solution)/shard_map/all_to_all | solution.py:861
  51.7 26.3 %collective-permute-start.8 = (bf16[1024,256]{1,0:T(8,128)(2,1)S(1)}, bf16[1024,256]{1,0:T(8,128)(2,1)S(1)}, u32[]{:S(2)}, u32[]{:S(2)}) collective-permute-start(bf16[1024,256]{1,0:T(8,128)(2,1)S(1)} %slice.936), channel_id=1, source_target_pairs={{0,8},{1,9},{2,10},{3,11},{4,12},{5,13},{6,14},{7,15},{8,0},{9,1},... | collective-permute-start | bytes 1572872 | tf_op jit(solution)/shard_map/ppermute | solution.py:648
  57.9 23.1 %collective-permute-start.5 = (bf16[256,1152]{1,0:T(8,128)(2,1)S(1)}, bf16[256,1152]{1,0:T(8,128)(2,1)S(1)}, u32[]{:S(2)}, u32[]{:S(2)}) collective-permute-start(bf16[256,1152]{1,0:T(8,128)(2,1)S(1)} %get-tuple-element.225.refs_0_), channel_id=1, source_target_pairs={{0,2},{1,3},{2,0},{3,1},{4,6},{5,7},{6,4},{7,5},{8,10},{9,11},{10,... | collective-permute-start | bytes 1769480 | tf_op jit(solution)/shard_map/ppermute | solution.py:648
  85.4 36.0 %collective-permute-start.10 = (bf16[512,1152]{1,0:T(8,128)(2,1)}, bf16[512,1152]{1,0:T(8,128)(2,1)S(1)}, u32[]{:S(2)}, u32[]{:S(2)}) collective-permute-start(bf16[512,1152]{1,0:T(8,128)(2,1)} %get-tuple-element.236.refs_1_), channel_id=1, source_target_pairs={{0,4},{1,5},{2,6},{3,7},{4,0},{5,1},{6,2},{7,3},{8,12},{9,13},{10,... | collective-permute-start | bytes 3538952 | tf_op jit(solution)/shard_map/ppermute | solution.py:648
  85.4 35.9 %collective-permute-start.9 = (bf16[512,1152]{1,0:T(8,128)(2,1)}, bf16[512,1152]{1,0:T(8,128)(2,1)}, u32[]{:S(2)}, u32[]{:S(2)}) collective-permute-start(bf16[512,1152]{1,0:T(8,128)(2,1)} %get-tuple-element.235.refs_0_), channel_id=1, source_target_pairs={{0,1},{1,0},{2,3},{3,2},{4,5},{5,4},{6,7},{7,6},{8,9},{9,8},{10,11... | collective-permute-start | bytes 3538952 | tf_op jit(solution)/shard_map/ppermute | solution.py:648
  86.2 33.2 %collective-permute-start.11 = (bf16[512,1024]{1,0:T(8,128)(2,1)}, bf16[512,1024]{1,0:T(8,128)(2,1)}, u32[]{:S(2)}, u32[]{:S(2)}) collective-permute-start(bf16[512,1024]{1,0:T(8,128)(2,1)} %get-tuple-element.237.refs_2_), channel_id=1, source_target_pairs={{0,2},{1,3},{2,0},{3,1},{4,6},{5,7},{6,4},{7,5},{8,10},{9,11},{10,... | collective-permute-start | bytes 3145736 | tf_op jit(solution)/shard_map/ppermute | solution.py:648
  92.9 26.5 %collective-permute-start.12 = (bf16[1024,256]{1,0:T(8,128)(2,1)}, bf16[1024,256]{1,0:T(8,128)(2,1)}, u32[]{:S(2)}, u32[]{:S(2)}) collective-permute-start(bf16[1024,256]{1,0:T(8,128)(2,1)} %slice.939), channel_id=1, source_target_pairs={{0,8},{1,9},{2,10},{3,11},{4,12},{5,13},{6,14},{7,15},{8,0},{9,1},... | collective-permute-start | bytes 1572872 | tf_op jit(solution)/shard_map/ppermute | solution.py:648
  112.7 27.0 %collective-permute-start.13 = (bf16[512,3328]{1,0:T(8,128)(2,1)}, bf16[512,3328]{1,0:T(8,128)(2,1)}, u32[]{:S(2)}, u32[]{:S(2)}) collective-permute-start(bf16[512,3328]{1,0:T(8,128)(2,1)} %get-tuple-element.241), channel_id=1, source_target_pairs={{0,16},{1,17},{2,18},{3,19},{4,20},{5,21},{6,22},{7,23},{8,24},{9,... | collective-permute-start | bytes 10223624 | tf_op jit(solution)/shard_map/ppermute | solution.py:648
  131.6 48.4 %all-to-all-start.1 = ((bf16[16,64,1088]{2,1,0:T(8,128)(2,1)}), bf16[16,64,1088]{2,1,0:T(8,128)(2,1)}, u32[]{:S(2)}, u32[]{:S(2)}) async-start(bf16[16,64,1088]{2,1,0:T(8,128)(2,1)} %concatenate.191), calls=%async_computation.1 | async-start | bytes 4718592 | tf_op jit(solution)/shard_map/all_to_all | solution.py:861
  155.8 24.3 %collective-permute-start.16 = (bf16[128,640]{1,0:T(8,128)(2,1)}, bf16[128,640]{1,0:T(8,128)(2,1)}, u32[]{:S(2)}, u32[]{:S(2)}) collective-permute-start(bf16[128,640]{1,0:T(8,128)(2,1)} %get-tuple-element.248.refs_1_), channel_id=1, source_target_pairs={{0,2},{1,3},{2,0},{3,1},{4,6},{5,7},{6,4},{7,5},{8,10},{9,11},{10,... | collective-permute-start | bytes 491528 | tf_op jit(solution)/shard_map/ppermute | solution.py:648
  157.8 22.2 %collective-permute-start.17 = (bf16[128,640]{1,0:T(8,128)(2,1)}, bf16[128,640]{1,0:T(8,128)(2,1)}, u32[]{:S(2)}, u32[]{:S(2)}) collective-permute-start(bf16[128,640]{1,0:T(8,128)(2,1)} %get-tuple-element.249.refs_2_), channel_id=1, source_target_pairs={{0,1},{1,0},{2,3},{3,2},{4,5},{5,4},{6,7},{7,6},{8,9},{9,8},{10,11... | collective-permute-start | bytes 491528 | tf_op jit(solution)/shard_map/ppermute | solution.py:648
  188.7 33.3 %collective-permute-start.21 = (bf16[1024,320]{0,1:T(8,128)(2,1)}, bf16[1024,320]{0,1:T(8,128)(2,1)S(1)}, u32[]{:S(2)}, u32[]{:S(2)}) collective-permute-start(bf16[1024,320]{0,1:T(8,128)(2,1)} %copy.115), channel_id=1, source_target_pairs={{0,8},{1,9},{2,10},{3,11},{4,12},{5,13},{6,14},{7,15},{8,0},{9,1},... | collective-permute-start | bytes 1966088 | tf_op jit(solution)/shard_map/ppermute | solution.py:648
  228.5 26.4 %collective-permute-start.28 = (bf16[1024,256]{1,0:T(8,128)(2,1)}, bf16[1024,256]{1,0:T(8,128)(2,1)}, u32[]{:S(2)}, u32[]{:S(2)}) collective-permute-start(bf16[1024,256]{1,0:T(8,128)(2,1)} %get-tuple-element.472), channel_id=1, source_target_pairs={{0,8},{1,9},{2,10},{3,11},{4,12},{5,13},{6,14},{7,15},{8,0},{9,1},... | collective-permute-start | bytes 1572872 | tf_op jit(solution)/shard_map/ppermute | solution.py:648
  260.3 26.0 %collective-permute-start.29 = (bf16[1024,2048]{1,0:T(8,128)(2,1)}, bf16[1024,2048]{1,0:T(8,128)(2,1)}, u32[]{:S(2)}, u32[]{:S(2)}) collective-permute-start(bf16[1024,2048]{1,0:T(8,128)(2,1)} %multiply_convert_fusion), channel_id=1, source_target_pairs={{0,16},{1,17},{2,18},{3,19},{4,20},{5,21},{6,22},{7,23},{8,24},{9,... | collective-permute-start | bytes 12582920 | tf_op jit(solution)/shard_map/ppermute | solution.py:648
  260.3 26.0 %collective-permute-start.30 = (bf16[1024,256]{1,0:T(8,128)(2,1)S(1)}, bf16[1024,256]{1,0:T(8,128)(2,1)S(1)}, u32[]{:S(2)}, u32[]{:S(2)}) collective-permute-start(bf16[1024,256]{1,0:T(8,128)(2,1)S(1)} %copy-done.80), channel_id=1, source_target_pairs={{0,8},{1,9},{2,10},{3,11},{4,12},{5,13},{6,14},{7,15},{8,0},{9,1},... | collective-permute-start | bytes 1572872 | tf_op jit(solution)/shard_map/ppermute | solution.py:648
  292.1 31.7 %collective-permute-start.31 = (bf16[1,2,2,128,768]{4,3,2,1,0:T(8,128)(2,1)S(1)}, bf16[1,2,2,128,768]{4,3,2,1,0:T(8,128)(2,1)S(1)}, u32[]{:S(2)}, u32[]{:S(2)}) collective-permute-start(bf16[1,2,2,128,768]{4,3,2,1,0:T(8,128)(2,1)S(1)} %get-tuple-element.446), channel_id=1, source_target_pairs={{0,4},{1,5},{2,6},{3,7},{4,0},{5,1},{6,2},{7,3},{8,12},{9,13},{10,... | collective-permute-start | bytes 2359304 | tf_op jit(solution)/shard_map/ppermute | solution.py:648
  294.0 31.6 %collective-permute-start.32 = (bf16[2,1,2,128,640]{4,3,2,1,0:T(8,128)(2,1)S(1)}, bf16[2,1,2,128,640]{4,3,2,1,0:T(8,128)(2,1)S(1)}, u32[]{:S(2)}, u32[]{:S(2)}) collective-permute-start(bf16[2,1,2,128,640]{4,3,2,1,0:T(8,128)(2,1)S(1)} %get-tuple-element.444), channel_id=1, source_target_pairs={{0,2},{1,3},{2,0},{3,1},{4,6},{5,7},{6,4},{7,5},{8,10},{9,11},{10,... | collective-permute-start | bytes 1966088 | tf_op jit(solution)/shard_map/ppermute | solution.py:648
  295.5 30.9 %collective-permute-start.37 = (bf16[1024,256]{1,0:T(8,128)(2,1)S(1)}, bf16[1024,256]{1,0:T(8,128)(2,1)S(1)}, u32[]{:S(2)}, u32[]{:S(2)}) collective-permute-start(bf16[1024,256]{1,0:T(8,128)(2,1)S(1)} %copy-done.78), channel_id=1, source_target_pairs={{0,8},{1,9},{2,10},{3,11},{4,12},{5,13},{6,14},{7,15},{8,0},{9,1},... | collective-permute-start | bytes 1572872 | tf_op jit(solution)/shard_map/ppermute | solution.py:648
  305.4 24.3 %collective-permute-start.36 = (bf16[1,2,1,128,640]{4,3,2,1,0:T(8,128)(2,1)S(1)}, bf16[1,2,1,128,640]{4,3,2,1,0:T(8,128)(2,1)S(1)}, u32[]{:S(2)}, u32[]{:S(2)}) collective-permute-start(bf16[1,2,1,128,640]{4,3,2,1,0:T(8,128)(2,1)S(1)} %get-tuple-element.493), channel_id=1, source_target_pairs={{0,4},{1,5},{2,6},{3,7},{4,0},{5,1},{6,2},{7,3},{8,12},{9,13},{10,... | collective-permute-start | bytes 983048 | tf_op jit(solution)/shard_map/ppermute | solution.py:648
  356.9 24.5 %collective-permute-start.41 = (bf16[512,768]{1,0:T(8,128)(2,1)S(1)}, bf16[512,768]{1,0:T(8,128)(2,1)S(1)}, u32[]{:S(2)}, u32[]{:S(2)}) collective-permute-start(bf16[512,768]{1,0:T(8,128)(2,1)S(1)} %get-tuple-element.291.refs_0_), channel_id=1, source_target_pairs={{0,1},{1,0},{2,3},{3,2},{4,5},{5,4},{6,7},{7,6},{8,9},{9,8},{10,11... | collective-permute-start | bytes 2359304 | tf_op jit(solution)/shard_map/ppermute | solution.py:648
  457.6 42.4 %collective-permute-start.75 = (bf16[1024,2048]{1,0:T(8,128)(2,1)}, bf16[1024,2048]{1,0:T(8,128)(2,1)}, u32[]{:S(2)}, u32[]{:S(2)}) collective-permute-start(bf16[1024,2048]{1,0:T(8,128)(2,1)} %convolution_convert_fusion.3), channel_id=1, source_target_pairs={{0,16},{1,17},{2,18},{3,19},{4,20},{5,21},{6,22},{7,23},{8,24},{9,... | collective-permute-start | bytes 12582920 | tf_op jit(solution)/shard_map/ppermute | solution.py:648
  461.5 25.7 %collective-permute-start.67 = (bf16[1024,256]{1,0:T(8,128)(2,1)S(1)}, bf16[1024,256]{1,0:T(8,128)(2,1)S(1)}, u32[]{:S(2)}, u32[]{:S(2)}) collective-permute-start(bf16[1024,256]{1,0:T(8,128)(2,1)S(1)} %slice.1047), channel_id=1, source_target_pairs={{0,8},{1,9},{2,10},{3,11},{4,12},{5,13},{6,14},{7,15},{8,0},{9,1},... | collective-permute-start | bytes 1572872 | tf_op jit(solution)/shard_map/ppermute | solution.py:648
  493.0 24.3 %collective-permute-start.74 = (bf16[1024,256]{1,0:T(8,128)(2,1)S(1)}, bf16[1024,256]{1,0:T(8,128)(2,1)S(1)}, u32[]{:S(2)}, u32[]{:S(2)}) collective-permute-start(bf16[1024,256]{1,0:T(8,128)(2,1)S(1)} %slice.1049), channel_id=1, source_target_pairs={{0,8},{1,9},{2,10},{3,11},{4,12},{5,13},{6,14},{7,15},{8,0},{9,1},... | collective-permute-start | bytes 1572872 | tf_op jit(solution)/shard_map/ppermute | solution.py:648
  541.0 33.5 %collective-permute-start.87 = (bf16[1024,256]{1,0:T(8,128)(2,1)}, bf16[1024,256]{1,0:T(8,128)(2,1)}, u32[]{:S(2)}, u32[]{:S(2)}) collective-permute-start(bf16[1024,256]{1,0:T(8,128)(2,1)} %slice.1055), channel_id=1, source_target_pairs={{0,8},{1,9},{2,10},{3,11},{4,12},{5,13},{6,14},{7,15},{8,0},{9,1},... | collective-permute-start | bytes 1572872 | tf_op jit(solution)/shard_map/ppermute | solution.py:648
  577.4 39.3 %all-to-all-start.2 = ((bf16[16,64,768]{2,1,0:T(8,128)(2,1)}), bf16[16,64,768]{2,1,0:T(8,128)(2,1)}, u32[]{:S(2)}, u32[]{:S(2)}) async-start(bf16[16,64,768]{2,1,0:T(8,128)(2,1)} %bitcast.209), calls=%async_computation.2 | async-start | bytes 3145728 | tf_op jit(solution)/shard_map/all_to_all | solution.py:861
  584.2 31.2 %collective-permute-start.88 = (bf16[1024,320]{0,1:T(8,128)(2,1)}, bf16[1024,320]{0,1:T(8,128)(2,1)}, u32[]{:S(2)}, u32[]{:S(2)}) collective-permute-start(bf16[1024,320]{0,1:T(8,128)(2,1)} %slice.1057), channel_id=1, source_target_pairs={{0,8},{1,9},{2,10},{3,11},{4,12},{5,13},{6,14},{7,15},{8,0},{9,1},... | collective-permute-start | bytes 1966088 | tf_op jit(solution)/shard_map/ppermute | solution.py:648
  616.6 71.5 %all-to-all-start.3 = ((bf16[8,128,2048]{2,1,0:T(8,128)(2,1)}), bf16[8,128,2048]{2,1,0:T(8,128)(2,1)}, u32[]{:S(2)}, u32[]{:S(2)}) async-start(bf16[8,128,2048]{2,1,0:T(8,128)(2,1)} %bitcast.198), calls=%async_computation.3 | async-start | bytes 8388608 | tf_op jit(solution)/shard_map/all_to_all | solution.py:1839
  674.3 123.5 %collective-permute-start.111 = (bf16[1024,320]{0,1:T(8,128)(2,1)}, bf16[1024,320]{0,1:T(8,128)(2,1)}, u32[]{:S(2)}, u32[]{:S(2)}) collective-permute-start(bf16[1024,320]{0,1:T(8,128)(2,1)} %slice.1156), channel_id=1, source_target_pairs={{0,8},{1,9},{2,10},{3,11},{4,12},{5,13},{6,14},{7,15},{8,0},{9,1},... | collective-permute-start | bytes 1966088 | tf_op jit(solution)/shard_map/ppermute | solution.py:648
  759.7 25.2 %collective-permute-start.104 = (bf16[1024,251]{0,1:T(8,128)(2,1)S(1)}, bf16[1024,251]{0,1:T(8,128)(2,1)S(1)}, u32[]{:S(2)}, u32[]{:S(2)}) collective-permute-start(bf16[1024,251]{0,1:T(8,128)(2,1)S(1)} %slice.1131), channel_id=1, source_target_pairs={{0,8},{1,9},{2,10},{3,11},{4,12},{5,13},{6,14},{7,15},{8,0},{9,1},... | collective-permute-start | bytes 1542152 | tf_op jit(solution)/shard_map/ppermute | solution.py:648
  803.6 42.9 %all-to-all-start.4 = ((bf16[16,64,891]{2,1,0:T(8,128)(2,1)}), bf16[16,64,891]{2,1,0:T(8,128)(2,1)S(1)}, u32[]{:S(2)}, u32[]{:S(2)}) async-start(bf16[16,64,891]{2,1,0:T(8,128)(2,1)} %bitcast.208), calls=%async_computation.4 | async-start | bytes 3670016 | tf_op jit(solution)/shard_map/all_to_all | solution.py:861
  (210 other events, 2258.6 us)

commit v3 on v2

--- a/solution.py
+++ b/solution.py
@@ -921,7 +921,7 @@
 
 HEADS_HERE = 3
 OWN = HEADS_HERE * MP
-TAIL = 8
+TAIL = 16
 KEYS_AT = 2 * NS
 
 
@@ -972,16 +972,16 @@
         last_m[...] = jnp.zeros_like(last_m)
 
     lane = lax.broadcasted_iota(jnp.int32, (1, OWN), 1)
-    gate = own_ref[:, :OWN]
-    x_raw = own_ref[:, OWN : 2 * OWN]
-    m_raw = s_ref[:, : 2 * NS]
+    gate = own_ref[:, :OWN].astype(f32)
+    x_raw = own_ref[:, OWN : 2 * OWN].astype(f32)
+    m_raw = s_ref[:, : 2 * NS].astype(f32)
     cosine, sine = cos_ref[...], sin_ref[...]
 
     def turned(value):
         return (value * cosine + pltpu.roll(value, HD // 2, 1) * sine).astype(bf16)
 
-    q_ref[...] = turned(own_ref[:, 2 * OWN :])
-    k_ref[...] = turned(s_ref[:, KEYS_AT : KEYS_AT + HD])
+    q_ref[...] = turned(own_ref[:, 2 * OWN :].astype(f32))
+    k_ref[...] = turned(s_ref[:, KEYS_AT : KEYS_AT + HD].astype(f32))
     v_ref[...] = s_ref[:, KEYS_AT + HD : KEYS_AT + 2 * HD].astype(bf16)
 
     s_x = shifted_sum(
@@ -1070,13 +1070,13 @@
     def unturned(value):
         return value * cosine - pltpu.roll(value, HD // 2, 1) * sine
 
-    x_raw = own_ref[:, OWN : 2 * OWN]
-    m_raw = s_ref[:, : 2 * NS]
+    x_raw = own_ref[:, OWN : 2 * OWN].astype(f32)
+    m_raw = s_ref[:, : 2 * NS].astype(f32)
     first = block == 0
     x_pad = jnp.concatenate(
-        [jnp.where(first, 0.0, own_tail_ref[:, OWN : 2 * OWN]), x_raw], axis=0
-    )
-    m_pad = jnp.concatenate([jnp.where(first, 0.0, s_tail_ref[:, : 2 * NS]), m_raw], axis=0)
+        [jnp.where(first, 0.0, own_tail_ref[:, OWN : 2 * OWN].astype(f32)), x_raw], axis=0
+    )
+    m_pad = jnp.concatenate([jnp.where(first, 0.0, s_tail_ref[:, : 2 * NS].astype(f32)), m_raw], axis=0)
     s_x = shifted_sum(x_pad, taps_x_ref, TAIL - KC + 1, 1) + taps_x_ref[KC : KC + 1]
     s_m = shifted_sum(m_pad, taps_m_ref, TAIL - KC + 1, 1) + taps_m_ref[KC : KC + 1]
     sig_x, sig_m = logistic(s_x), logistic(s_m)
@@ -1695,13 +1695,13 @@
     g_out_bf, normed = joint(g_out_bf, normed)
     g_out = gather_start(g_out_bf, info)
     g_out.hop()
-    raw_s = mm(normed, w_s)
+    raw_s = mm(normed, w_s).astype(bf16)
     g_out.state, raw_s, got, normed = joint(g_out.state, raw_s, got, normed)
     cuts = [0, mine + HD] + [mine + HD + i * ffc for i in (1, 2, 3)]
     got = [got[:, a:b] for a, b in zip(cuts[:-1], cuts[1:])]
     other = [flip(got[0], BIT_ZH), None, None, None]
     g_out.hop()
-    raw_own = mm(normed, w_own)
+    raw_own = mm(normed, w_own).astype(bf16)
     g_out.state, raw_own = joint(g_out.state, raw_own)
     g_out.hop()
 
@@ -1814,7 +1814,7 @@
     d_q, d_k, d_v = run_attend_backward(
         info, queries, keys, values, attended_f, logs, g_att, cosine, sine
     )
-    gate = raw_own[:, :mine]
+    gate = raw_own[:, :mine].astype(f32)
     gate_sig = jax.nn.sigmoid(gate)
     y_rows = y.astype(f32)
     normed_mix = y_rows * (gate * gate_sig) * inv_mix_rows
@@ -1910,7 +1910,6 @@
     both = swap_sequences(both)
     output, grad_tokens = both[None, :rows], both[None, rows:].astype(f32)
     shared_sums.hop()
-    shared_sums.state, own_back = joint(shared_sums.state, own_back)
     shared_sums.hop()
     shared_sums.hop()
     shared_sums.state, own_back, late_got, early_got = joint(

time: 875 us -> 863 us (0.986)
    unnamed x249 -> x257, local copies, waits for them, and re-layouts: 26.6 us -> 26.5 us
  transfers between devices with their start and end apart: 118 -> 118, of which waited for: 50 -> 51; matrix products, arithmetic and copies ran while one was open for 25% -> 25% of each run, Pallas kernels for 12% -> 13%
where the time goes in v3:
time: 863 us; the launch traced here: 854 us
  waiting for transfers between devices  290 us (34%)
  starting transfers between devices  148 us (17%)
  Pallas kernels  121 us (14%)
  matrix products  116 us (13%)
  other arithmetic  89.3 us (10%)
  local copies, waits for them, and re-layouts  85 us (10%)
    ppermute x111, waiting for transfers between devices, flip(): return lax.ppermute(value, BOTH, [(i, i ^ mask) for i in range(DEVICES)])  275 us
    ppermute x111, starting transfers between devices, flip(): return lax.ppermute(value, BOTH, [(i, i ^ mask) for i in range(DEVICES)])  117 us
    pallas_call x18, Pallas kernels, assemble(): pl.pallas_call(kernel, in_specs=[pl.BlockSpec(memory_space=pltpu.SMEM)] +...  53.3 us
    dot_general x9, matrix products, mm_nt(): lax.dot_general(a, b, (((1,), (1,)), ((), ())), preferred_element_type=f32)  42 us
    dot_general x6, matrix products, mm(): return jnp.dot(a, b, preferred_element_type=f32)  39 us
    dot_general x8, matrix products, mm_tn(): lax.dot_general(a, b, (((0,), (0,)), ((), ())), preferred_element_type=f32)  35.3 us
    pallas_call x1, Pallas kernels, run_mix_backward(): pl.pallas_call(mix_backward, grid_spec=pltpu.PrefetchScalarGridSpec(num_s...  30.1 us
    unnamed x257, local copies, waits for them, and re-layouts  26.5 us
  transfers between devices with their start and end apart: 118, of which 51 were waited for; matrix products, arithmetic and copies ran while one was open for 25% of the time, Pallas kernels for 13%

profile of v3, /device:TPU:0, one launch (start us, length us, event | category | flops | bytes accessed | tf_op | source)
XLA Modules:
  0.0 853.6 jit_solution(12197930512189265980)
XLA Ops:
  18.4 22.0 %collective-permute-done.1 = bf16[64,1280]{1,0:T(8,128)(2,1)S(1)} collective-permute-done((bf16[64,1280]{1,0:T(8,128)(2,1)S(1)}, bf16[64,1280]{1,0:T(8,128)(2,1)S(1)}, u32[]{:S(2)}, u32[]{:S(2)}) %collective-permute-start.1) | collective-permute-done | bytes 163872 | tf_op jit(solution)/shard_map/ppermute | solution.py:648
  61.1 16.8 %collective-permute-done.8 = bf16[1024,256]{1,0:T(8,128)(2,1)S(1)} collective-permute-done((bf16[1024,256]{1,0:T(8,128)(2,1)S(1)}, bf16[1024,256]{1,0:T(8,128)(2,1)S(1)}, u32[]{:S(2)}, u32[]{:S(2)}) %collective-permute-start.8) | collective-permute-done | bytes 524320 | tf_op jit(solution)/shard_map/ppermute | solution.py:648
  131.6 8.3 all-to-all-start.1
  139.9 10.0 %assemble.21 = (bf16[2048,2048]{1,0:T(8,128)(2,1)}, bf16[2048,896]{1,0:T(8,128)(2,1)S(1)}, bf16[2048,128]{1,0:T(8,128)(2,1)S(1)}) custom-call(s32[4]{0:T(128)S(1)} %pad_add_fusion.info_ref.info, bf16[512,1152]{1,0:T(8,128)(2,1)} %get-tuple-element.228.refs_0_, bf16[512,1152]{1,0:T(8,128)(2,1)} %get-tuple-element.229.refs_1_, ...), custom_call_target="tpu_custom_call" | custom-call | flops 1000 | bytes 1000 | tf_op jit(solution)/shard_map/assemble/pallas_call | solution.py:694
  161.6 13.5 %convolution_convert_fusion.6.s_ref.s_tail_ref = bf16[2048,896]{1,0:T(8,128)(2,1)} fusion(bf16[2048,2048]{1,0:T(8,128)(2,1)} %get-tuple-element.249, bf16[2048,896]{1,0:T(8,128)(2,1)} %copy-done.12), kind=kOutput, calls=%fused_computation.28 | convolution fusion | flops 7518027776 | bytes 15728640 | tf_op jit(solution)/shard_map/dot_general | solution.py:865
  185.7 8.5 convolution_convert_fusion.8.own_ref.own_tail_ref
  195.6 18.4 %mix_forward.1 = (bf16[2048,192]{1,0:T(8,128)(2,1)S(1)}, bf16[2048,192]{1,0:T(8,128)(2,1)S(1)}, f32[16,8,128]{2,1,0:T(8,128)S(1)}, bf16[16,256,192]{2,1,0:T(8,12...) custom-call(s32[4]{0:T(128)S(1)} %pad_add_fusion.info_ref.info, ...), custom_call_target="tpu_custom_call" | custom-call | flops 1000 | bytes 1000 | tf_op jit(solution)/shard_map/mix_forward/pallas_call | solution.py:1207
  238.5 14.0 %collective-permute-done.28 = bf16[1024,256]{1,0:T(8,128)(2,1)} collective-permute-done((bf16[1024,256]{1,0:T(8,128)(2,1)}, bf16[1024,256]{1,0:T(8,128)(2,1)}, u32[]{:S(2)}, u32[]{:S(2)}) %collective-permute-start.28) | collective-permute-done | bytes 524320 | tf_op jit(solution)/shard_map/ppermute | solution.py:648
  258.0 9.0 %attend_forward.1 = (bf16[1024,128]{1,0:T(8,128)(2,1)S(1)}, f32[1024,128]{1,0:T(8,128)S(1)}, f32[8,8,128]{2,1,0:T(8,128)S(1)}) custom-call(s32[4]{0:T(128)S(1)} %pad_add_fusion.info_ref.info, bf16[2048,128]{1,0:T(8,128)(2,1)S(1)} %copy-done.17, bf16[2048,128]{1,0:T(8,128)(2,1)S(1)} %copy-done.20, bf16[2048,128]{1,0:T(8,128)(2,1)S(1)} %copy-done.23), custom_call_target="tpu_custom_call" | custom-call | flops 1000 | bytes 1000 | tf_op jit(solution)/shard_map/attend_forward/pallas_call | solution.py:1376
  270.0 13.0 %collective-permute-done.30 = bf16[1024,256]{1,0:T(8,128)(2,1)S(1)} collective-permute-done((bf16[1024,256]{1,0:T(8,128)(2,1)S(1)}, bf16[1024,256]{1,0:T(8,128)(2,1)S(1)}, u32[]{:S(2)}, u32[]{:S(2)}) %collective-permute-start.30) | collective-permute-done | bytes 524320 | tf_op jit(solution)/shard_map/ppermute | solution.py:648
  293.1 8.5 collective-permute-done.33
  301.9 17.3 %collective-permute-done.31 = bf16[1,2,2,128,768]{4,3,2,1,0:T(8,128)(2,1)S(1)} collective-permute-done((bf16[1,2,2,128,768]{4,3,2,1,0:T(8,128)(2,1)S(1)}, bf16[1,2,2,128,768]{4,3,2,1,0:T(8,128)(2,1)S(1)}, u32[]{:S(2)}, u32[]{:S(2)}) %collective-permute-start.31) | collective-permute-done | bytes 786464 | tf_op jit(solution)/shard_map/ppermute | solution.py:648
  352.4 7.3 collective-permute-done.50.refs_4_
  368.0 8.9 %collective-permute-done.43.refs_2_.refs_5_ = bf16[512,640]{1,0:T(8,128)(2,1)S(1)} collective-permute-done((bf16[512,640]{1,0:T(8,128)(2,1)S(1)}, bf16[512,640]{1,0:T(8,128)(2,1)S(1)}, u32[]{:S(2)}, u32[]{:S(2)}) %collective-permute-start.43) | collective-permute-done | bytes 655392 | tf_op jit(solution)/shard_map/ppermute | solution.py:648
  417.3 6.4 convolution_convert_fusion.7
  435.1 9.0 %collective-permute-done.60 = bf16[2,2,1,128,640]{4,3,2,1,0:T(8,128)(2,1)S(1)} collective-permute-done((bf16[2,2,1,128,640]{4,3,2,1,0:T(8,128)(2,1)S(1)}, bf16[2,2,1,128,640]{4,3,2,1,0:T(8,128)(2,1)S(1)}, u32[]{:S(2)}, u32[]{:S(2)}) %collective-permute-start.60) | collective-permute-done | bytes 655392 | tf_op jit(solution)/shard_map/ppermute | solution.py:648
  457.8 5.8 collective-permute-done.63
  466.4 6.6 collective-permute-done.65
  503.2 6.3 collective-permute-done.74
  513.4 14.5 %collective-permute-done.77.refs_1_.refs_4_ = bf16[512,640]{1,0:T(8,128)(2,1)S(1)} collective-permute-done((bf16[512,640]{1,0:T(8,128)(2,1)S(1)}, bf16[512,640]{1,0:T(8,128)(2,1)S(1)}, u32[]{:S(2)}, u32[]{:S(2)}) %collective-permute-start.77) | collective-permute-done | bytes 655392 | tf_op jit(solution)/shard_map/ppermute | solution.py:648
  557.3 9.9 %attend_backward.1 = (bf16[1024,128]{1,0:T(8,128)(2,1)S(1)}, f32[2048,128]{1,0:T(8,128)S(1)}, f32[2048,128]{1,0:T(8,128)S(1)}) custom-call(s32[4]{0:T(128)S(1)} %pad_add_fusion.info_ref.info, bf16[2048,128]{1,0:T(8,128)(2,1)S(1)} %copy-done.18, bf16[2048,128]{1,0:T(8,128)(2,1)S(1)} %copy-done.21, bf16[2048,128]{1,0:T(8,128)(2,1)S(1)} %copy-done.24, ...), custom_call_target="tpu_custom_call" | custom-call | flops 1000 | bytes 1000 | tf_op jit(solution)/shard_map/attend_backward/pallas_call | solution.py:1403
  590.4 17.2 %collective-permute-done.88 = bf16[1024,320]{0,1:T(8,128)(2,1)} collective-permute-done((bf16[1024,320]{0,1:T(8,128)(2,1)}, bf16[1024,320]{0,1:T(8,128)(2,1)}, u32[]{:S(2)}, u32[]{:S(2)}) %collective-permute-start.88) | collective-permute-done | bytes 655392 | tf_op jit(solution)/shard_map/ppermute | solution.py:648
  624.6 30.1 %mix_backward.1 = (bf16[2048,1408]{1,0:T(8,128)(2,1)}, f32[8,192]{1,0:T(8,128)S(1)}, f32[8,512]{1,0:T(8,128)S(1)}, f32[8,192]{1,0:T(8,128)S(1)}, f32[8,128]{1,0:T(8,128)S(1)}) custom-call(s32[4]{0:T(128)S(1)} %pad_add_fusion.info_ref.info, bf16[2048,512]{1,0:T(8,128)(2,1)S(1)} %convolution_convert_fusion.8.own_ref.own_tail_ref, ...), custom_call_target="tpu_custom_call" | custom-call | flops 1000 | bytes 1000 | tf_op jit(solution)/shard_map/mix_backward/pallas_call | solution.py:1293
  654.7 11.1 %convolution_convert_fusion = bf16[1024,2048]{1,0:T(8,128)(2,1)} fusion(bf16[2048,1408]{1,0:T(8,128)(2,1)} %pad_maximum_fusion, bf16[2048,1408]{1,0:T(8,128)(2,1)} %get-tuple-element.366), kind=kOutput, calls=%fused_computation.11 | convolution fusion | flops 5907677184 | bytes 12845056 | tf_op jit(solution)/shard_map/dot_general | solution.py:869
  669.3 11.0 %convolution_convert_fusion.1 = bf16[1024,2048]{1,0:T(8,128)(2,1)} fusion(bf16[2048,1408]{1,0:T(8,128)(2,1)} %pad_maximum_fusion, bf16[2048,1408]{1,0:T(8,128)(2,1)} %get-tuple-element.366), kind=kOutput, calls=%fused_computation.12 | convolution fusion | flops 5907677184 | bytes 12845056 | tf_op jit(solution)/shard_map/dot_general | solution.py:869
  686.8 12.9 %fusion.8 = bf16[2048,896]{1,0:T(8,128)(2,1)S(1)} fusion(bf16[2048,2048]{1,0:T(8,128)(2,1)} %get-tuple-element.249, bf16[2048,1408]{1,0:T(8,128)(2,1)} %get-tuple-element.366), kind=kOutput, calls=%fused_computation.27 | convolution fusion | flops 7518027776 | bytes 15728640 | tf_op jit(solution)/shard_map/dot_general | solution.py:873
  708.2 8.6 %collective-permute-done.92 = bf16[2,2,1,128,640]{4,3,2,1,0:T(8,128)(2,1)S(1)} collective-permute-done((bf16[2,2,1,128,640]{4,3,2,1,0:T(8,128)(2,1)S(1)}, bf16[2,2,1,128,640]{4,3,2,1,0:T(8,128)(2,1)S(1)}, u32[]{:S(2)}, u32[]{:S(2)}) %collective-permute-start.92) | collective-permute-done | bytes 655392 | tf_op jit(solution)/shard_map/ppermute | solution.py:648
  729.8 8.7 %assemble.35 = bf16[2048,1152]{1,0:T(8,128)(2,1)S(1)} custom-call(s32[4]{0:T(128)S(1)} %pad_add_fusion.info_ref.info, bf16[2048,1152]{1,0:T(8,128)(2,1)S(1)} %pad_maximum_fusion.1.refs_0_), custom_call_target="tpu_custom_call" | custom-call | flops 1000 | bytes 1000 | tf_op jit(solution)/shard_map/assemble/pallas_call | solution.py:694
  767.3 12.5 %collective-permute-done.101 = bf16[1,2,2,128,384]{4,3,2,1,0:T(8,128)(2,1)S(1)} collective-permute-done((bf16[1,2,2,128,384]{4,3,2,1,0:T(8,128)(2,1)S(1)}, bf16[1,2,2,128,384]{4,3,2,1,0:T(8,128)(2,1)S(1)}, u32[]{:S(2)}, u32[]{:S(2)}) %collective-permute-start.101) | collective-permute-done | bytes 393248 | tf_op jit(solution)/shard_map/ppermute | solution.py:648
  806.3 10.0 %collective-permute-start.112 = (bf16[64,1152]{1,0:T(8,128)(2,1)S(1)}, bf16[64,1152]{1,0:T(8,128)(2,1)S(1)}, u32[]{:S(2)}, u32[]{:S(2)}) collective-permute-start(bf16[64,1152]{1,0:T(8,128)(2,1)S(1)} %slice.1623), channel_id=1, source_target_pairs={{0,8},{1,9},{2,10},{3,11},{4,12},{5,13},{6,14},{7,15},{8,0},{9,1},... | collective-permute-start | bytes 442376 | tf_op jit(solution)/shard_map/ppermute | solution.py:648
  817.6 6.5 collective-permute-done.112
  825.5 10.2 %all-to-all-done.4 = bf16[16,64,891]{2,1,0:T(8,128)(2,1)S(1)} async-done(((bf16[16,64,891]{2,1,0:T(8,128)(2,1)}), bf16[16,64,891]{2,1,0:T(8,128)(2,1)S(1)}, u32[]{:S(2)}, u32[]{:S(2)}) %all-to-all-start.4) | async-done | bytes 1824800 | tf_op jit(solution)/shard_map/all_to_all | solution.py:861
  (778 shorter events, 476.9 us)
Async XLA Ops:
  3.1 37.3 %collective-permute-start = (bf16[256,2048]{1,0:T(8,128)(2,1)}, bf16[256,2048]{1,0:T(8,128)(2,1)}, u32[]{:S(2)}, u32[]{:S(2)}) collective-permute-start(bf16[256,2048]{1,0:T(8,128)(2,1)} %pad_maximum_fusion.9), channel_id=1, source_target_pairs={{8,16},{9,17},{10,18},{11,19},{12,20},{13,21},{14,22},{15,23},{16,... | collective-permute-start | bytes 3145736 | tf_op jit(solution)/shard_map/ppermute | solution.py:658
  5.7 34.6 %collective-permute-start.1 = (bf16[64,1280]{1,0:T(8,128)(2,1)S(1)}, bf16[64,1280]{1,0:T(8,128)(2,1)S(1)}, u32[]{:S(2)}, u32[]{:S(2)}) collective-permute-start(bf16[64,1280]{1,0:T(8,128)(2,1)S(1)} %concatenate.183), channel_id=1, source_target_pairs={{0,8},{1,9},{2,10},{3,11},{4,12},{5,13},{6,14},{7,15},{8,0},{9,1},... | collective-permute-start | bytes 491528 | tf_op jit(solution)/shard_map/ppermute | solution.py:648
  13.2 33.4 %all-to-all-start = ((bf16[16,64,512]{2,1,0:T(8,128)(2,1)}), bf16[16,64,512]{2,1,0:T(8,128)(2,1)S(1)}, u32[]{:S(2)}, u32[]{:S(2)}) async-start(bf16[16,64,512]{2,1,0:T(8,128)(2,1)} %maximum_maximum_fusion.2), calls=%async_computation | async-start | bytes 2097152 | tf_op jit(solution)/shard_map/all_to_all | solution.py:861
  51.6 26.3 %collective-permute-start.8 = (bf16[1024,256]{1,0:T(8,128)(2,1)S(1)}, bf16[1024,256]{1,0:T(8,128)(2,1)S(1)}, u32[]{:S(2)}, u32[]{:S(2)}) collective-permute-start(bf16[1024,256]{1,0:T(8,128)(2,1)S(1)} %slice.936), channel_id=1, source_target_pairs={{0,8},{1,9},{2,10},{3,11},{4,12},{5,13},{6,14},{7,15},{8,0},{9,1},... | collective-permute-start | bytes 1572872 | tf_op jit(solution)/shard_map/ppermute | solution.py:648
  57.9 23.1 %collective-permute-start.5 = (bf16[256,1152]{1,0:T(8,128)(2,1)S(1)}, bf16[256,1152]{1,0:T(8,128)(2,1)S(1)}, u32[]{:S(2)}, u32[]{:S(2)}) collective-permute-start(bf16[256,1152]{1,0:T(8,128)(2,1)S(1)} %get-tuple-element.218.refs_0_), channel_id=1, source_target_pairs={{0,2},{1,3},{2,0},{3,1},{4,6},{5,7},{6,4},{7,5},{8,10},{9,11},{10,... | collective-permute-start | bytes 1769480 | tf_op jit(solution)/shard_map/ppermute | solution.py:648
  85.3 36.0 %collective-permute-start.10 = (bf16[512,1152]{1,0:T(8,128)(2,1)}, bf16[512,1152]{1,0:T(8,128)(2,1)S(1)}, u32[]{:S(2)}, u32[]{:S(2)}) collective-permute-start(bf16[512,1152]{1,0:T(8,128)(2,1)} %get-tuple-element.229.refs_1_), channel_id=1, source_target_pairs={{0,4},{1,5},{2,6},{3,7},{4,0},{5,1},{6,2},{7,3},{8,12},{9,13},{10,... | collective-permute-start | bytes 3538952 | tf_op jit(solution)/shard_map/ppermute | solution.py:648
  85.4 35.9 %collective-permute-start.9 = (bf16[512,1152]{1,0:T(8,128)(2,1)}, bf16[512,1152]{1,0:T(8,128)(2,1)S(1)}, u32[]{:S(2)}, u32[]{:S(2)}) collective-permute-start(bf16[512,1152]{1,0:T(8,128)(2,1)} %get-tuple-element.228.refs_0_), channel_id=1, source_target_pairs={{0,1},{1,0},{2,3},{3,2},{4,5},{5,4},{6,7},{7,6},{8,9},{9,8},{10,11... | collective-permute-start | bytes 3538952 | tf_op jit(solution)/shard_map/ppermute | solution.py:648
  86.1 33.2 %collective-permute-start.11 = (bf16[512,1024]{1,0:T(8,128)(2,1)}, bf16[512,1024]{1,0:T(8,128)(2,1)}, u32[]{:S(2)}, u32[]{:S(2)}) collective-permute-start(bf16[512,1024]{1,0:T(8,128)(2,1)} %get-tuple-element.230.refs_2_), channel_id=1, source_target_pairs={{0,2},{1,3},{2,0},{3,1},{4,6},{5,7},{6,4},{7,5},{8,10},{9,11},{10,... | collective-permute-start | bytes 3145736 | tf_op jit(solution)/shard_map/ppermute | solution.py:648
  92.9 26.5 %collective-permute-start.12 = (bf16[1024,256]{1,0:T(8,128)(2,1)}, bf16[1024,256]{1,0:T(8,128)(2,1)}, u32[]{:S(2)}, u32[]{:S(2)}) collective-permute-start(bf16[1024,256]{1,0:T(8,128)(2,1)} %slice.939), channel_id=1, source_target_pairs={{0,8},{1,9},{2,10},{3,11},{4,12},{5,13},{6,14},{7,15},{8,0},{9,1},... | collective-permute-start | bytes 1572872 | tf_op jit(solution)/shard_map/ppermute | solution.py:648
  115.0 24.9 %collective-permute-start.13 = (bf16[512,3328]{1,0:T(8,128)(2,1)}, bf16[512,3328]{1,0:T(8,128)(2,1)}, u32[]{:S(2)}, u32[]{:S(2)}) collective-permute-start(bf16[512,3328]{1,0:T(8,128)(2,1)} %get-tuple-element.234), channel_id=1, source_target_pairs={{0,16},{1,17},{2,18},{3,19},{4,20},{5,21},{6,22},{7,23},{8,24},{9,... | collective-permute-start | bytes 10223624 | tf_op jit(solution)/shard_map/ppermute | solution.py:648
  131.6 45.0 %all-to-all-start.1 = ((bf16[16,64,1088]{2,1,0:T(8,128)(2,1)}), bf16[16,64,1088]{2,1,0:T(8,128)(2,1)}, u32[]{:S(2)}, u32[]{:S(2)}) async-start(bf16[16,64,1088]{2,1,0:T(8,128)(2,1)} %concatenate.191), calls=%async_computation.1 | async-start | bytes 4718592 | tf_op jit(solution)/shard_map/all_to_all | solution.py:861
  154.2 22.3 %collective-permute-start.16 = (bf16[128,640]{1,0:T(8,128)(2,1)S(1)}, bf16[128,640]{1,0:T(8,128)(2,1)S(1)}, u32[]{:S(2)}, u32[]{:S(2)}) collective-permute-start(bf16[128,640]{1,0:T(8,128)(2,1)S(1)} %get-tuple-element.241.refs_1_), channel_id=1, source_target_pairs={{0,2},{1,3},{2,0},{3,1},{4,6},{5,7},{6,4},{7,5},{8,10},{9,11},{10,... | collective-permute-start | bytes 491528 | tf_op jit(solution)/shard_map/ppermute | solution.py:648
  184.1 35.7 %collective-permute-start.21 = (bf16[1024,320]{0,1:T(8,128)(2,1)}, bf16[1024,320]{0,1:T(8,128)(2,1)S(1)}, u32[]{:S(2)}, u32[]{:S(2)}) collective-permute-start(bf16[1024,320]{0,1:T(8,128)(2,1)} %copy.115), channel_id=1, source_target_pairs={{0,8},{1,9},{2,10},{3,11},{4,12},{5,13},{6,14},{7,15},{8,0},{9,1},... | collective-permute-start | bytes 1966088 | tf_op jit(solution)/shard_map/ppermute | solution.py:648
  226.0 26.6 %collective-permute-start.28 = (bf16[1024,256]{1,0:T(8,128)(2,1)}, bf16[1024,256]{1,0:T(8,128)(2,1)}, u32[]{:S(2)}, u32[]{:S(2)}) collective-permute-start(bf16[1024,256]{1,0:T(8,128)(2,1)} %get-tuple-element.458), channel_id=1, source_target_pairs={{0,8},{1,9},{2,10},{3,11},{4,12},{5,13},{6,14},{7,15},{8,0},{9,1},... | collective-permute-start | bytes 1572872 | tf_op jit(solution)/shard_map/ppermute | solution.py:648
  258.0 25.0 %collective-permute-start.29 = (bf16[1024,2048]{1,0:T(8,128)(2,1)}, bf16[1024,2048]{1,0:T(8,128)(2,1)}, u32[]{:S(2)}, u32[]{:S(2)}) collective-permute-start(bf16[1024,2048]{1,0:T(8,128)(2,1)} %multiply_convert_fusion), channel_id=1, source_target_pairs={{0,16},{1,17},{2,18},{3,19},{4,20},{5,21},{6,22},{7,23},{8,24},{9,... | collective-permute-start | bytes 12582920 | tf_op jit(solution)/shard_map/ppermute | solution.py:648
  258.0 25.0 %collective-permute-start.30 = (bf16[1024,256]{1,0:T(8,128)(2,1)S(1)}, bf16[1024,256]{1,0:T(8,128)(2,1)S(1)}, u32[]{:S(2)}, u32[]{:S(2)}) collective-permute-start(bf16[1024,256]{1,0:T(8,128)(2,1)S(1)} %copy-done.85), channel_id=1, source_target_pairs={{0,8},{1,9},{2,10},{3,11},{4,12},{5,13},{6,14},{7,15},{8,0},{9,1},... | collective-permute-start | bytes 1572872 | tf_op jit(solution)/shard_map/ppermute | solution.py:648
  287.4 31.7 %collective-permute-start.31 = (bf16[1,2,2,128,768]{4,3,2,1,0:T(8,128)(2,1)S(1)}, bf16[1,2,2,128,768]{4,3,2,1,0:T(8,128)(2,1)S(1)}, u32[]{:S(2)}, u32[]{:S(2)}) collective-permute-start(bf16[1,2,2,128,768]{4,3,2,1,0:T(8,128)(2,1)S(1)} %get-tuple-element.432), channel_id=1, source_target_pairs={{0,4},{1,5},{2,6},{3,7},{4,0},{5,1},{6,2},{7,3},{8,12},{9,13},{10,... | collective-permute-start | bytes 2359304 | tf_op jit(solution)/shard_map/ppermute | solution.py:648
  289.3 31.6 %collective-permute-start.32 = (bf16[2,1,2,128,640]{4,3,2,1,0:T(8,128)(2,1)S(1)}, bf16[2,1,2,128,640]{4,3,2,1,0:T(8,128)(2,1)S(1)}, u32[]{:S(2)}, u32[]{:S(2)}) collective-permute-start(bf16[2,1,2,128,640]{4,3,2,1,0:T(8,128)(2,1)S(1)} %get-tuple-element.430), channel_id=1, source_target_pairs={{0,2},{1,3},{2,0},{3,1},{4,6},{5,7},{6,4},{7,5},{8,10},{9,11},{10,... | collective-permute-start | bytes 1966088 | tf_op jit(solution)/shard_map/ppermute | solution.py:648
  290.8 30.9 %collective-permute-start.37 = (bf16[1024,256]{1,0:T(8,128)(2,1)S(1)}, bf16[1024,256]{1,0:T(8,128)(2,1)S(1)}, u32[]{:S(2)}, u32[]{:S(2)}) collective-permute-start(bf16[1024,256]{1,0:T(8,128)(2,1)S(1)} %copy-done.84), channel_id=1, source_target_pairs={{0,8},{1,9},{2,10},{3,11},{4,12},{5,13},{6,14},{7,15},{8,0},{9,1},... | collective-permute-start | bytes 1572872 | tf_op jit(solution)/shard_map/ppermute | solution.py:648
  301.8 23.2 %collective-permute-start.36 = (bf16[1,2,1,128,640]{4,3,2,1,0:T(8,128)(2,1)S(1)}, bf16[1,2,1,128,640]{4,3,2,1,0:T(8,128)(2,1)S(1)}, u32[]{:S(2)}, u32[]{:S(2)}) collective-permute-start(bf16[1,2,1,128,640]{4,3,2,1,0:T(8,128)(2,1)S(1)} %get-tuple-element.479), channel_id=1, source_target_pairs={{0,4},{1,5},{2,6},{3,7},{4,0},{5,1},{6,2},{7,3},{8,12},{9,13},{10,... | collective-permute-start | bytes 983048 | tf_op jit(solution)/shard_map/ppermute | solution.py:648
  352.1 24.9 %collective-permute-start.41 = (bf16[512,768]{1,0:T(8,128)(2,1)S(1)}, bf16[512,768]{1,0:T(8,128)(2,1)S(1)}, u32[]{:S(2)}, u32[]{:S(2)}) collective-permute-start(bf16[512,768]{1,0:T(8,128)(2,1)S(1)} %get-tuple-element.284.refs_0_), channel_id=1, source_target_pairs={{0,1},{1,0},{2,3},{3,2},{4,5},{5,4},{6,7},{7,6},{8,9},{9,8},{10,11... | collective-permute-start | bytes 2359304 | tf_op jit(solution)/shard_map/ppermute | solution.py:648
  448.4 43.9 %collective-permute-start.75 = (bf16[1024,2048]{1,0:T(8,128)(2,1)}, bf16[1024,2048]{1,0:T(8,128)(2,1)}, u32[]{:S(2)}, u32[]{:S(2)}) collective-permute-start(bf16[1024,2048]{1,0:T(8,128)(2,1)} %convolution_convert_fusion.3), channel_id=1, source_target_pairs={{0,16},{1,17},{2,18},{3,19},{4,20},{5,21},{6,22},{7,23},{8,24},{9,... | collective-permute-start | bytes 12582920 | tf_op jit(solution)/shard_map/ppermute | solution.py:648
  452.7 25.7 %collective-permute-start.67 = (bf16[1024,256]{1,0:T(8,128)(2,1)S(1)}, bf16[1024,256]{1,0:T(8,128)(2,1)S(1)}, u32[]{:S(2)}, u32[]{:S(2)}) collective-permute-start(bf16[1024,256]{1,0:T(8,128)(2,1)S(1)} %slice.1047), channel_id=1, source_target_pairs={{0,8},{1,9},{2,10},{3,11},{4,12},{5,13},{6,14},{7,15},{8,0},{9,1},... | collective-permute-start | bytes 1572872 | tf_op jit(solution)/shard_map/ppermute | solution.py:648
  485.2 24.3 %collective-permute-start.74 = (bf16[1024,256]{1,0:T(8,128)(2,1)S(1)}, bf16[1024,256]{1,0:T(8,128)(2,1)S(1)}, u32[]{:S(2)}, u32[]{:S(2)}) collective-permute-start(bf16[1024,256]{1,0:T(8,128)(2,1)S(1)} %slice.1049), channel_id=1, source_target_pairs={{0,8},{1,9},{2,10},{3,11},{4,12},{5,13},{6,14},{7,15},{8,0},{9,1},... | collective-permute-start | bytes 1572872 | tf_op jit(solution)/shard_map/ppermute | solution.py:648
  533.0 34.3 %collective-permute-start.87 = (bf16[1024,256]{1,0:T(8,128)(2,1)}, bf16[1024,256]{1,0:T(8,128)(2,1)}, u32[]{:S(2)}, u32[]{:S(2)}) collective-permute-start(bf16[1024,256]{1,0:T(8,128)(2,1)} %slice.1055), channel_id=1, source_target_pairs={{0,8},{1,9},{2,10},{3,11},{4,12},{5,13},{6,14},{7,15},{8,0},{9,1},... | collective-permute-start | bytes 1572872 | tf_op jit(solution)/shard_map/ppermute | solution.py:648
  570.2 38.9 %all-to-all-start.2 = ((bf16[16,64,768]{2,1,0:T(8,128)(2,1)}), bf16[16,64,768]{2,1,0:T(8,128)(2,1)}, u32[]{:S(2)}, u32[]{:S(2)}) async-start(bf16[16,64,768]{2,1,0:T(8,128)(2,1)} %bitcast.209), calls=%async_computation.2 | async-start | bytes 3145728 | tf_op jit(solution)/shard_map/all_to_all | solution.py:861
  576.5 31.1 %collective-permute-start.88 = (bf16[1024,320]{0,1:T(8,128)(2,1)}, bf16[1024,320]{0,1:T(8,128)(2,1)}, u32[]{:S(2)}, u32[]{:S(2)}) collective-permute-start(bf16[1024,320]{0,1:T(8,128)(2,1)} %slice.1057), channel_id=1, source_target_pairs={{0,8},{1,9},{2,10},{3,11},{4,12},{5,13},{6,14},{7,15},{8,0},{9,1},... | collective-permute-start | bytes 1966088 | tf_op jit(solution)/shard_map/ppermute | solution.py:648
  609.0 71.3 %all-to-all-start.3 = ((bf16[8,128,2048]{2,1,0:T(8,128)(2,1)}), bf16[8,128,2048]{2,1,0:T(8,128)(2,1)}, u32[]{:S(2)}, u32[]{:S(2)}) async-start(bf16[8,128,2048]{2,1,0:T(8,128)(2,1)} %bitcast.198), calls=%async_computation.3 | async-start | bytes 8388608 | tf_op jit(solution)/shard_map/all_to_all | solution.py:1839
  666.7 121.8 %collective-permute-start.111 = (bf16[1024,320]{0,1:T(8,128)(2,1)}, bf16[1024,320]{0,1:T(8,128)(2,1)}, u32[]{:S(2)}, u32[]{:S(2)}) collective-permute-start(bf16[1024,320]{0,1:T(8,128)(2,1)} %slice.1156), channel_id=1, source_target_pairs={{0,8},{1,9},{2,10},{3,11},{4,12},{5,13},{6,14},{7,15},{8,0},{9,1},... | collective-permute-start | bytes 1966088 | tf_op jit(solution)/shard_map/ppermute | solution.py:648
  751.9 38.3 %collective-permute-start.110 = (bf16[1024,251]{0,1:T(8,128)(2,1)S(1)}, bf16[1024,251]{0,1:T(8,128)(2,1)S(1)}, u32[]{:S(2)}, u32[]{:S(2)}) collective-permute-start(bf16[1024,251]{0,1:T(8,128)(2,1)S(1)} %slice.1155), channel_id=1, source_target_pairs={{0,8},{1,9},{2,10},{3,11},{4,12},{5,13},{6,14},{7,15},{8,0},{9,1},... | collective-permute-start | bytes 1542152 | tf_op jit(solution)/shard_map/ppermute | solution.py:648
  757.7 22.2 %collective-permute-start.101 = (bf16[1,2,2,128,384]{4,3,2,1,0:T(8,128)(2,1)S(1)}, bf16[1,2,2,128,384]{4,3,2,1,0:T(8,128)(2,1)S(1)}, u32[]{:S(2)}, u32[]{:S(2)}) collective-permute-start(bf16[1,2,2,128,384]{4,3,2,1,0:T(8,128)(2,1)S(1)} %get-tuple-element.442), channel_id=1, source_target_pairs={{0,4},{1,5},{2,6},{3,7},{4,0},{5,1},{6,2},{7,3},{8,12},{9,13},{10,... | collective-permute-start | bytes 1179656 | tf_op jit(solution)/shard_map/ppermute | solution.py:648
  795.4 40.3 %all-to-all-start.4 = ((bf16[16,64,891]{2,1,0:T(8,128)(2,1)}), bf16[16,64,891]{2,1,0:T(8,128)(2,1)S(1)}, u32[]{:S(2)}, u32[]{:S(2)}) async-start(bf16[16,64,891]{2,1,0:T(8,128)(2,1)} %bitcast.208), calls=%async_computation.4 | async-start | bytes 3670016 | tf_op jit(solution)/shard_map/all_to_all | solution.py:861
  (214 other events, 2097.2 us)

commit v4 on v3

--- a/solution.py
+++ b/solution.py
@@ -903,6 +903,12 @@
     return 1.0 / (1.0 + jnp.exp(-value))
 
 
+def softplus(value):
+    small = jnp.exp(-jnp.abs(value))
+    series = small * (1.0 - small * (0.5 - small * (1.0 / 3.0 - 0.25 * small)))
+    return jnp.maximum(value, 0.0) + jnp.where(small < 0.01, series, jnp.log(1.0 + small))
+
+
 def by_head(columns, lane):
     spread = columns[:, 0:1]
     for head in range(1, HEADS_HERE):
@@ -999,7 +1005,7 @@
     place = info[0]
     picked = k_mm(s_ref[:, KEYS_AT + 2 * HD :].astype(bf16), step_lanes(place, lane).astype(bf16))
     raised = picked + vec_ref[0:1]
-    step = jnp.maximum(raised, 0.0) + jnp.log(1.0 + jnp.exp(-jnp.abs(raised)))
+    step = softplus(raised)
     cum, last, reach = block_decays(cum_col_ref[...], cum_row_ref[0], lane)
     scaled = step * x
     inter = k_nt(c_map, b_map)
@@ -1086,7 +1092,7 @@
     select = step_lanes(place, lane)
     step_raw = s_ref[:, KEYS_AT + 2 * HD :].astype(bf16)
     raised = k_mm(step_raw, select.astype(bf16)) + vec_ref[0:1]
-    step = jnp.maximum(raised, 0.0) + jnp.log(1.0 + jnp.exp(-jnp.abs(raised)))
+    step = softplus(raised)
     cum, last, reach = block_decays(cum_col_ref[...], cum_row_ref[0], lane)
     scaled = step * x
 

time: 863 us -> 864 us (level)
  no operation moved by 1% of the time
where the time goes in v4:
time: 864 us; the launch traced here: 855 us
  waiting for transfers between devices  290 us (34%)
  starting transfers between devices  148 us (17%)
  Pallas kernels  122 us (14%)
  matrix products  116 us (13%)
  other arithmetic  89.3 us (10%)
  local copies, waits for them, and re-layouts  85 us (10%)
    ppermute x111, waiting for transfers between devices, flip(): return lax.ppermute(value, BOTH, [(i, i ^ mask) for i in range(DEVICES)])  276 us
    ppermute x111, starting transfers between devices, flip(): return lax.ppermute(value, BOTH, [(i, i ^ mask) for i in range(DEVICES)])  117 us
    pallas_call x18, Pallas kernels, assemble(): pl.pallas_call(kernel, in_specs=[pl.BlockSpec(memory_space=pltpu.SMEM)] +...  53.3 us
    dot_general x9, matrix products, mm_nt(): lax.dot_general(a, b, (((1,), (1,)), ((), ())), preferred_element_type=f32)  42 us
    dot_general x6, matrix products, mm(): return jnp.dot(a, b, preferred_element_type=f32)  39 us
    dot_general x8, matrix products, mm_tn(): lax.dot_general(a, b, (((0,), (0,)), ((), ())), preferred_element_type=f32)  35.3 us
    pallas_call x1, Pallas kernels, run_mix_backward(): pl.pallas_call(mix_backward, grid_spec=pltpu.PrefetchScalarGridSpec(num_s...  30.9 us
    unnamed x257, local copies, waits for them, and re-layouts  26.5 us
  transfers between devices with their start and end apart: 118, of which 51 were waited for; matrix products, arithmetic and copies ran while one was open for 25% of the time, Pallas kernels for 13%

profile of v4, /device:TPU:0, one launch (start us, length us, event | category | flops | bytes accessed | tf_op | source)
XLA Modules:
  0.0 855.0 jit_solution(15722418277856458951)
XLA Ops:
  18.4 22.0 %collective-permute-done.1 = bf16[64,1280]{1,0:T(8,128)(2,1)S(1)} collective-permute-done((bf16[64,1280]{1,0:T(8,128)(2,1)S(1)}, bf16[64,1280]{1,0:T(8,128)(2,1)S(1)}, u32[]{:S(2)}, u32[]{:S(2)}) %collective-permute-start.1) | collective-permute-done | bytes 163872 | tf_op jit(solution)/shard_map/ppermute | solution.py:648
  61.1 16.8 %collective-permute-done.8 = bf16[1024,256]{1,0:T(8,128)(2,1)S(1)} collective-permute-done((bf16[1024,256]{1,0:T(8,128)(2,1)S(1)}, bf16[1024,256]{1,0:T(8,128)(2,1)S(1)}, u32[]{:S(2)}, u32[]{:S(2)}) %collective-permute-start.8) | collective-permute-done | bytes 524320 | tf_op jit(solution)/shard_map/ppermute | solution.py:648
  131.6 8.3 all-to-all-start.1
  139.9 10.0 %assemble.21 = (bf16[2048,2048]{1,0:T(8,128)(2,1)}, bf16[2048,896]{1,0:T(8,128)(2,1)S(1)}, bf16[2048,128]{1,0:T(8,128)(2,1)S(1)}) custom-call(s32[4]{0:T(128)S(1)} %pad_add_fusion.info_ref.info, bf16[512,1152]{1,0:T(8,128)(2,1)} %get-tuple-element.228.refs_0_, bf16[512,1152]{1,0:T(8,128)(2,1)} %get-tuple-element.229.refs_1_, ...), custom_call_target="tpu_custom_call" | custom-call | flops 1000 | bytes 1000 | tf_op jit(solution)/shard_map/assemble/pallas_call | solution.py:694
  161.6 13.5 %convolution_convert_fusion.6.s_ref.s_tail_ref = bf16[2048,896]{1,0:T(8,128)(2,1)} fusion(bf16[2048,2048]{1,0:T(8,128)(2,1)} %get-tuple-element.249, bf16[2048,896]{1,0:T(8,128)(2,1)} %copy-done.12), kind=kOutput, calls=%fused_computation.28 | convolution fusion | flops 7518027776 | bytes 15728640 | tf_op jit(solution)/shard_map/dot_general | solution.py:865
  185.7 8.5 convolution_convert_fusion.8.own_ref.own_tail_ref
  195.6 19.1 %mix_forward.1 = (bf16[2048,192]{1,0:T(8,128)(2,1)S(1)}, bf16[2048,192]{1,0:T(8,128)(2,1)S(1)}, f32[16,8,128]{2,1,0:T(8,128)S(1)}, bf16[16,256,192]{2,1,0:T(8,12...) custom-call(s32[4]{0:T(128)S(1)} %pad_add_fusion.info_ref.info, ...), custom_call_target="tpu_custom_call" | custom-call | flops 1000 | bytes 1000 | tf_op jit(solution)/shard_map/mix_forward/pallas_call | solution.py:1213
  239.1 14.0 %collective-permute-done.28 = bf16[1024,256]{1,0:T(8,128)(2,1)} collective-permute-done((bf16[1024,256]{1,0:T(8,128)(2,1)}, bf16[1024,256]{1,0:T(8,128)(2,1)}, u32[]{:S(2)}, u32[]{:S(2)}) %collective-permute-start.28) | collective-permute-done | bytes 524320 | tf_op jit(solution)/shard_map/ppermute | solution.py:648
  258.6 9.0 %attend_forward.1 = (bf16[1024,128]{1,0:T(8,128)(2,1)S(1)}, f32[1024,128]{1,0:T(8,128)S(1)}, f32[8,8,128]{2,1,0:T(8,128)S(1)}) custom-call(s32[4]{0:T(128)S(1)} %pad_add_fusion.info_ref.info, bf16[2048,128]{1,0:T(8,128)(2,1)S(1)} %copy-done.17, bf16[2048,128]{1,0:T(8,128)(2,1)S(1)} %copy-done.20, bf16[2048,128]{1,0:T(8,128)(2,1)S(1)} %copy-done.23), custom_call_target="tpu_custom_call" | custom-call | flops 1000 | bytes 1000 | tf_op jit(solution)/shard_map/attend_forward/pallas_call | solution.py:1382
  270.6 13.0 %collective-permute-done.30 = bf16[1024,256]{1,0:T(8,128)(2,1)S(1)} collective-permute-done((bf16[1024,256]{1,0:T(8,128)(2,1)S(1)}, bf16[1024,256]{1,0:T(8,128)(2,1)S(1)}, u32[]{:S(2)}, u32[]{:S(2)}) %collective-permute-start.30) | collective-permute-done | bytes 524320 | tf_op jit(solution)/shard_map/ppermute | solution.py:648
  293.7 8.5 collective-permute-done.33
  302.5 17.3 %collective-permute-done.31 = bf16[1,2,2,128,768]{4,3,2,1,0:T(8,128)(2,1)S(1)} collective-permute-done((bf16[1,2,2,128,768]{4,3,2,1,0:T(8,128)(2,1)S(1)}, bf16[1,2,2,128,768]{4,3,2,1,0:T(8,128)(2,1)S(1)}, u32[]{:S(2)}, u32[]{:S(2)}) %collective-permute-start.31) | collective-permute-done | bytes 786464 | tf_op jit(solution)/shard_map/ppermute | solution.py:648
  353.1 7.2 collective-permute-done.50.refs_4_
  368.7 8.9 %collective-permute-done.43.refs_2_.refs_5_ = bf16[512,640]{1,0:T(8,128)(2,1)S(1)} collective-permute-done((bf16[512,640]{1,0:T(8,128)(2,1)S(1)}, bf16[512,640]{1,0:T(8,128)(2,1)S(1)}, u32[]{:S(2)}, u32[]{:S(2)}) %collective-permute-start.43) | collective-permute-done | bytes 655392 | tf_op jit(solution)/shard_map/ppermute | solution.py:648
  417.9 6.4 convolution_convert_fusion.7
  435.8 9.0 %collective-permute-done.60 = bf16[2,2,1,128,640]{4,3,2,1,0:T(8,128)(2,1)S(1)} collective-permute-done((bf16[2,2,1,128,640]{4,3,2,1,0:T(8,128)(2,1)S(1)}, bf16[2,2,1,128,640]{4,3,2,1,0:T(8,128)(2,1)S(1)}, u32[]{:S(2)}, u32[]{:S(2)}) %collective-permute-start.60) | collective-permute-done | bytes 655392 | tf_op jit(solution)/shard_map/ppermute | solution.py:648
  458.5 5.9 collective-permute-done.63
  467.0 6.6 collective-permute-done.65
  503.9 6.3 collective-permute-done.74
  514.0 14.5 %collective-permute-done.77.refs_1_.refs_4_ = bf16[512,640]{1,0:T(8,128)(2,1)S(1)} collective-permute-done((bf16[512,640]{1,0:T(8,128)(2,1)S(1)}, bf16[512,640]{1,0:T(8,128)(2,1)S(1)}, u32[]{:S(2)}, u32[]{:S(2)}) %collective-permute-start.77) | collective-permute-done | bytes 655392 | tf_op jit(solution)/shard_map/ppermute | solution.py:648
  557.9 9.9 %attend_backward.1 = (bf16[1024,128]{1,0:T(8,128)(2,1)S(1)}, f32[2048,128]{1,0:T(8,128)S(1)}, f32[2048,128]{1,0:T(8,128)S(1)}) custom-call(s32[4]{0:T(128)S(1)} %pad_add_fusion.info_ref.info, bf16[2048,128]{1,0:T(8,128)(2,1)S(1)} %copy-done.18, bf16[2048,128]{1,0:T(8,128)(2,1)S(1)} %copy-done.21, bf16[2048,128]{1,0:T(8,128)(2,1)S(1)} %copy-done.24, ...), custom_call_target="tpu_custom_call" | custom-call | flops 1000 | bytes 1000 | tf_op jit(solution)/shard_map/attend_backward/pallas_call | solution.py:1409
  591.0 17.2 %collective-permute-done.88 = bf16[1024,320]{0,1:T(8,128)(2,1)} collective-permute-done((bf16[1024,320]{0,1:T(8,128)(2,1)}, bf16[1024,320]{0,1:T(8,128)(2,1)}, u32[]{:S(2)}, u32[]{:S(2)}) %collective-permute-start.88) | collective-permute-done | bytes 655392 | tf_op jit(solution)/shard_map/ppermute | solution.py:648
  625.2 30.9 %mix_backward.1 = (bf16[2048,1408]{1,0:T(8,128)(2,1)}, f32[8,192]{1,0:T(8,128)S(1)}, f32[8,512]{1,0:T(8,128)S(1)}, f32[8,192]{1,0:T(8,128)S(1)}, f32[8,128]{1,0:T(8,128)S(1)}) custom-call(s32[4]{0:T(128)S(1)} %pad_add_fusion.info_ref.info, bf16[2048,512]{1,0:T(8,128)(2,1)S(1)} %convolution_convert_fusion.8.own_ref.own_tail_ref, ...), custom_call_target="tpu_custom_call" | custom-call | flops 1000 | bytes 1000 | tf_op jit(solution)/shard_map/mix_backward/pallas_call | solution.py:1299
  656.1 11.1 %convolution_convert_fusion = bf16[1024,2048]{1,0:T(8,128)(2,1)} fusion(bf16[2048,1408]{1,0:T(8,128)(2,1)} %pad_maximum_fusion, bf16[2048,1408]{1,0:T(8,128)(2,1)} %get-tuple-element.366), kind=kOutput, calls=%fused_computation.11 | convolution fusion | flops 5907677184 | bytes 12845056 | tf_op jit(solution)/shard_map/dot_general | solution.py:869
  670.7 11.0 %convolution_convert_fusion.1 = bf16[1024,2048]{1,0:T(8,128)(2,1)} fusion(bf16[2048,1408]{1,0:T(8,128)(2,1)} %pad_maximum_fusion, bf16[2048,1408]{1,0:T(8,128)(2,1)} %get-tuple-element.366), kind=kOutput, calls=%fused_computation.12 | convolution fusion | flops 5907677184 | bytes 12845056 | tf_op jit(solution)/shard_map/dot_general | solution.py:869
  688.2 12.9 %fusion.8 = bf16[2048,896]{1,0:T(8,128)(2,1)S(1)} fusion(bf16[2048,2048]{1,0:T(8,128)(2,1)} %get-tuple-element.249, bf16[2048,1408]{1,0:T(8,128)(2,1)} %get-tuple-element.366), kind=kOutput, calls=%fused_computation.27 | convolution fusion | flops 7518027776 | bytes 15728640 | tf_op jit(solution)/shard_map/dot_general | solution.py:873
  709.6 8.6 %collective-permute-done.92 = bf16[2,2,1,128,640]{4,3,2,1,0:T(8,128)(2,1)S(1)} collective-permute-done((bf16[2,2,1,128,640]{4,3,2,1,0:T(8,128)(2,1)S(1)}, bf16[2,2,1,128,640]{4,3,2,1,0:T(8,128)(2,1)S(1)}, u32[]{:S(2)}, u32[]{:S(2)}) %collective-permute-start.92) | collective-permute-done | bytes 655392 | tf_op jit(solution)/shard_map/ppermute | solution.py:648
  731.2 8.7 %assemble.35 = bf16[2048,1152]{1,0:T(8,128)(2,1)S(1)} custom-call(s32[4]{0:T(128)S(1)} %pad_add_fusion.info_ref.info, bf16[2048,1152]{1,0:T(8,128)(2,1)S(1)} %pad_maximum_fusion.1.refs_0_), custom_call_target="tpu_custom_call" | custom-call | flops 1000 | bytes 1000 | tf_op jit(solution)/shard_map/assemble/pallas_call | solution.py:694
  768.8 12.5 %collective-permute-done.101 = bf16[1,2,2,128,384]{4,3,2,1,0:T(8,128)(2,1)S(1)} collective-permute-done((bf16[1,2,2,128,384]{4,3,2,1,0:T(8,128)(2,1)S(1)}, bf16[1,2,2,128,384]{4,3,2,1,0:T(8,128)(2,1)S(1)}, u32[]{:S(2)}, u32[]{:S(2)}) %collective-permute-start.101) | collective-permute-done | bytes 393248 | tf_op jit(solution)/shard_map/ppermute | solution.py:648
  807.8 10.0 %collective-permute-start.112 = (bf16[64,1152]{1,0:T(8,128)(2,1)S(1)}, bf16[64,1152]{1,0:T(8,128)(2,1)S(1)}, u32[]{:S(2)}, u32[]{:S(2)}) collective-permute-start(bf16[64,1152]{1,0:T(8,128)(2,1)S(1)} %slice.1623), channel_id=1, source_target_pairs={{0,8},{1,9},{2,10},{3,11},{4,12},{5,13},{6,14},{7,15},{8,0},{9,1},... | collective-permute-start | bytes 442376 | tf_op jit(solution)/shard_map/ppermute | solution.py:648
  819.1 6.5 collective-permute-done.112
  826.9 10.2 %all-to-all-done.4 = bf16[16,64,891]{2,1,0:T(8,128)(2,1)S(1)} async-done(((bf16[16,64,891]{2,1,0:T(8,128)(2,1)}), bf16[16,64,891]{2,1,0:T(8,128)(2,1)S(1)}, u32[]{:S(2)}, u32[]{:S(2)}) %all-to-all-start.4) | async-done | bytes 1824800 | tf_op jit(solution)/shard_map/all_to_all | solution.py:861
  (778 shorter events, 476.9 us)
Async XLA Ops:
  3.1 37.3 %collective-permute-start = (bf16[256,2048]{1,0:T(8,128)(2,1)}, bf16[256,2048]{1,0:T(8,128)(2,1)}, u32[]{:S(2)}, u32[]{:S(2)}) collective-permute-start(bf16[256,2048]{1,0:T(8,128)(2,1)} %pad_maximum_fusion.9), channel_id=1, source_target_pairs={{8,16},{9,17},{10,18},{11,19},{12,20},{13,21},{14,22},{15,23},{16,... | collective-permute-start | bytes 3145736 | tf_op jit(solution)/shard_map/ppermute | solution.py:658
  5.7 34.6 %collective-permute-start.1 = (bf16[64,1280]{1,0:T(8,128)(2,1)S(1)}, bf16[64,1280]{1,0:T(8,128)(2,1)S(1)}, u32[]{:S(2)}, u32[]{:S(2)}) collective-permute-start(bf16[64,1280]{1,0:T(8,128)(2,1)S(1)} %concatenate.183), channel_id=1, source_target_pairs={{0,8},{1,9},{2,10},{3,11},{4,12},{5,13},{6,14},{7,15},{8,0},{9,1},... | collective-permute-start | bytes 491528 | tf_op jit(solution)/shard_map/ppermute | solution.py:648
  13.2 33.4 %all-to-all-start = ((bf16[16,64,512]{2,1,0:T(8,128)(2,1)}), bf16[16,64,512]{2,1,0:T(8,128)(2,1)S(1)}, u32[]{:S(2)}, u32[]{:S(2)}) async-start(bf16[16,64,512]{2,1,0:T(8,128)(2,1)} %maximum_maximum_fusion.2), calls=%async_computation | async-start | bytes 2097152 | tf_op jit(solution)/shard_map/all_to_all | solution.py:861
  51.6 26.3 %collective-permute-start.8 = (bf16[1024,256]{1,0:T(8,128)(2,1)S(1)}, bf16[1024,256]{1,0:T(8,128)(2,1)S(1)}, u32[]{:S(2)}, u32[]{:S(2)}) collective-permute-start(bf16[1024,256]{1,0:T(8,128)(2,1)S(1)} %slice.936), channel_id=1, source_target_pairs={{0,8},{1,9},{2,10},{3,11},{4,12},{5,13},{6,14},{7,15},{8,0},{9,1},... | collective-permute-start | bytes 1572872 | tf_op jit(solution)/shard_map/ppermute | solution.py:648
  57.9 23.1 %collective-permute-start.5 = (bf16[256,1152]{1,0:T(8,128)(2,1)S(1)}, bf16[256,1152]{1,0:T(8,128)(2,1)S(1)}, u32[]{:S(2)}, u32[]{:S(2)}) collective-permute-start(bf16[256,1152]{1,0:T(8,128)(2,1)S(1)} %get-tuple-element.218.refs_0_), channel_id=1, source_target_pairs={{0,2},{1,3},{2,0},{3,1},{4,6},{5,7},{6,4},{7,5},{8,10},{9,11},{10,... | collective-permute-start | bytes 1769480 | tf_op jit(solution)/shard_map/ppermute | solution.py:648
  85.3 36.0 %collective-permute-start.10 = (bf16[512,1152]{1,0:T(8,128)(2,1)}, bf16[512,1152]{1,0:T(8,128)(2,1)S(1)}, u32[]{:S(2)}, u32[]{:S(2)}) collective-permute-start(bf16[512,1152]{1,0:T(8,128)(2,1)} %get-tuple-element.229.refs_1_), channel_id=1, source_target_pairs={{0,4},{1,5},{2,6},{3,7},{4,0},{5,1},{6,2},{7,3},{8,12},{9,13},{10,... | collective-permute-start | bytes 3538952 | tf_op jit(solution)/shard_map/ppermute | solution.py:648
  85.4 35.9 %collective-permute-start.9 = (bf16[512,1152]{1,0:T(8,128)(2,1)}, bf16[512,1152]{1,0:T(8,128)(2,1)S(1)}, u32[]{:S(2)}, u32[]{:S(2)}) collective-permute-start(bf16[512,1152]{1,0:T(8,128)(2,1)} %get-tuple-element.228.refs_0_), channel_id=1, source_target_pairs={{0,1},{1,0},{2,3},{3,2},{4,5},{5,4},{6,7},{7,6},{8,9},{9,8},{10,11... | collective-permute-start | bytes 3538952 | tf_op jit(solution)/shard_map/ppermute | solution.py:648
  86.1 33.2 %collective-permute-start.11 = (bf16[512,1024]{1,0:T(8,128)(2,1)}, bf16[512,1024]{1,0:T(8,128)(2,1)}, u32[]{:S(2)}, u32[]{:S(2)}) collective-permute-start(bf16[512,1024]{1,0:T(8,128)(2,1)} %get-tuple-element.230.refs_2_), channel_id=1, source_target_pairs={{0,2},{1,3},{2,0},{3,1},{4,6},{5,7},{6,4},{7,5},{8,10},{9,11},{10,... | collective-permute-start | bytes 3145736 | tf_op jit(solution)/shard_map/ppermute | solution.py:648
  92.9 26.5 %collective-permute-start.12 = (bf16[1024,256]{1,0:T(8,128)(2,1)}, bf16[1024,256]{1,0:T(8,128)(2,1)}, u32[]{:S(2)}, u32[]{:S(2)}) collective-permute-start(bf16[1024,256]{1,0:T(8,128)(2,1)} %slice.939), channel_id=1, source_target_pairs={{0,8},{1,9},{2,10},{3,11},{4,12},{5,13},{6,14},{7,15},{8,0},{9,1},... | collective-permute-start | bytes 1572872 | tf_op jit(solution)/shard_map/ppermute | solution.py:648
  115.0 24.9 %collective-permute-start.13 = (bf16[512,3328]{1,0:T(8,128)(2,1)}, bf16[512,3328]{1,0:T(8,128)(2,1)}, u32[]{:S(2)}, u32[]{:S(2)}) collective-permute-start(bf16[512,3328]{1,0:T(8,128)(2,1)} %get-tuple-element.234), channel_id=1, source_target_pairs={{0,16},{1,17},{2,18},{3,19},{4,20},{5,21},{6,22},{7,23},{8,24},{9,... | collective-permute-start | bytes 10223624 | tf_op jit(solution)/shard_map/ppermute | solution.py:648
  131.6 45.0 %all-to-all-start.1 = ((bf16[16,64,1088]{2,1,0:T(8,128)(2,1)}), bf16[16,64,1088]{2,1,0:T(8,128)(2,1)}, u32[]{:S(2)}, u32[]{:S(2)}) async-start(bf16[16,64,1088]{2,1,0:T(8,128)(2,1)} %concatenate.191), calls=%async_computation.1 | async-start | bytes 4718592 | tf_op jit(solution)/shard_map/all_to_all | solution.py:861
  154.2 22.3 %collective-permute-start.16 = (bf16[128,640]{1,0:T(8,128)(2,1)S(1)}, bf16[128,640]{1,0:T(8,128)(2,1)S(1)}, u32[]{:S(2)}, u32[]{:S(2)}) collective-permute-start(bf16[128,640]{1,0:T(8,128)(2,1)S(1)} %get-tuple-element.241.refs_1_), channel_id=1, source_target_pairs={{0,2},{1,3},{2,0},{3,1},{4,6},{5,7},{6,4},{7,5},{8,10},{9,11},{10,... | collective-permute-start | bytes 491528 | tf_op jit(solution)/shard_map/ppermute | solution.py:648
  184.1 36.3 %collective-permute-start.21 = (bf16[1024,320]{0,1:T(8,128)(2,1)}, bf16[1024,320]{0,1:T(8,128)(2,1)S(1)}, u32[]{:S(2)}, u32[]{:S(2)}) collective-permute-start(bf16[1024,320]{0,1:T(8,128)(2,1)} %copy.115), channel_id=1, source_target_pairs={{0,8},{1,9},{2,10},{3,11},{4,12},{5,13},{6,14},{7,15},{8,0},{9,1},... | collective-permute-start | bytes 1966088 | tf_op jit(solution)/shard_map/ppermute | solution.py:648
  226.6 26.6 %collective-permute-start.28 = (bf16[1024,256]{1,0:T(8,128)(2,1)}, bf16[1024,256]{1,0:T(8,128)(2,1)}, u32[]{:S(2)}, u32[]{:S(2)}) collective-permute-start(bf16[1024,256]{1,0:T(8,128)(2,1)} %get-tuple-element.458), channel_id=1, source_target_pairs={{0,8},{1,9},{2,10},{3,11},{4,12},{5,13},{6,14},{7,15},{8,0},{9,1},... | collective-permute-start | bytes 1572872 | tf_op jit(solution)/shard_map/ppermute | solution.py:648
  258.6 25.0 %collective-permute-start.29 = (bf16[1024,2048]{1,0:T(8,128)(2,1)}, bf16[1024,2048]{1,0:T(8,128)(2,1)}, u32[]{:S(2)}, u32[]{:S(2)}) collective-permute-start(bf16[1024,2048]{1,0:T(8,128)(2,1)} %multiply_convert_fusion), channel_id=1, source_target_pairs={{0,16},{1,17},{2,18},{3,19},{4,20},{5,21},{6,22},{7,23},{8,24},{9,... | collective-permute-start | bytes 12582920 | tf_op jit(solution)/shard_map/ppermute | solution.py:648
  258.6 25.0 %collective-permute-start.30 = (bf16[1024,256]{1,0:T(8,128)(2,1)S(1)}, bf16[1024,256]{1,0:T(8,128)(2,1)S(1)}, u32[]{:S(2)}, u32[]{:S(2)}) collective-permute-start(bf16[1024,256]{1,0:T(8,128)(2,1)S(1)} %copy-done.85), channel_id=1, source_target_pairs={{0,8},{1,9},{2,10},{3,11},{4,12},{5,13},{6,14},{7,15},{8,0},{9,1},... | collective-permute-start | bytes 1572872 | tf_op jit(solution)/shard_map/ppermute | solution.py:648
  288.1 31.7 %collective-permute-start.31 = (bf16[1,2,2,128,768]{4,3,2,1,0:T(8,128)(2,1)S(1)}, bf16[1,2,2,128,768]{4,3,2,1,0:T(8,128)(2,1)S(1)}, u32[]{:S(2)}, u32[]{:S(2)}) collective-permute-start(bf16[1,2,2,128,768]{4,3,2,1,0:T(8,128)(2,1)S(1)} %get-tuple-element.432), channel_id=1, source_target_pairs={{0,4},{1,5},{2,6},{3,7},{4,0},{5,1},{6,2},{7,3},{8,12},{9,13},{10,... | collective-permute-start | bytes 2359304 | tf_op jit(solution)/shard_map/ppermute | solution.py:648
  289.9 31.6 %collective-permute-start.32 = (bf16[2,1,2,128,640]{4,3,2,1,0:T(8,128)(2,1)S(1)}, bf16[2,1,2,128,640]{4,3,2,1,0:T(8,128)(2,1)S(1)}, u32[]{:S(2)}, u32[]{:S(2)}) collective-permute-start(bf16[2,1,2,128,640]{4,3,2,1,0:T(8,128)(2,1)S(1)} %get-tuple-element.430), channel_id=1, source_target_pairs={{0,2},{1,3},{2,0},{3,1},{4,6},{5,7},{6,4},{7,5},{8,10},{9,11},{10,... | collective-permute-start | bytes 1966088 | tf_op jit(solution)/shard_map/ppermute | solution.py:648
  291.4 30.9 %collective-permute-start.37 = (bf16[1024,256]{1,0:T(8,128)(2,1)S(1)}, bf16[1024,256]{1,0:T(8,128)(2,1)S(1)}, u32[]{:S(2)}, u32[]{:S(2)}) collective-permute-start(bf16[1024,256]{1,0:T(8,128)(2,1)S(1)} %copy-done.84), channel_id=1, source_target_pairs={{0,8},{1,9},{2,10},{3,11},{4,12},{5,13},{6,14},{7,15},{8,0},{9,1},... | collective-permute-start | bytes 1572872 | tf_op jit(solution)/shard_map/ppermute | solution.py:648
  302.4 23.2 %collective-permute-start.36 = (bf16[1,2,1,128,640]{4,3,2,1,0:T(8,128)(2,1)S(1)}, bf16[1,2,1,128,640]{4,3,2,1,0:T(8,128)(2,1)S(1)}, u32[]{:S(2)}, u32[]{:S(2)}) collective-permute-start(bf16[1,2,1,128,640]{4,3,2,1,0:T(8,128)(2,1)S(1)} %get-tuple-element.479), channel_id=1, source_target_pairs={{0,4},{1,5},{2,6},{3,7},{4,0},{5,1},{6,2},{7,3},{8,12},{9,13},{10,... | collective-permute-start | bytes 983048 | tf_op jit(solution)/shard_map/ppermute | solution.py:648
  352.7 24.9 %collective-permute-start.41 = (bf16[512,768]{1,0:T(8,128)(2,1)S(1)}, bf16[512,768]{1,0:T(8,128)(2,1)S(1)}, u32[]{:S(2)}, u32[]{:S(2)}) collective-permute-start(bf16[512,768]{1,0:T(8,128)(2,1)S(1)} %get-tuple-element.284.refs_0_), channel_id=1, source_target_pairs={{0,1},{1,0},{2,3},{3,2},{4,5},{5,4},{6,7},{7,6},{8,9},{9,8},{10,11... | collective-permute-start | bytes 2359304 | tf_op jit(solution)/shard_map/ppermute | solution.py:648
  449.1 43.9 %collective-permute-start.75 = (bf16[1024,2048]{1,0:T(8,128)(2,1)}, bf16[1024,2048]{1,0:T(8,128)(2,1)}, u32[]{:S(2)}, u32[]{:S(2)}) collective-permute-start(bf16[1024,2048]{1,0:T(8,128)(2,1)} %convolution_convert_fusion.3), channel_id=1, source_target_pairs={{0,16},{1,17},{2,18},{3,19},{4,20},{5,21},{6,22},{7,23},{8,24},{9,... | collective-permute-start | bytes 12582920 | tf_op jit(solution)/shard_map/ppermute | solution.py:648
  453.4 25.7 %collective-permute-start.67 = (bf16[1024,256]{1,0:T(8,128)(2,1)S(1)}, bf16[1024,256]{1,0:T(8,128)(2,1)S(1)}, u32[]{:S(2)}, u32[]{:S(2)}) collective-permute-start(bf16[1024,256]{1,0:T(8,128)(2,1)S(1)} %slice.1047), channel_id=1, source_target_pairs={{0,8},{1,9},{2,10},{3,11},{4,12},{5,13},{6,14},{7,15},{8,0},{9,1},... | collective-permute-start | bytes 1572872 | tf_op jit(solution)/shard_map/ppermute | solution.py:648
  485.9 24.3 %collective-permute-start.74 = (bf16[1024,256]{1,0:T(8,128)(2,1)S(1)}, bf16[1024,256]{1,0:T(8,128)(2,1)S(1)}, u32[]{:S(2)}, u32[]{:S(2)}) collective-permute-start(bf16[1024,256]{1,0:T(8,128)(2,1)S(1)} %slice.1049), channel_id=1, source_target_pairs={{0,8},{1,9},{2,10},{3,11},{4,12},{5,13},{6,14},{7,15},{8,0},{9,1},... | collective-permute-start | bytes 1572872 | tf_op jit(solution)/shard_map/ppermute | solution.py:648
  533.7 34.3 %collective-permute-start.87 = (bf16[1024,256]{1,0:T(8,128)(2,1)}, bf16[1024,256]{1,0:T(8,128)(2,1)}, u32[]{:S(2)}, u32[]{:S(2)}) collective-permute-start(bf16[1024,256]{1,0:T(8,128)(2,1)} %slice.1055), channel_id=1, source_target_pairs={{0,8},{1,9},{2,10},{3,11},{4,12},{5,13},{6,14},{7,15},{8,0},{9,1},... | collective-permute-start | bytes 1572872 | tf_op jit(solution)/shard_map/ppermute | solution.py:648
  570.8 38.9 %all-to-all-start.2 = ((bf16[16,64,768]{2,1,0:T(8,128)(2,1)}), bf16[16,64,768]{2,1,0:T(8,128)(2,1)}, u32[]{:S(2)}, u32[]{:S(2)}) async-start(bf16[16,64,768]{2,1,0:T(8,128)(2,1)} %bitcast.209), calls=%async_computation.2 | async-start | bytes 3145728 | tf_op jit(solution)/shard_map/all_to_all | solution.py:861
  577.2 31.1 %collective-permute-start.88 = (bf16[1024,320]{0,1:T(8,128)(2,1)}, bf16[1024,320]{0,1:T(8,128)(2,1)}, u32[]{:S(2)}, u32[]{:S(2)}) collective-permute-start(bf16[1024,320]{0,1:T(8,128)(2,1)} %slice.1057), channel_id=1, source_target_pairs={{0,8},{1,9},{2,10},{3,11},{4,12},{5,13},{6,14},{7,15},{8,0},{9,1},... | collective-permute-start | bytes 1966088 | tf_op jit(solution)/shard_map/ppermute | solution.py:648
  609.7 72.1 %all-to-all-start.3 = ((bf16[8,128,2048]{2,1,0:T(8,128)(2,1)}), bf16[8,128,2048]{2,1,0:T(8,128)(2,1)}, u32[]{:S(2)}, u32[]{:S(2)}) async-start(bf16[8,128,2048]{2,1,0:T(8,128)(2,1)} %bitcast.198), calls=%async_computation.3 | async-start | bytes 8388608 | tf_op jit(solution)/shard_map/all_to_all | solution.py:1845
  668.2 121.8 %collective-permute-start.111 = (bf16[1024,320]{0,1:T(8,128)(2,1)}, bf16[1024,320]{0,1:T(8,128)(2,1)}, u32[]{:S(2)}, u32[]{:S(2)}) collective-permute-start(bf16[1024,320]{0,1:T(8,128)(2,1)} %slice.1156), channel_id=1, source_target_pairs={{0,8},{1,9},{2,10},{3,11},{4,12},{5,13},{6,14},{7,15},{8,0},{9,1},... | collective-permute-start | bytes 1966088 | tf_op jit(solution)/shard_map/ppermute | solution.py:648
  753.3 38.3 %collective-permute-start.110 = (bf16[1024,251]{0,1:T(8,128)(2,1)S(1)}, bf16[1024,251]{0,1:T(8,128)(2,1)S(1)}, u32[]{:S(2)}, u32[]{:S(2)}) collective-permute-start(bf16[1024,251]{0,1:T(8,128)(2,1)S(1)} %slice.1155), channel_id=1, source_target_pairs={{0,8},{1,9},{2,10},{3,11},{4,12},{5,13},{6,14},{7,15},{8,0},{9,1},... | collective-permute-start | bytes 1542152 | tf_op jit(solution)/shard_map/ppermute | solution.py:648
  759.1 22.2 %collective-permute-start.101 = (bf16[1,2,2,128,384]{4,3,2,1,0:T(8,128)(2,1)S(1)}, bf16[1,2,2,128,384]{4,3,2,1,0:T(8,128)(2,1)S(1)}, u32[]{:S(2)}, u32[]{:S(2)}) collective-permute-start(bf16[1,2,2,128,384]{4,3,2,1,0:T(8,128)(2,1)S(1)} %get-tuple-element.442), channel_id=1, source_target_pairs={{0,4},{1,5},{2,6},{3,7},{4,0},{5,1},{6,2},{7,3},{8,12},{9,13},{10,... | collective-permute-start | bytes 1179656 | tf_op jit(solution)/shard_map/ppermute | solution.py:648
  796.8 40.3 %all-to-all-start.4 = ((bf16[16,64,891]{2,1,0:T(8,128)(2,1)}), bf16[16,64,891]{2,1,0:T(8,128)(2,1)S(1)}, u32[]{:S(2)}, u32[]{:S(2)}) async-start(bf16[16,64,891]{2,1,0:T(8,128)(2,1)} %bitcast.208), calls=%async_computation.4 | async-start | bytes 3670016 | tf_op jit(solution)/shard_map/all_to_all | solution.py:861
  (214 other events, 2097.5 us)

commit v5 on v4

--- a/solution.py
+++ b/solution.py
@@ -1871,12 +1871,12 @@
     sums.state, out_got = joint(sums.state, out_got)
     sums.hop()
     (g_all,) = sums.then(g_all)
+    d_shared = mm_tn(normed, g_all[:, own_width:]).astype(bf16)
+    sums.state, d_shared, g_all = joint(sums.state, d_shared, g_all)
+    sums.hop()
+    d_shared, g_all, d_ff_got, out_got = sums.then(d_shared, g_all, d_ff_got, out_got)
     d_own = mm_tn(normed, g_all[:, mine : 2 * mine]).astype(bf16)
     d_own = jnp.concatenate([d_own, small_grads], axis=1)
-    d_shared = mm_tn(normed, g_all[:, own_width:]).astype(bf16)
-    sums.state, d_own, d_shared = joint(sums.state, d_own, d_shared)
-    sums.hop()
-    d_shared, d_ff_got, out_got = sums.then(d_shared, d_ff_got, out_got)
     out_part = jnp.sum(out_got.astype(f32), axis=0)
     out_rows = (hidden + out_part).astype(bf16)
 
@@ -1902,7 +1902,7 @@
 
         moves.append((0, fixed(block * shard, shard, 0, d_shared.shape[1]), goal))
     d_shared = assemble([d_shared], [(d_shared.shape, bf16, moves)], info)[0]
-    sums.state, d_shared = joint(sums.state, d_shared)
+    sums.state, d_shared, d_own = joint(sums.state, d_shared, d_own)
     shared_sums = Scatter(d_shared[:half_rows], d_shared[half_rows:])
     sums.hop()
     g_in, d_own = joint(sums.result(), d_own)

time: 864 us -> 863 us (level)
  transfers between devices with their start and end apart: 118 -> 118, of which waited for: 51 -> 50; matrix products, arithmetic and copies ran while one was open for 25% -> 25% of each run, Pallas kernels for 13% -> 13%
where the time goes in v5:
time: 863 us; the launch traced here: 853 us
  waiting for transfers between devices  285 us (33%)
  starting transfers between devices  152 us (18%)
  Pallas kernels  122 us (14%)
  matrix products  116 us (13%)
  other arithmetic  89.3 us (10%)
  local copies, waits for them, and re-layouts  85.2 us (10%)
    ppermute x111, waiting for transfers between devices, flip(): return lax.ppermute(value, BOTH, [(i, i ^ mask) for i in range(DEVICES)])  270 us
    ppermute x111, starting transfers between devices, flip(): return lax.ppermute(value, BOTH, [(i, i ^ mask) for i in range(DEVICES)])  121 us
    pallas_call x18, Pallas kernels, assemble(): pl.pallas_call(kernel, in_specs=[pl.BlockSpec(memory_space=pltpu.SMEM)] +...  53.3 us
    dot_general x9, matrix products, mm_nt(): lax.dot_general(a, b, (((1,), (1,)), ((), ())), preferred_element_type=f32)  42 us
    dot_general x6, matrix products, mm(): return jnp.dot(a, b, preferred_element_type=f32)  39 us
    dot_general x8, matrix products, mm_tn(): lax.dot_general(a, b, (((0,), (0,)), ((), ())), preferred_element_type=f32)  35.1 us
    pallas_call x1, Pallas kernels, run_mix_backward(): pl.pallas_call(mix_backward, grid_spec=pltpu.PrefetchScalarGridSpec(num_s...  30.9 us
    unnamed x257, local copies, waits for them, and re-layouts  26.8 us
  transfers between devices with their start and end apart: 118, of which 50 were waited for; matrix products, arithmetic and copies ran while one was open for 25% of the time, Pallas kernels for 13%

profile of v5, /device:TPU:0, one launch (start us, length us, event | category | flops | bytes accessed | tf_op | source)
XLA Modules:
  0.0 853.3 jit_solution(17983904984663133022)
XLA Ops:
  18.4 22.0 %collective-permute-done.1 = bf16[64,1280]{1,0:T(8,128)(2,1)S(1)} collective-permute-done((bf16[64,1280]{1,0:T(8,128)(2,1)S(1)}, bf16[64,1280]{1,0:T(8,128)(2,1)S(1)}, u32[]{:S(2)}, u32[]{:S(2)}) %collective-permute-start.1) | collective-permute-done | bytes 163872 | tf_op jit(solution)/shard_map/ppermute | solution.py:648
  61.1 16.8 %collective-permute-done.8 = bf16[1024,256]{1,0:T(8,128)(2,1)S(1)} collective-permute-done((bf16[1024,256]{1,0:T(8,128)(2,1)S(1)}, bf16[1024,256]{1,0:T(8,128)(2,1)S(1)}, u32[]{:S(2)}, u32[]{:S(2)}) %collective-permute-start.8) | collective-permute-done | bytes 524320 | tf_op jit(solution)/shard_map/ppermute | solution.py:648
  131.6 8.3 all-to-all-start.1
  139.9 10.0 %assemble.21 = (bf16[2048,2048]{1,0:T(8,128)(2,1)}, bf16[2048,896]{1,0:T(8,128)(2,1)S(1)}, bf16[2048,128]{1,0:T(8,128)(2,1)S(1)}) custom-call(s32[4]{0:T(128)S(1)} %pad_add_fusion.info_ref.info, bf16[512,1152]{1,0:T(8,128)(2,1)} %get-tuple-element.230.refs_0_, bf16[512,1152]{1,0:T(8,128)(2,1)} %get-tuple-element.231.refs_1_, ...), custom_call_target="tpu_custom_call" | custom-call | flops 1000 | bytes 1000 | tf_op jit(solution)/shard_map/assemble/pallas_call | solution.py:694
  161.6 13.5 %convolution_convert_fusion.6.s_ref.s_tail_ref = bf16[2048,896]{1,0:T(8,128)(2,1)} fusion(bf16[2048,2048]{1,0:T(8,128)(2,1)} %get-tuple-element.251, bf16[2048,896]{1,0:T(8,128)(2,1)} %copy-done.12), kind=kOutput, calls=%fused_computation.28 | convolution fusion | flops 7518027776 | bytes 15728640 | tf_op jit(solution)/shard_map/dot_general | solution.py:865
  185.7 8.5 convolution_convert_fusion.8.own_ref.own_tail_ref
  195.6 19.1 %mix_forward.1 = (bf16[2048,192]{1,0:T(8,128)(2,1)S(1)}, bf16[2048,192]{1,0:T(8,128)(2,1)S(1)}, f32[16,8,128]{2,1,0:T(8,128)S(1)}, bf16[16,256,192]{2,1,0:T(8,12...) custom-call(s32[4]{0:T(128)S(1)} %pad_add_fusion.info_ref.info, ...), custom_call_target="tpu_custom_call" | custom-call | flops 1000 | bytes 1000 | tf_op jit(solution)/shard_map/mix_forward/pallas_call | solution.py:1213
  239.1 14.0 %collective-permute-done.28 = bf16[1024,256]{1,0:T(8,128)(2,1)} collective-permute-done((bf16[1024,256]{1,0:T(8,128)(2,1)}, bf16[1024,256]{1,0:T(8,128)(2,1)}, u32[]{:S(2)}, u32[]{:S(2)}) %collective-permute-start.28) | collective-permute-done | bytes 524320 | tf_op jit(solution)/shard_map/ppermute | solution.py:648
  258.6 9.0 %attend_forward.1 = (bf16[1024,128]{1,0:T(8,128)(2,1)S(1)}, f32[1024,128]{1,0:T(8,128)S(1)}, f32[8,8,128]{2,1,0:T(8,128)S(1)}) custom-call(s32[4]{0:T(128)S(1)} %pad_add_fusion.info_ref.info, bf16[2048,128]{1,0:T(8,128)(2,1)S(1)} %copy-done.17, bf16[2048,128]{1,0:T(8,128)(2,1)S(1)} %copy-done.20, bf16[2048,128]{1,0:T(8,128)(2,1)S(1)} %copy-done.23), custom_call_target="tpu_custom_call" | custom-call | flops 1000 | bytes 1000 | tf_op jit(solution)/shard_map/attend_forward/pallas_call | solution.py:1382
  270.6 13.0 %collective-permute-done.30 = bf16[1024,256]{1,0:T(8,128)(2,1)S(1)} collective-permute-done((bf16[1024,256]{1,0:T(8,128)(2,1)S(1)}, bf16[1024,256]{1,0:T(8,128)(2,1)S(1)}, u32[]{:S(2)}, u32[]{:S(2)}) %collective-permute-start.30) | collective-permute-done | bytes 524320 | tf_op jit(solution)/shard_map/ppermute | solution.py:648
  293.7 8.5 %collective-permute-done.33 = bf16[2,2,1,128,640]{4,3,2,1,0:T(8,128)(2,1)S(1)} collective-permute-done((bf16[2,2,1,128,640]{4,3,2,1,0:T(8,128)(2,1)S(1)}, bf16[2,2,1,128,640]{4,3,2,1,0:T(8,128)(2,1)S(1)}, u32[]{:S(2)}, u32[]{:S(2)}) %collective-permute-start.33) | collective-permute-done | bytes 655392 | tf_op jit(solution)/shard_map/ppermute | solution.py:648
  302.5 17.3 %collective-permute-done.31 = bf16[1,2,2,128,768]{4,3,2,1,0:T(8,128)(2,1)S(1)} collective-permute-done((bf16[1,2,2,128,768]{4,3,2,1,0:T(8,128)(2,1)S(1)}, bf16[1,2,2,128,768]{4,3,2,1,0:T(8,128)(2,1)S(1)}, u32[]{:S(2)}, u32[]{:S(2)}) %collective-permute-start.31) | collective-permute-done | bytes 786464 | tf_op jit(solution)/shard_map/ppermute | solution.py:648
  353.1 7.2 collective-permute-done.50.refs_4_
  368.7 8.9 %collective-permute-done.43.refs_2_.refs_5_ = bf16[512,640]{1,0:T(8,128)(2,1)S(1)} collective-permute-done((bf16[512,640]{1,0:T(8,128)(2,1)S(1)}, bf16[512,640]{1,0:T(8,128)(2,1)S(1)}, u32[]{:S(2)}, u32[]{:S(2)}) %collective-permute-start.43) | collective-permute-done | bytes 655392 | tf_op jit(solution)/shard_map/ppermute | solution.py:648
  417.9 6.4 convolution_convert_fusion.7
  435.8 9.0 %collective-permute-done.60 = bf16[2,2,1,128,640]{4,3,2,1,0:T(8,128)(2,1)S(1)} collective-permute-done((bf16[2,2,1,128,640]{4,3,2,1,0:T(8,128)(2,1)S(1)}, bf16[2,2,1,128,640]{4,3,2,1,0:T(8,128)(2,1)S(1)}, u32[]{:S(2)}, u32[]{:S(2)}) %collective-permute-start.60) | collective-permute-done | bytes 655392 | tf_op jit(solution)/shard_map/ppermute | solution.py:648
  467.0 6.6 collective-permute-done.65
  500.6 10.6 %collective-permute-done.73.refs_5_ = bf16[256,640]{1,0:T(8,128)(2,1)S(1)} collective-permute-done((bf16[256,640]{1,0:T(8,128)(2,1)S(1)}, bf16[256,640]{1,0:T(8,128)(2,1)S(1)}, u32[]{:S(2)}, u32[]{:S(2)}) %collective-permute-start.73) | collective-permute-done | bytes 327712 | tf_op jit(solution)/shard_map/ppermute | solution.py:648
  515.1 13.4 %collective-permute-done.77.refs_1_.refs_4_ = bf16[512,640]{1,0:T(8,128)(2,1)S(1)} collective-permute-done((bf16[512,640]{1,0:T(8,128)(2,1)S(1)}, bf16[512,640]{1,0:T(8,128)(2,1)S(1)}, u32[]{:S(2)}, u32[]{:S(2)}) %collective-permute-start.77) | collective-permute-done | bytes 655392 | tf_op jit(solution)/shard_map/ppermute | solution.py:648
  558.0 9.9 %attend_backward.1 = (bf16[1024,128]{1,0:T(8,128)(2,1)S(1)}, f32[2048,128]{1,0:T(8,128)S(1)}, f32[2048,128]{1,0:T(8,128)S(1)}) custom-call(s32[4]{0:T(128)S(1)} %pad_add_fusion.info_ref.info, bf16[2048,128]{1,0:T(8,128)(2,1)S(1)} %copy-done.18, bf16[2048,128]{1,0:T(8,128)(2,1)S(1)} %copy-done.21, bf16[2048,128]{1,0:T(8,128)(2,1)S(1)} %copy-done.24, ...), custom_call_target="tpu_custom_call" | custom-call | flops 1000 | bytes 1000 | tf_op jit(solution)/shard_map/attend_backward/pallas_call | solution.py:1409
  591.1 17.2 %collective-permute-done.88 = bf16[1024,320]{0,1:T(8,128)(2,1)} collective-permute-done((bf16[1024,320]{0,1:T(8,128)(2,1)}, bf16[1024,320]{0,1:T(8,128)(2,1)}, u32[]{:S(2)}, u32[]{:S(2)}) %collective-permute-start.88) | collective-permute-done | bytes 655392 | tf_op jit(solution)/shard_map/ppermute | solution.py:648
  625.3 30.9 %mix_backward.1 = (bf16[2048,1408]{1,0:T(8,128)(2,1)}, f32[8,192]{1,0:T(8,128)S(1)}, f32[8,512]{1,0:T(8,128)S(1)}, f32[8,192]{1,0:T(8,128)S(1)}, f32[8,128]{1,0:T(8,128)S(1)}) custom-call(s32[4]{0:T(128)S(1)} %pad_add_fusion.info_ref.info, bf16[2048,512]{1,0:T(8,128)(2,1)S(1)} %convolution_convert_fusion.8.own_ref.own_tail_ref, ...), custom_call_target="tpu_custom_call" | custom-call | flops 1000 | bytes 1000 | tf_op jit(solution)/shard_map/mix_backward/pallas_call | solution.py:1299
  656.2 11.1 %convolution_convert_fusion = bf16[1024,2048]{1,0:T(8,128)(2,1)} fusion(bf16[2048,1408]{1,0:T(8,128)(2,1)} %pad_maximum_fusion, bf16[2048,1408]{1,0:T(8,128)(2,1)} %get-tuple-element.384), kind=kOutput, calls=%fused_computation.11 | convolution fusion | flops 5907677184 | bytes 12845056 | tf_op jit(solution)/shard_map/dot_general | solution.py:869
  670.8 11.0 %convolution_convert_fusion.1 = bf16[1024,2048]{1,0:T(8,128)(2,1)} fusion(bf16[2048,1408]{1,0:T(8,128)(2,1)} %pad_maximum_fusion, bf16[2048,1408]{1,0:T(8,128)(2,1)} %get-tuple-element.384), kind=kOutput, calls=%fused_computation.12 | convolution fusion | flops 5907677184 | bytes 12845056 | tf_op jit(solution)/shard_map/dot_general | solution.py:869
  693.2 12.7 %fusion.8 = bf16[2048,896]{1,0:T(8,128)(2,1)S(1)} fusion(bf16[2048,2048]{1,0:T(8,128)(2,1)} %get-tuple-element.251, bf16[2048,1408]{1,0:T(8,128)(2,1)} %get-tuple-element.384), kind=kOutput, calls=%fused_computation.27 | convolution fusion | flops 7518027776 | bytes 15728640 | tf_op jit(solution)/shard_map/dot_general | solution.py:873
  706.8 10.5 %collective-permute-done.90 = bf16[1,2,2,128,768]{4,3,2,1,0:T(8,128)(2,1)S(1)} collective-permute-done((bf16[1,2,2,128,768]{4,3,2,1,0:T(8,128)(2,1)S(1)}, bf16[1,2,2,128,768]{4,3,2,1,0:T(8,128)(2,1)S(1)}, u32[]{:S(2)}, u32[]{:S(2)}) %collective-permute-start.90) | collective-permute-done | bytes 786464 | tf_op jit(solution)/shard_map/ppermute | solution.py:648
  729.5 8.7 %assemble.35 = bf16[2048,1152]{1,0:T(8,128)(2,1)S(1)} custom-call(s32[4]{0:T(128)S(1)} %pad_add_fusion.info_ref.info, bf16[2048,1152]{1,0:T(8,128)(2,1)S(1)} %pad_maximum_fusion.1.refs_0_), custom_call_target="tpu_custom_call" | custom-call | flops 1000 | bytes 1000 | tf_op jit(solution)/shard_map/assemble/pallas_call | solution.py:694
  758.7 6.2 collective-permute-done.105
  767.7 10.7 %collective-permute-done.101 = bf16[1,2,2,128,384]{4,3,2,1,0:T(8,128)(2,1)S(1)} collective-permute-done((bf16[1,2,2,128,384]{4,3,2,1,0:T(8,128)(2,1)S(1)}, bf16[1,2,2,128,384]{4,3,2,1,0:T(8,128)(2,1)S(1)}, u32[]{:S(2)}, u32[]{:S(2)}) %collective-permute-start.101) | collective-permute-done | bytes 393248 | tf_op jit(solution)/shard_map/ppermute | solution.py:648
  806.1 9.7 %collective-permute-start.112 = (bf16[64,1152]{1,0:T(8,128)(2,1)S(1)}, bf16[64,1152]{1,0:T(8,128)(2,1)S(1)}, u32[]{:S(2)}, u32[]{:S(2)}) collective-permute-start(bf16[64,1152]{1,0:T(8,128)(2,1)S(1)} %slice.1623), channel_id=1, source_target_pairs={{0,8},{1,9},{2,10},{3,11},{4,12},{5,13},{6,14},{7,15},{8,0},{9,1},... | collective-permute-start | bytes 442376 | tf_op jit(solution)/shard_map/ppermute | solution.py:648
  817.0 6.9 collective-permute-done.112
  825.3 10.1 %all-to-all-done.4 = bf16[16,64,891]{2,1,0:T(8,128)(2,1)S(1)} async-done(((bf16[16,64,891]{2,1,0:T(8,128)(2,1)}), bf16[16,64,891]{2,1,0:T(8,128)(2,1)S(1)}, u32[]{:S(2)}, u32[]{:S(2)}) %all-to-all-start.4) | async-done | bytes 1824800 | tf_op jit(solution)/shard_map/all_to_all | solution.py:861
  (778 shorter events, 471.7 us)
Async XLA Ops:
  3.1 37.3 %collective-permute-start = (bf16[256,2048]{1,0:T(8,128)(2,1)}, bf16[256,2048]{1,0:T(8,128)(2,1)}, u32[]{:S(2)}, u32[]{:S(2)}) collective-permute-start(bf16[256,2048]{1,0:T(8,128)(2,1)} %pad_maximum_fusion.9), channel_id=1, source_target_pairs={{8,16},{9,17},{10,18},{11,19},{12,20},{13,21},{14,22},{15,23},{16,... | collective-permute-start | bytes 3145736 | tf_op jit(solution)/shard_map/ppermute | solution.py:658
  5.7 34.6 %collective-permute-start.1 = (bf16[64,1280]{1,0:T(8,128)(2,1)S(1)}, bf16[64,1280]{1,0:T(8,128)(2,1)S(1)}, u32[]{:S(2)}, u32[]{:S(2)}) collective-permute-start(bf16[64,1280]{1,0:T(8,128)(2,1)S(1)} %concatenate.183), channel_id=1, source_target_pairs={{0,8},{1,9},{2,10},{3,11},{4,12},{5,13},{6,14},{7,15},{8,0},{9,1},... | collective-permute-start | bytes 491528 | tf_op jit(solution)/shard_map/ppermute | solution.py:648
  13.2 33.4 %all-to-all-start = ((bf16[16,64,512]{2,1,0:T(8,128)(2,1)}), bf16[16,64,512]{2,1,0:T(8,128)(2,1)S(1)}, u32[]{:S(2)}, u32[]{:S(2)}) async-start(bf16[16,64,512]{2,1,0:T(8,128)(2,1)} %maximum_maximum_fusion.2), calls=%async_computation | async-start | bytes 2097152 | tf_op jit(solution)/shard_map/all_to_all | solution.py:861
  51.6 26.3 %collective-permute-start.8 = (bf16[1024,256]{1,0:T(8,128)(2,1)S(1)}, bf16[1024,256]{1,0:T(8,128)(2,1)S(1)}, u32[]{:S(2)}, u32[]{:S(2)}) collective-permute-start(bf16[1024,256]{1,0:T(8,128)(2,1)S(1)} %slice.936), channel_id=1, source_target_pairs={{0,8},{1,9},{2,10},{3,11},{4,12},{5,13},{6,14},{7,15},{8,0},{9,1},... | collective-permute-start | bytes 1572872 | tf_op jit(solution)/shard_map/ppermute | solution.py:648
  57.9 23.1 %collective-permute-start.5 = (bf16[256,1152]{1,0:T(8,128)(2,1)S(1)}, bf16[256,1152]{1,0:T(8,128)(2,1)S(1)}, u32[]{:S(2)}, u32[]{:S(2)}) collective-permute-start(bf16[256,1152]{1,0:T(8,128)(2,1)S(1)} %get-tuple-element.220.refs_0_), channel_id=1, source_target_pairs={{0,2},{1,3},{2,0},{3,1},{4,6},{5,7},{6,4},{7,5},{8,10},{9,11},{10,... | collective-permute-start | bytes 1769480 | tf_op jit(solution)/shard_map/ppermute | solution.py:648
  85.3 36.0 %collective-permute-start.10 = (bf16[512,1152]{1,0:T(8,128)(2,1)}, bf16[512,1152]{1,0:T(8,128)(2,1)S(1)}, u32[]{:S(2)}, u32[]{:S(2)}) collective-permute-start(bf16[512,1152]{1,0:T(8,128)(2,1)} %get-tuple-element.231.refs_1_), channel_id=1, source_target_pairs={{0,4},{1,5},{2,6},{3,7},{4,0},{5,1},{6,2},{7,3},{8,12},{9,13},{10,... | collective-permute-start | bytes 3538952 | tf_op jit(solution)/shard_map/ppermute | solution.py:648
  85.4 35.9 %collective-permute-start.9 = (bf16[512,1152]{1,0:T(8,128)(2,1)}, bf16[512,1152]{1,0:T(8,128)(2,1)S(1)}, u32[]{:S(2)}, u32[]{:S(2)}) collective-permute-start(bf16[512,1152]{1,0:T(8,128)(2,1)} %get-tuple-element.230.refs_0_), channel_id=1, source_target_pairs={{0,1},{1,0},{2,3},{3,2},{4,5},{5,4},{6,7},{7,6},{8,9},{9,8},{10,11... | collective-permute-start | bytes 3538952 | tf_op jit(solution)/shard_map/ppermute | solution.py:648
  86.1 33.2 %collective-permute-start.11 = (bf16[512,1024]{1,0:T(8,128)(2,1)}, bf16[512,1024]{1,0:T(8,128)(2,1)}, u32[]{:S(2)}, u32[]{:S(2)}) collective-permute-start(bf16[512,1024]{1,0:T(8,128)(2,1)} %get-tuple-element.232.refs_2_), channel_id=1, source_target_pairs={{0,2},{1,3},{2,0},{3,1},{4,6},{5,7},{6,4},{7,5},{8,10},{9,11},{10,... | collective-permute-start | bytes 3145736 | tf_op jit(solution)/shard_map/ppermute | solution.py:648
  92.9 26.5 %collective-permute-start.12 = (bf16[1024,256]{1,0:T(8,128)(2,1)}, bf16[1024,256]{1,0:T(8,128)(2,1)}, u32[]{:S(2)}, u32[]{:S(2)}) collective-permute-start(bf16[1024,256]{1,0:T(8,128)(2,1)} %slice.939), channel_id=1, source_target_pairs={{0,8},{1,9},{2,10},{3,11},{4,12},{5,13},{6,14},{7,15},{8,0},{9,1},... | collective-permute-start | bytes 1572872 | tf_op jit(solution)/shard_map/ppermute | solution.py:648
  115.0 24.9 %collective-permute-start.13 = (bf16[512,3328]{1,0:T(8,128)(2,1)}, bf16[512,3328]{1,0:T(8,128)(2,1)}, u32[]{:S(2)}, u32[]{:S(2)}) collective-permute-start(bf16[512,3328]{1,0:T(8,128)(2,1)} %get-tuple-element.236), channel_id=1, source_target_pairs={{0,16},{1,17},{2,18},{3,19},{4,20},{5,21},{6,22},{7,23},{8,24},{9,... | collective-permute-start | bytes 10223624 | tf_op jit(solution)/shard_map/ppermute | solution.py:648
  131.6 45.0 %all-to-all-start.1 = ((bf16[16,64,1088]{2,1,0:T(8,128)(2,1)}), bf16[16,64,1088]{2,1,0:T(8,128)(2,1)}, u32[]{:S(2)}, u32[]{:S(2)}) async-start(bf16[16,64,1088]{2,1,0:T(8,128)(2,1)} %concatenate.191), calls=%async_computation.1 | async-start | bytes 4718592 | tf_op jit(solution)/shard_map/all_to_all | solution.py:861
  154.2 22.3 %collective-permute-start.16 = (bf16[128,640]{1,0:T(8,128)(2,1)S(1)}, bf16[128,640]{1,0:T(8,128)(2,1)S(1)}, u32[]{:S(2)}, u32[]{:S(2)}) collective-permute-start(bf16[128,640]{1,0:T(8,128)(2,1)S(1)} %get-tuple-element.243.refs_1_), channel_id=1, source_target_pairs={{0,2},{1,3},{2,0},{3,1},{4,6},{5,7},{6,4},{7,5},{8,10},{9,11},{10,... | collective-permute-start | bytes 491528 | tf_op jit(solution)/shard_map/ppermute | solution.py:648
  184.1 36.3 %collective-permute-start.21 = (bf16[1024,320]{0,1:T(8,128)(2,1)}, bf16[1024,320]{0,1:T(8,128)(2,1)S(1)}, u32[]{:S(2)}, u32[]{:S(2)}) collective-permute-start(bf16[1024,320]{0,1:T(8,128)(2,1)} %copy.115), channel_id=1, source_target_pairs={{0,8},{1,9},{2,10},{3,11},{4,12},{5,13},{6,14},{7,15},{8,0},{9,1},... | collective-permute-start | bytes 1966088 | tf_op jit(solution)/shard_map/ppermute | solution.py:648
  226.6 26.6 %collective-permute-start.28 = (bf16[1024,256]{1,0:T(8,128)(2,1)}, bf16[1024,256]{1,0:T(8,128)(2,1)}, u32[]{:S(2)}, u32[]{:S(2)}) collective-permute-start(bf16[1024,256]{1,0:T(8,128)(2,1)} %get-tuple-element.462), channel_id=1, source_target_pairs={{0,8},{1,9},{2,10},{3,11},{4,12},{5,13},{6,14},{7,15},{8,0},{9,1},... | collective-permute-start | bytes 1572872 | tf_op jit(solution)/shard_map/ppermute | solution.py:648
  258.6 25.0 %collective-permute-start.29 = (bf16[1024,2048]{1,0:T(8,128)(2,1)}, bf16[1024,2048]{1,0:T(8,128)(2,1)}, u32[]{:S(2)}, u32[]{:S(2)}) collective-permute-start(bf16[1024,2048]{1,0:T(8,128)(2,1)} %multiply_convert_fusion), channel_id=1, source_target_pairs={{0,16},{1,17},{2,18},{3,19},{4,20},{5,21},{6,22},{7,23},{8,24},{9,... | collective-permute-start | bytes 12582920 | tf_op jit(solution)/shard_map/ppermute | solution.py:648
  258.6 25.0 %collective-permute-start.30 = (bf16[1024,256]{1,0:T(8,128)(2,1)S(1)}, bf16[1024,256]{1,0:T(8,128)(2,1)S(1)}, u32[]{:S(2)}, u32[]{:S(2)}) collective-permute-start(bf16[1024,256]{1,0:T(8,128)(2,1)S(1)} %copy-done.85), channel_id=1, source_target_pairs={{0,8},{1,9},{2,10},{3,11},{4,12},{5,13},{6,14},{7,15},{8,0},{9,1},... | collective-permute-start | bytes 1572872 | tf_op jit(solution)/shard_map/ppermute | solution.py:648
  288.1 31.7 %collective-permute-start.31 = (bf16[1,2,2,128,768]{4,3,2,1,0:T(8,128)(2,1)S(1)}, bf16[1,2,2,128,768]{4,3,2,1,0:T(8,128)(2,1)S(1)}, u32[]{:S(2)}, u32[]{:S(2)}) collective-permute-start(bf16[1,2,2,128,768]{4,3,2,1,0:T(8,128)(2,1)S(1)} %get-tuple-element.436), channel_id=1, source_target_pairs={{0,4},{1,5},{2,6},{3,7},{4,0},{5,1},{6,2},{7,3},{8,12},{9,13},{10,... | collective-permute-start | bytes 2359304 | tf_op jit(solution)/shard_map/ppermute | solution.py:648
  289.9 31.6 %collective-permute-start.32 = (bf16[2,1,2,128,640]{4,3,2,1,0:T(8,128)(2,1)S(1)}, bf16[2,1,2,128,640]{4,3,2,1,0:T(8,128)(2,1)S(1)}, u32[]{:S(2)}, u32[]{:S(2)}) collective-permute-start(bf16[2,1,2,128,640]{4,3,2,1,0:T(8,128)(2,1)S(1)} %get-tuple-element.434), channel_id=1, source_target_pairs={{0,2},{1,3},{2,0},{3,1},{4,6},{5,7},{6,4},{7,5},{8,10},{9,11},{10,... | collective-permute-start | bytes 1966088 | tf_op jit(solution)/shard_map/ppermute | solution.py:648
  291.4 30.9 %collective-permute-start.37 = (bf16[1024,256]{1,0:T(8,128)(2,1)S(1)}, bf16[1024,256]{1,0:T(8,128)(2,1)S(1)}, u32[]{:S(2)}, u32[]{:S(2)}) collective-permute-start(bf16[1024,256]{1,0:T(8,128)(2,1)S(1)} %copy-done.84), channel_id=1, source_target_pairs={{0,8},{1,9},{2,10},{3,11},{4,12},{5,13},{6,14},{7,15},{8,0},{9,1},... | collective-permute-start | bytes 1572872 | tf_op jit(solution)/shard_map/ppermute | solution.py:648
  302.4 23.2 %collective-permute-start.36 = (bf16[1,2,1,128,640]{4,3,2,1,0:T(8,128)(2,1)S(1)}, bf16[1,2,1,128,640]{4,3,2,1,0:T(8,128)(2,1)S(1)}, u32[]{:S(2)}, u32[]{:S(2)}) collective-permute-start(bf16[1,2,1,128,640]{4,3,2,1,0:T(8,128)(2,1)S(1)} %get-tuple-element.483), channel_id=1, source_target_pairs={{0,4},{1,5},{2,6},{3,7},{4,0},{5,1},{6,2},{7,3},{8,12},{9,13},{10,... | collective-permute-start | bytes 983048 | tf_op jit(solution)/shard_map/ppermute | solution.py:648
  352.7 24.9 %collective-permute-start.41 = (bf16[512,768]{1,0:T(8,128)(2,1)S(1)}, bf16[512,768]{1,0:T(8,128)(2,1)S(1)}, u32[]{:S(2)}, u32[]{:S(2)}) collective-permute-start(bf16[512,768]{1,0:T(8,128)(2,1)S(1)} %get-tuple-element.286.refs_0_), channel_id=1, source_target_pairs={{0,1},{1,0},{2,3},{3,2},{4,5},{5,4},{6,7},{7,6},{8,9},{9,8},{10,11... | collective-permute-start | bytes 2359304 | tf_op jit(solution)/shard_map/ppermute | solution.py:648
  449.1 45.7 %collective-permute-start.75 = (bf16[1024,2048]{1,0:T(8,128)(2,1)}, bf16[1024,2048]{1,0:T(8,128)(2,1)}, u32[]{:S(2)}, u32[]{:S(2)}) collective-permute-start(bf16[1024,2048]{1,0:T(8,128)(2,1)} %convolution_convert_fusion.3), channel_id=1, source_target_pairs={{0,16},{1,17},{2,18},{3,19},{4,20},{5,21},{6,22},{7,23},{8,24},{9,... | collective-permute-start | bytes 12582920 | tf_op jit(solution)/shard_map/ppermute | solution.py:648
  453.4 25.7 %collective-permute-start.67 = (bf16[1024,256]{1,0:T(8,128)(2,1)S(1)}, bf16[1024,256]{1,0:T(8,128)(2,1)S(1)}, u32[]{:S(2)}, u32[]{:S(2)}) collective-permute-start(bf16[1024,256]{1,0:T(8,128)(2,1)S(1)} %slice.1047), channel_id=1, source_target_pairs={{0,8},{1,9},{2,10},{3,11},{4,12},{5,13},{6,14},{7,15},{8,0},{9,1},... | collective-permute-start | bytes 1572872 | tf_op jit(solution)/shard_map/ppermute | solution.py:648
  485.9 25.4 %collective-permute-start.74 = (bf16[1024,256]{1,0:T(8,128)(2,1)S(1)}, bf16[1024,256]{1,0:T(8,128)(2,1)S(1)}, u32[]{:S(2)}, u32[]{:S(2)}) collective-permute-start(bf16[1024,256]{1,0:T(8,128)(2,1)S(1)} %slice.1049), channel_id=1, source_target_pairs={{0,8},{1,9},{2,10},{3,11},{4,12},{5,13},{6,14},{7,15},{8,0},{9,1},... | collective-permute-start | bytes 1572872 | tf_op jit(solution)/shard_map/ppermute | solution.py:648
  533.7 34.3 %collective-permute-start.87 = (bf16[1024,256]{1,0:T(8,128)(2,1)}, bf16[1024,256]{1,0:T(8,128)(2,1)}, u32[]{:S(2)}, u32[]{:S(2)}) collective-permute-start(bf16[1024,256]{1,0:T(8,128)(2,1)} %slice.1055), channel_id=1, source_target_pairs={{0,8},{1,9},{2,10},{3,11},{4,12},{5,13},{6,14},{7,15},{8,0},{9,1},... | collective-permute-start | bytes 1572872 | tf_op jit(solution)/shard_map/ppermute | solution.py:648
  570.8 38.9 %all-to-all-start.2 = ((bf16[16,64,768]{2,1,0:T(8,128)(2,1)}), bf16[16,64,768]{2,1,0:T(8,128)(2,1)}, u32[]{:S(2)}, u32[]{:S(2)}) async-start(bf16[16,64,768]{2,1,0:T(8,128)(2,1)} %bitcast.209), calls=%async_computation.2 | async-start | bytes 3145728 | tf_op jit(solution)/shard_map/all_to_all | solution.py:861
  577.2 31.1 %collective-permute-start.88 = (bf16[1024,320]{0,1:T(8,128)(2,1)}, bf16[1024,320]{0,1:T(8,128)(2,1)}, u32[]{:S(2)}, u32[]{:S(2)}) collective-permute-start(bf16[1024,320]{0,1:T(8,128)(2,1)} %slice.1057), channel_id=1, source_target_pairs={{0,8},{1,9},{2,10},{3,11},{4,12},{5,13},{6,14},{7,15},{8,0},{9,1},... | collective-permute-start | bytes 1966088 | tf_op jit(solution)/shard_map/ppermute | solution.py:648
  609.7 72.1 %all-to-all-start.3 = ((bf16[8,128,2048]{2,1,0:T(8,128)(2,1)}), bf16[8,128,2048]{2,1,0:T(8,128)(2,1)}, u32[]{:S(2)}, u32[]{:S(2)}) async-start(bf16[8,128,2048]{2,1,0:T(8,128)(2,1)} %bitcast.198), calls=%async_computation.3 | async-start | bytes 8388608 | tf_op jit(solution)/shard_map/all_to_all | solution.py:1845
  668.2 119.7 %collective-permute-start.111 = (bf16[1024,320]{0,1:T(8,128)(2,1)}, bf16[1024,320]{0,1:T(8,128)(2,1)}, u32[]{:S(2)}, u32[]{:S(2)}) collective-permute-start(bf16[1024,320]{0,1:T(8,128)(2,1)} %slice.1156), channel_id=1, source_target_pairs={{0,8},{1,9},{2,10},{3,11},{4,12},{5,13},{6,14},{7,15},{8,0},{9,1},... | collective-permute-start | bytes 1966088 | tf_op jit(solution)/shard_map/ppermute | solution.py:648
  691.7 25.6 %collective-permute-start.90 = (bf16[1,2,2,128,768]{4,3,2,1,0:T(8,128)(2,1)S(1)}, bf16[1,2,2,128,768]{4,3,2,1,0:T(8,128)(2,1)S(1)}, u32[]{:S(2)}, u32[]{:S(2)}) collective-permute-start(bf16[1,2,2,128,768]{4,3,2,1,0:T(8,128)(2,1)S(1)} %get-tuple-element.423), channel_id=1, source_target_pairs={{0,4},{1,5},{2,6},{3,7},{4,0},{5,1},{6,2},{7,3},{8,12},{9,13},{10,... | collective-permute-start | bytes 2359304 | tf_op jit(solution)/shard_map/ppermute | solution.py:648
  752.1 37.5 %collective-permute-start.110 = (bf16[1024,251]{0,1:T(8,128)(2,1)S(1)}, bf16[1024,251]{0,1:T(8,128)(2,1)S(1)}, u32[]{:S(2)}, u32[]{:S(2)}) collective-permute-start(bf16[1024,251]{0,1:T(8,128)(2,1)S(1)} %slice.1155), channel_id=1, source_target_pairs={{0,8},{1,9},{2,10},{3,11},{4,12},{5,13},{6,14},{7,15},{8,0},{9,1},... | collective-permute-start | bytes 1542152 | tf_op jit(solution)/shard_map/ppermute | solution.py:648
  795.1 40.3 %all-to-all-start.4 = ((bf16[16,64,891]{2,1,0:T(8,128)(2,1)}), bf16[16,64,891]{2,1,0:T(8,128)(2,1)S(1)}, u32[]{:S(2)}, u32[]{:S(2)}) async-start(bf16[16,64,891]{2,1,0:T(8,128)(2,1)} %bitcast.208), calls=%async_computation.4 | async-start | bytes 3670016 | tf_op jit(solution)/shard_map/all_to_all | solution.py:861
  (214 other events, 2128.6 us)
